TPU v7x, 1024 devices: a whole 8x8x8 slice. The times are simulated.
1024 devices in a mesh: rep: 32 (over z, x_hi), fsdp: 32 (over x_lo, y, core).
Axes of the slice: x: 8 (x_hi: 4, x_lo: 2; x = x_hi * 2 + x_lo), y: 8, z: 8, core: 2. Of those that a mesh axis runs over, the one named last changes fastest.
Arguments:
- attn_out: bfloat16 [16384, 4096], P(('rep', 'fsdp')), may hold values from -6 to 6
- residual: bfloat16 [16384, 8192], P('rep', 'fsdp')
- out_weight: bfloat16 [4096, 8192], P(None, 'fsdp'), may hold values from -0.09375 to 0.09375
- tangent: bfloat16 [4096, 8192], P(None, 'fsdp'), may hold values from -0.09375 to 0.09375
- norm_gain: bfloat16 [8192], P('fsdp'), may hold values from 0.5 to 1.5
- cotangent: bfloat16 [16384, 8192], P('rep', 'fsdp'), may hold values from -6 to 6
- seq_len: int32 [32], P('rep'), may hold values from 256 to 512, as said below
Outputs:
- hvp: bfloat16 [4096, 8192], P('rep', 'fsdp')
Inputs may be any that keep to these rules, and one draw needn't show every extreme that they name: `seq_len`: every value lies in 256 to 512, and some group has exactly 512.
All inputs are finite; a program needn't handle non-finite values.
Results may differ from a plain program's by a relative error of at most 0.02.
Values may be sent and summed in bfloat16 or wider, within the bound.
No kernel may reach another device: no remote copies, remote signals or barrier semaphores. Data moves between devices by JAX's collectives and lax.ppermute only.
A program may use at most 32 MiB of HBM per device.

v0:
```python
import jax
import jax.numpy as jnp
from jax import lax
from jax.sharding import PartitionSpec as P

D = 8192


EPS = 1e-05


def second_order(stream, moved, weighted, sum_sq, along_c, tangent_c, cross):
    inv = lax.rsqrt(sum_sq / D + EPS)
    inv3 = inv * inv * inv
    inv5 = inv3 * inv * inv
    share = cross / D
    curv = -inv3 * share * weighted + 3.0 * inv5 * share * along_c * stream / D
    curv = curv - inv3 * tangent_c * stream / D - inv3 * along_c * moved / D
    return curv.astype(jnp.bfloat16)


def local(attn_out, residual, out_weight, tangent, norm_gain, cotangent, seq_len):
    gathered = lax.all_gather(attn_out, "fsdp", axis=0, tiled=True)
    count = gathered.shape[0]
    stream = residual.astype(jnp.float32) + jnp.dot(
        gathered, out_weight, preferred_element_type=jnp.float32
    )
    moved = jnp.dot(gathered, tangent, preferred_element_type=jnp.float32)
    live_rows = (jnp.arange(count, dtype=jnp.int32) < seq_len[0]).astype(jnp.float32)[:, None]
    weighted = cotangent.astype(jnp.float32) * norm_gain.astype(jnp.float32)[None, :] * live_rows
    sum_sq, along_c, tangent_c, cross = lax.psum(
        (
            jnp.sum(stream * stream, axis=1, keepdims=True),
            jnp.sum(weighted * stream, axis=1, keepdims=True),
            jnp.sum(weighted * moved, axis=1, keepdims=True),
            jnp.sum(stream * moved, axis=1, keepdims=True),
        ),
        "fsdp",
    )
    curv = second_order(stream, moved, weighted, sum_sq, along_c, tangent_c, cross)
    term = lax.dot_general(
        gathered, curv, (((0,), (0,)), ((), ())), preferred_element_type=jnp.float32
    )
    total = lax.psum_scatter(term.astype(jnp.bfloat16), "rep", scatter_dimension=0, tiled=True)
    return total


def solution(mesh):
    in_specs = (
        P(("rep", "fsdp"), None),
        P("rep", "fsdp"),
        P(None, "fsdp"),
        P(None, "fsdp"),
        P("fsdp"),
        P("rep", "fsdp"),
        P("rep"),
    )
    out_specs = P("rep", "fsdp")
    return jax.shard_map(local, mesh=mesh, in_specs=in_specs, out_specs=out_specs, check_vma=False)
```

profile of v0, /device:TPU:1, one launch (start us, length us, event | category | flops | bytes accessed | tf_op | source)
XLA Modules:
  0.0 398.0 jit_solution(18152369247533694160)
XLA Ops:
  6.5 0.0 copy-start
  6.5 0.0 all-gather.2.cloned.1.call-start
  6.5 0.7 all-gather.2.cloned.1.call-update
  7.3 0.0 reduce-scatter.4.cloned.1.call-start
  8.0 0.7 convert_element_type.27
  8.6 1.1 copy.15
  9.7 1.8 copy.14
  11.5 83.5 %all-gather.2.cloned.1.call-done = bf16[512,4096]{1,0:T(8,128)(2,1)} async-done(((bf16[16,4096]{1,0:T(8,128)(2,1)}), bf16[512,4096]{1,0:T(8,128)(2,1)}) %all-gather.2.cloned.1.call-update) | async-done | bytes 4194320 | tf_op jit(solution)/shard_map/all_gather | solution.py:23
  95.0 0.0 copy-start.1
  95.0 0.0 copy-start.2
  95.0 4.3 %fusion.15 = f32[512,256]{0,1:T(8,128)S(1)} fusion(bf16[512,4096]{1,0:T(8,128)(2,1)} %all-gather.2.cloned.1.call-done, bf16[4096,256]{1,0:T(8,128)(2,1)} %param.10), kind=kOutput, calls=%fused_computation.28 | convolution fusion | flops 1073741824 | bytes 6815744 | tf_op jit(solution)/shard_map/dot_general | solution.py:28
  99.3 0.0 copy-done
  99.3 0.0 copy-done.1
  99.3 0.0 copy-done.2
  99.3 1.5 multiply_reduce_fusion.2
  100.8 53.6 %all-reduce = (f32[512,1]{0,1:T(1,128)S(1)}, f32[512,1]{0,1:T(1,128)S(1)}, f32[512,1]{0,1:T(1,128)S(1)}, f32[512,1]{0,1:T(1,128)S(1)}) all-reduce(f32[512,1]{0,1:T(1,128)S(1)} %bitcast.24, f32[512,1]{0,1:T(1,128)S(1)} %bitcast.25, f32[512,1]{0,1:T(1,128)S(1)} %bitcast.23, ...), channel_id=1, replica_groups=mesh['rep'=32,'fsdp'=32] {'fsdp'}, use_global_device_ids=true, to_apply=%region_5.0 | all-reduce | flops 2048 | bytes 16384 | tf_op jit(solution)/shard_map/psum | solution.py:31
  154.4 5.0 %fusion = bf16[4096,256]{0,1:T(8,128)(2,1)} fusion(bf16[512,4096]{1,0:T(8,128)(2,1)} %all-gather.2.cloned.1.call-done, f32[512,256]{0,1:T(8,128)S(1)} %fusion.15, f32[512,256]{0,1:T(8,128)S(1)} %get-tuple-element.17, bf16[512,256]{0,1:T(8,128)(2,1)S(1)} %copy.15, f32[512]{0:T(512)S(1)} %bitcast.20, f32[512]{0:T(512)S(1)} %bitcast.21, f32[512]{0:T(512)S(1)} %bitcast.19, ...), kind=kOutput, calls=%fused_computation.1 | convolution fusion | flops 1076625408 | bytes 7613440 | tf_op jit(solution)/shard_map/dot_general | solution.py:41
  159.4 4.1 %copy.17 = bf16[4096,256]{1,0:T(8,128)(2,1)} copy(bf16[4096,256]{0,1:T(8,128)(2,1)} %fusion) | data formatting | bytes 4194304
  163.5 0.0 reduce-scatter.4.cloned.1.call-update
  163.5 227.7 %reduce-scatter.4.cloned.1.call-done = bf16[128,256]{1,0:T(8,128)(2,1)} async-done(((bf16[4096,256]{1,0:T(8,128)(2,1)}), bf16[128,256]{1,0:T(8,128)(2,1)}) %reduce-scatter.4.cloned.1.call-update) | async-done | bytes 65552 | tf_op jit(solution)/shard_map/reduce_scatter | solution.py:44
  (2 shorter events, 0.0 us)
Async XLA Ops:
  6.5 92.7 %copy-start = (bf16[4096,256]{1,0:T(8,128)(2,1)S(1)}, bf16[4096,256]{1,0:T(8,128)(2,1)}, u32[]{:S(2)}) copy-start(bf16[4096,256]{1,0:T(8,128)(2,1)} %param.9) | copy-start | bytes 6291460
  6.5 88.4 %all-gather.2.cloned.1.call-start = ((), (), s32[]{:S(2)}) async-start(), calls=%async_computation.1 | async-start | bytes 4325376 | tf_op jit(solution)/shard_map/all_gather | solution.py:23
  7.3 383.9 %reduce-scatter.4.cloned.1.call-start = ((), (), s32[]{:S(2)}) async-start(), calls=%async_computation.2 | async-start | bytes 2162688 | tf_op jit(solution)/shard_map/reduce_scatter | solution.py:44
  95.0 4.3 %copy-start.1 = (bf16[512,4096]{1,0:T(8,128)(2,1)S(1)}, bf16[512,4096]{1,0:T(8,128)(2,1)}, u32[]{:S(2)}) copy-start(bf16[512,4096]{1,0:T(8,128)(2,1)} %all-gather.2.cloned.1.call-done) | copy-start | bytes 12582916
  95.0 4.3 %copy-start.2 = (bf16[512,256]{0,1:T(8,128)(2,1)S(1)}, bf16[512,256]{0,1:T(8,128)(2,1)}, u32[]{:S(2)}) copy-start(bf16[512,256]{0,1:T(8,128)(2,1)} %copy.14) | copy-start | bytes 786436
Sparse Core Ops, SparseCore 0:
  10.1 84.8 all-gather.1
  163.6 227.5 reduce-scatter.3
where the time goes:
time: 402 us; the launch traced here: 398 us
  waiting for transfers between devices  312 us (78%)
  blocking collectives  53.6 us (13%)
  between operations  14.1 us (4%)
  matrix products  10.7 us (3%)
  local copies, waits for them, and re-layouts  6.98 us (2%)
    reduce_scatter x1, waiting for transfers between devices, local(): lax.psum_scatter(term.astype(jnp.bfloat16), 'rep', scatter_dimension=0, t...  228 us
    all_gather x1, waiting for transfers between devices, local(): gathered = lax.all_gather(attn_out, 'fsdp', axis=0, tiled=True)  83.5 us
    psum x1, blocking collectives, local(): lax.psum((jnp.sum(stream * stream, axis=1, keepdims=True), jnp.sum(weight...  53.6 us
  transfers between devices with their start and end apart: 2, of which 2 were waited for; matrix products, arithmetic and copies ran while one was open for 1% of the time, Pallas kernels for 0%

commit v1 on v0

v1 whole, which is shorter than its diff:
```python
import jax
import jax.numpy as jnp
from jax import lax
from jax.experimental import pallas as pl
from jax.experimental.pallas import tpu as pltpu
from jax.sharding import PartitionSpec as P

D = 8192
EPS = 1e-05
NX, NY, NC = 2, 8, 2
NZ, NH = 8, 4
SHARD = 16
VMEM = pl.BlockSpec(memory_space=pltpu.VMEM)
SMEM = pl.BlockSpec(memory_space=pltpu.SMEM)
ANY = pl.BlockSpec(memory_space=pl.ANY)
PARAMS = pltpu.CompilerParams(vmem_limit_bytes=48 * 1024 * 1024)


def fsdp_perm(dx, dy, dc):
    moves = []
    for x in range(NX):
        for y in range(NY):
            for c in range(NC):
                there = (((x + dx) % NX) * NY + (y + dy) % NY) * NC + (c + dc) % NC
                moves.append(((x * NY + y) * NC + c, there))
    return moves


def rep_perm(dz, dh):
    return [
        (z * NH + h, ((z + dz) % NZ) * NH + (h + dh) % NH)
        for z in range(NZ)
        for h in range(NH)
    ]


CLASSES = [
    [z * NH + h for z in range(NZ) for h in range(NH) if (z + 2 * h) % 4 == c]
    for c in range(4)
]


def token_blocks(me, other_core):
    x, y, c = me // (NY * NC), (me // NC) % NY, me % NC
    c = 1 - c if other_core else c
    blocks = []
    for gx, gy in ((0, 0), (0, -1), (0, 1), (1, 0)):
        for sx, sy in ((0, 0), (0, 4), (1, -2), (1, 2)):
            cx = (x + gx + sx) % NX
            cy = (y + gy + sy + NY) % NY
            blocks.append((cx * NY + cy) * NC + c)
    return blocks


def rows_of(block):
    return pl.ds(pl.multiple_of(block * SHARD, SHARD), SHARD)


def weighted_of(cot_ref, gain_ref, length, rows, first):
    token = first + lax.broadcasted_iota(jnp.int32, (rows, 1), 0)
    live = (token < length).astype(jnp.float32)
    return (
        cot_ref[pl.ds(first, rows), :].astype(jnp.float32)
        * gain_ref[...].astype(jnp.float32)
        * live
    )


def first_kernel(me_ref, len_ref, *refs):
    pieces = refs[:8]
    w_ref, t_ref, res_ref, cot_ref, gain_ref = refs[8:13]
    a_ref, stream_ref, moved_ref, stats_ref, sems = refs[13:]
    rows = a_ref.shape[0]
    part = rows // 8
    copies = [
        pltpu.make_async_copy(piece, a_ref.at[pl.ds(i * part, part)], sems.at[i])
        for i, piece in enumerate(pieces)
    ]
    for copy in copies:
        copy.start()
    me = me_ref[0]
    for half in range(2):
        for copy in copies[4 * half : 4 * half + 4]:
            copy.wait()
        a = a_ref[pl.ds(half * 4 * part, 4 * part), :]
        s = jnp.dot(a, w_ref[...], preferred_element_type=jnp.float32)
        m = jnp.dot(a, t_ref[...], preferred_element_type=jnp.float32)
        for i, block in enumerate(token_blocks(me, half == 1)):
            stream_ref[rows_of(block), :] = s[i * SHARD : (i + 1) * SHARD]
            moved_ref[rows_of(block), :] = m[i * SHARD : (i + 1) * SHARD]
    stream = stream_ref[...] + res_ref[...].astype(jnp.float32)
    stream_ref[...] = stream
    moved = moved_ref[...]
    weighted = weighted_of(cot_ref, gain_ref, len_ref[0], rows, 0)
    sums = [
        jnp.sum(stream * stream, axis=1, keepdims=True),
        jnp.sum(weighted * stream, axis=1, keepdims=True),
        jnp.sum(weighted * moved, axis=1, keepdims=True),
        jnp.sum(stream * moved, axis=1, keepdims=True),
    ]
    lane = lax.broadcasted_iota(jnp.int32, (rows, 128), 1)
    table = jnp.zeros((rows, 128), jnp.float32)
    for i, value in enumerate(sums):
        table = jnp.where(lane == i, value, table)
    turned = table.T
    half = rows // 2
    packed = jnp.concatenate([turned[:4, :half], turned[:4, half:]], axis=0)
    for i in range(stats_ref.shape[0]):
        stats_ref[i] = packed


def second_kernel(
    ids_ref, len_ref, stats_ref, stream_ref, moved_ref, cot_ref, gain_ref, a_ref,
    own_ref, up_ref, down_ref, right_ref, left_ref, curv_ref,
):
    total = jnp.sum(stats_ref[...], axis=0)
    half = total.shape[1]
    coefs = []
    for h in range(2):
        sum_sq, along_c, tangent_c, cross = (
            total[4 * h + i : 4 * h + i + 1] for i in range(4)
        )
        inv = lax.rsqrt(sum_sq / D + EPS)
        inv3 = inv * inv * inv
        inv5 = inv3 * inv * inv
        share = cross / D
        coefs.append(-inv3 * share)
        coefs.append((3.0 * inv5 * share * along_c - inv3 * tangent_c) / D)
        coefs.append(-inv3 * along_c / D)
    coefs.append(jnp.zeros((128 - len(coefs), half), jnp.float32))
    turned = jnp.concatenate(coefs, axis=0).T
    for h in range(2):
        rows = pl.ds(h * half, half)
        weighted = weighted_of(cot_ref, gain_ref, len_ref[0], half, h * half)
        curv_ref[rows, :] = (
            turned[:, 3 * h : 3 * h + 1] * weighted
            + turned[:, 3 * h + 1 : 3 * h + 2] * stream_ref[rows, :]
            + turned[:, 3 * h + 2 : 3 * h + 3] * moved_ref[rows, :]
        )
    me = ids_ref[0]
    blocks = token_blocks(me, False) + token_blocks(me, True)
    curv = jnp.concatenate([curv_ref[rows_of(b), :] for b in blocks], axis=0)
    curv_t = curv.T.astype(jnp.bfloat16)
    color = ids_ref[1]
    for r in (1, 3, 2, 0):
        c = (color + r) % 4
        for pair in range(4):
            z = 2 * pair + c % 2
            h = ((z - c + 8) % 4) // 2
            columns = [
                a_ref[:, pl.ds(pl.multiple_of((z * NH + h + 2 * k) * 128, 128), 128)]
                for k in range(2)
            ]
            out = jnp.dot(
                curv_t,
                jnp.concatenate(columns, axis=1),
                preferred_element_type=jnp.float32,
            ).astype(jnp.bfloat16)
            for k in range(2):
                i = 2 * pair + k
                value = out[:, 128 * k : 128 * k + 128]
                if r == 0:
                    own_ref[i] = value
                elif r == 1:
                    up_ref[i] = value
                elif r == 3:
                    down_ref[i] = value
                elif i < 4:
                    right_ref[i] = value
                else:
                    left_ref[i - 4] = value


def third_kernel(own_ref, below_ref, above_ref, left_ref, right_ref, out_ref):
    f32 = jnp.float32
    for i in range(8):
        side = left_ref[i] if i < 4 else right_ref[i - 4]
        out_ref[i] = (
            own_ref[i].astype(f32)
            + below_ref[i].astype(f32)
            + above_ref[i].astype(f32)
            + side.astype(f32)
        ).astype(out_ref.dtype)


def last_kernel(parts_ref, out_ref):
    total = parts_ref[0].astype(jnp.float32)
    for i in range(1, parts_ref.shape[0]):
        total = total + parts_ref[i].astype(jnp.float32)
    out_ref[...] = total.T.astype(out_ref.dtype)


def local(attn_out, residual, out_weight, tangent, norm_gain, cotangent, seq_len):
    f32, bf16 = jnp.float32, jnp.bfloat16
    rows, columns = residual.shape
    features = attn_out.shape[1]
    me = lax.axis_index("fsdp")
    rep = lax.axis_index("rep")
    color = (rep // NH + 2 * (rep % NH)) % 4
    ids = jnp.stack([me, color]).astype(jnp.int32)
    gain = norm_gain[None, :]

    def send(x, *step):
        return lax.ppermute(x, "fsdp", fsdp_perm(*step))

    own = jnp.concatenate(
        [
            attn_out,
            send(attn_out, 0, 4, 0),
            send(attn_out, 1, 2, 0),
            send(attn_out, 1, -2, 0),
        ],
        axis=0,
    )
    near = [own, send(own, 0, 1, 0), send(own, 0, -1, 0), send(own, 1, 0, 0)]
    far = [send(x, 0, 0, 1) for x in near]

    a, stream, moved, stats = pl.pallas_call(
        first_kernel,
        out_shape=(
            jax.ShapeDtypeStruct((rows, features), bf16),
            jax.ShapeDtypeStruct((rows, columns), f32),
            jax.ShapeDtypeStruct((rows, columns), f32),
            jax.ShapeDtypeStruct((32, 8, rows // 2), f32),
        ),
        in_specs=[SMEM, SMEM] + [ANY] * 8 + [VMEM] * 5,
        out_specs=(VMEM,) * 4,
        scratch_shapes=[pltpu.SemaphoreType.DMA((8,))],
        compiler_params=PARAMS,
        name="first",
    )(ids, seq_len, *near, *far, out_weight, tangent, residual, cotangent, gain)

    stats = lax.all_to_all(stats, "fsdp", 0, 0)

    whole = jax.ShapeDtypeStruct((8, columns, 128), bf16)
    part = jax.ShapeDtypeStruct((4, columns, 128), bf16)
    mine, up, down, right, left = pl.pallas_call(
        second_kernel,
        out_shape=(whole, whole, whole, part, part),
        in_specs=[SMEM, SMEM] + [VMEM] * 6,
        out_specs=(VMEM,) * 5,
        scratch_shapes=[pltpu.VMEM((rows, columns), f32)],
        compiler_params=PARAMS,
        name="second",
    )(ids, seq_len, stats, stream, moved, cotangent, gain, a)

    below = lax.ppermute(up, "rep", rep_perm(1, 0))
    above = lax.ppermute(down, "rep", rep_perm(-1, 0))
    from_left = lax.ppermute(right, "rep", rep_perm(0, 1))
    from_right = lax.ppermute(left, "rep", rep_perm(0, -1))
    four = pl.pallas_call(
        third_kernel,
        out_shape=whole,
        in_specs=[VMEM] * 5,
        out_specs=VMEM,
        compiler_params=PARAMS,
        name="third",
    )(mine, below, above, from_left, from_right)
    parts = lax.all_to_all(four, "rep", 0, 0, axis_index_groups=CLASSES)
    return pl.pallas_call(
        last_kernel,
        out_shape=jax.ShapeDtypeStruct((128, columns), bf16),
        in_specs=[VMEM],
        out_specs=VMEM,
        compiler_params=PARAMS,
        name="last",
    )(parts)


def solution(mesh):
    in_specs = (
        P(("rep", "fsdp"), None),
        P("rep", "fsdp"),
        P(None, "fsdp"),
        P(None, "fsdp"),
        P("fsdp"),
        P("rep", "fsdp"),
        P("rep"),
    )
    out_specs = P("rep", "fsdp")
    return jax.shard_map(local, mesh=mesh, in_specs=in_specs, out_specs=out_specs, check_vma=False)
```

time: 402 us -> 147 us (0.37)
  waiting for transfers between devices: 312 us -> 15.6 us
  starting transfers between devices: 0.04 us -> 69.3 us
  between operations: 14.1 us -> 0.88 us
  Pallas kernels: 0 us -> 12.5 us
  matrix products: 10.7 us -> 0 us
  blocking collectives: 53.6 us -> 44.1 us
    reduce_scatter x1 -> x0, waiting for transfers between devices: 228 us -> none  [local(): lax.psum_scatter(term.astype(jnp.bfloat16), 'rep', scatter_dimension=0, t...]
    all_gather x1 -> x0, waiting for transfers between devices: 83.5 us -> none  [local(): gathered = lax.all_gather(attn_out, 'fsdp', axis=0, tiled=True)]
    ppermute x0 -> x14, starting transfers between devices: none -> 69.3 us  [the longest x10 45.8 us: send(): return lax.ppermute(x, 'fsdp', fsdp_perm(*step))]
    psum x1 -> x0, blocking collectives: 53.6 us -> none  [local(): lax.psum((jnp.sum(stream * stream, axis=1, keepdims=True), jnp.sum(weight...]
    all_to_all x0 -> x2, blocking collectives: none -> 44.1 us  [the longest x1 25.5 us: local(): parts = lax.all_to_all(four, 'rep', 0, 0, axis_index_groups=CLASSES)]
    ppermute x0 -> x14, waiting for transfers between devices: none -> 15.6 us  [the longest x1 6.33 us: local(): from_right = lax.ppermute(left, 'rep', rep_perm(0, -1))]
    pallas_call x0 -> x4, Pallas kernels: none -> 12.5 us  [the longest x1 7.28 us: local(): pl.pallas_call(first_kernel, out_shape=(jax.ShapeDtypeStruct((rows, featu...]
    dot_general x3 -> x0, matrix products: 10.7 us -> none  [the longest x1 4.98 us: local(): lax.dot_general(gathered, curv, (((0,), (0,)), ((), ())), preferred_eleme...]
  transfers between devices with their start and end apart: 2 -> 14, of which waited for: 2 -> 5; matrix products, arithmetic and copies ran while one was open for 1% -> 1% of each run, Pallas kernels for 0% -> 0%
where the time goes in v1:
time: 147 us; the launch traced here: 146 us
  starting transfers between devices  69.3 us (47%)
  blocking collectives  44.1 us (30%)
  waiting for transfers between devices  15.6 us (11%)
  Pallas kernels  12.5 us (9%)
  local copies, waits for them, and re-layouts  3.51 us (2%)
    ppermute x10, starting transfers between devices, send(): return lax.ppermute(x, 'fsdp', fsdp_perm(*step))  45.8 us
    all_to_all x1, blocking collectives, local(): parts = lax.all_to_all(four, 'rep', 0, 0, axis_index_groups=CLASSES)  25.5 us
    all_to_all x1, blocking collectives, local(): stats = lax.all_to_all(stats, 'fsdp', 0, 0)  18.6 us
    ppermute x1, starting transfers between devices, local(): above = lax.ppermute(down, 'rep', rep_perm(-1, 0))  11.4 us
    pallas_call x1, Pallas kernels, local(): pl.pallas_call(first_kernel, out_shape=(jax.ShapeDtypeStruct((rows, featu...  7.28 us
    ppermute x1, waiting for transfers between devices, local(): from_right = lax.ppermute(left, 'rep', rep_perm(0, -1))  6.33 us
    ppermute x1, waiting for transfers between devices, local(): from_left = lax.ppermute(right, 'rep', rep_perm(0, 1))  5.5 us
    ppermute x1, starting transfers between devices, local(): below = lax.ppermute(up, 'rep', rep_perm(1, 0))  4.74 us
  transfers between devices with their start and end apart: 14, of which 5 were waited for; matrix products, arithmetic and copies ran while one was open for 1% of the time, Pallas kernels for 0%

profile of v1, /device:TPU:1, one launch (start us, length us, event | category | flops | bytes accessed | tf_op | source)
XLA Modules:
  0.0 146.0 jit_solution(690360047852228138)
XLA Ops:
  0.0 6.2 %collective-permute-start.1 = (bf16[16,4096]{1,0:T(8,128)(2,1)}, bf16[16,4096]{1,0:T(8,128)(2,1)S(1)}, u32[]{:S(2)}, u32[]{:S(2)}) collective-permute-start(bf16[16,4096]{1,0:T(8,128)(2,1)} %param.7), channel_id=1, source_target_pairs={{0,20},{1,21},{2,22},{3,23},{4,24},{5,25},{6,26},{7,27},{8,28},{9,... | collective-permute-start | bytes 393224 | tf_op jit(solution)/shard_map/ppermute | solution.py:204
  6.2 6.1 %collective-permute-start = (bf16[16,4096]{1,0:T(8,128)(2,1)}, bf16[16,4096]{1,0:T(8,128)(2,1)S(1)}, u32[]{:S(2)}, u32[]{:S(2)}) collective-permute-start(bf16[16,4096]{1,0:T(8,128)(2,1)} %param.7), channel_id=1, source_target_pairs={{0,8},{1,9},{2,10},{3,11},{4,12},{5,13},{6,14},{7,15},{8,0},{9,1},... | collective-permute-start | bytes 393224 | tf_op jit(solution)/shard_map/ppermute | solution.py:204
  12.3 4.7 %collective-permute-start.2 = (bf16[16,4096]{1,0:T(8,128)(2,1)}, bf16[16,4096]{1,0:T(8,128)(2,1)S(1)}, u32[]{:S(2)}, u32[]{:S(2)}) collective-permute-start(bf16[16,4096]{1,0:T(8,128)(2,1)} %param.7), channel_id=1, source_target_pairs={{0,28},{1,29},{2,30},{3,31},{4,16},{5,17},{6,18},{7,19},{8,20},{9,... | collective-permute-start | bytes 393224 | tf_op jit(solution)/shard_map/ppermute | solution.py:204
  17.0 0.9 constant_dynamic-update-slice_fusion.3
  18.0 1.1 collective-permute-done
  19.1 0.0 collective-permute-done.1
  19.1 2.4 %collective-permute-done.2 = bf16[16,4096]{1,0:T(8,128)(2,1)S(1)} collective-permute-done((bf16[16,4096]{1,0:T(8,128)(2,1)}, bf16[16,4096]{1,0:T(8,128)(2,1)S(1)}, u32[]{:S(2)}, u32[]{:S(2)}) %collective-permute-start.2) | collective-permute-done | bytes 131104 | tf_op jit(solution)/shard_map/ppermute | solution.py:204
  21.6 3.6 %collective-permute-start.5 = (bf16[64,4096]{1,0:T(8,128)(2,1)S(1)}, bf16[64,4096]{1,0:T(8,128)(2,1)S(1)}, u32[]{:S(2)}, u32[]{:S(2)}) collective-permute-start(bf16[64,4096]{1,0:T(8,128)(2,1)S(1)} %constant_dynamic-update-slice_fusion.refs_0_), channel_id=1, source_target_pairs={{0,16},{1,17},{2,18},{3,19},{4,20},{5,21},{6,22},{7,23},{8,24},{9,... | collective-permute-start | bytes 1572872 | tf_op jit(solution)/shard_map/ppermute | solution.py:204
  25.2 4.8 %collective-permute-start.4 = (bf16[64,4096]{1,0:T(8,128)(2,1)S(1)}, bf16[64,4096]{1,0:T(8,128)(2,1)S(1)}, u32[]{:S(2)}, u32[]{:S(2)}) collective-permute-start(bf16[64,4096]{1,0:T(8,128)(2,1)S(1)} %constant_dynamic-update-slice_fusion.refs_0_), channel_id=1, source_target_pairs={{0,14},{1,15},{2,0},{3,1},{4,2},{5,3},{6,4},{7,5},{8,6},{9,7},{10,... | collective-permute-start | bytes 1572872 | tf_op jit(solution)/shard_map/ppermute | solution.py:204
  30.0 1.9 %collective-permute-start.3 = (bf16[64,4096]{1,0:T(8,128)(2,1)S(1)}, bf16[64,4096]{1,0:T(8,128)(2,1)S(1)}, u32[]{:S(2)}, u32[]{:S(2)}) collective-permute-start(bf16[64,4096]{1,0:T(8,128)(2,1)S(1)} %constant_dynamic-update-slice_fusion.refs_0_), channel_id=1, source_target_pairs={{0,2},{1,3},{2,4},{3,5},{4,6},{5,7},{6,8},{7,9},{8,10},{9,11},{10,... | collective-permute-start | bytes 1572872 | tf_op jit(solution)/shard_map/ppermute | solution.py:204
  31.9 9.6 %collective-permute-start.6 = (bf16[64,4096]{1,0:T(8,128)(2,1)S(1)}, bf16[64,4096]{1,0:T(8,128)(2,1)S(1)}, u32[]{:S(2)}, u32[]{:S(2)}) collective-permute-start(bf16[64,4096]{1,0:T(8,128)(2,1)S(1)} %constant_dynamic-update-slice_fusion.refs_0_), channel_id=1, source_target_pairs={{0,1},{1,0},{2,3},{3,2},{4,5},{5,4},{6,7},{7,6},{8,9},{9,8},{10,11... | collective-permute-start | bytes 1572872 | tf_op jit(solution)/shard_map/ppermute | solution.py:204
  41.5 0.0 collective-permute-done.5.refs_3_
  41.5 3.3 %collective-permute-start.9 = (bf16[64,4096]{1,0:T(8,128)(2,1)S(1)}, bf16[64,4096]{1,0:T(8,128)(2,1)S(1)}, u32[]{:S(2)}, u32[]{:S(2)}) collective-permute-start(bf16[64,4096]{1,0:T(8,128)(2,1)S(1)} %collective-permute-done.5.refs_3_), channel_id=1, source_target_pairs={{0,1},{1,0},{2,3},{3,2},{4,5},{5,4},{6,7},{7,6},{8,9},{9,8},{10,11... | collective-permute-start | bytes 1572872 | tf_op jit(solution)/shard_map/ppermute | solution.py:204
  44.8 0.0 collective-permute-done.4.refs_2_
  44.8 1.9 %collective-permute-start.8 = (bf16[64,4096]{1,0:T(8,128)(2,1)S(1)}, bf16[64,4096]{1,0:T(8,128)(2,1)}, u32[]{:S(2)}, u32[]{:S(2)}) collective-permute-start(bf16[64,4096]{1,0:T(8,128)(2,1)S(1)} %collective-permute-done.4.refs_2_), channel_id=1, source_target_pairs={{0,1},{1,0},{2,3},{3,2},{4,5},{5,4},{6,7},{7,6},{8,9},{9,8},{10,11... | collective-permute-start | bytes 1572872 | tf_op jit(solution)/shard_map/ppermute | solution.py:204
  46.7 0.0 collective-permute-done.3.refs_1_
  46.8 3.7 %collective-permute-start.7 = (bf16[64,4096]{1,0:T(8,128)(2,1)S(1)}, bf16[64,4096]{1,0:T(8,128)(2,1)}, u32[]{:S(2)}, u32[]{:S(2)}) collective-permute-start(bf16[64,4096]{1,0:T(8,128)(2,1)S(1)} %collective-permute-done.3.refs_1_), channel_id=1, source_target_pairs={{0,1},{1,0},{2,3},{3,2},{4,5},{5,4},{6,7},{7,6},{8,9},{9,8},{10,11... | collective-permute-start | bytes 1572872 | tf_op jit(solution)/shard_map/ppermute | solution.py:204
  51.1 0.7 broadcast_in_dim.3.refs_12_.gain_ref
  51.8 0.1 pad_add_fusion.me_ref.ids_ref
  51.9 0.0 collective-permute-done.6.refs_4_
  51.9 0.0 collective-permute-done.9.refs_7_
  51.9 0.0 collective-permute-done.8.refs_6_
  51.9 0.2 collective-permute-done.7.refs_5_
  52.1 0.0 copy-start
  52.1 0.9 copy-done
  53.0 0.0 copy-start.1
  53.0 0.9 copy-done.1
  54.0 7.3 %first.1 = (bf16[512,4096]{1,0:T(8,128)(2,1)}, f32[512,256]{1,0:T(8,128)S(1)}, f32[512,256]{1,0:T(8,128)S(1)}, f32[32,8,256]{2,1,0:T(8,128)S(1)}) custom-call(s32[2]{0:T(128)S(1)} %pad_add_fusion.me_ref.ids_ref, s32[1]{0:T(128)S(6)} %copy.11.len_ref, bf16[64,4096]{1,0:T(8,128)(2,1)S(1)} %constant_dynamic-update-slice_fusion.refs_0_, ...), custom_call_target="tpu_custom_call" | custom-call | tf_op jit(solution)/shard_map/first/pallas_call | solution.py:218
  61.3 18.6 %all_to_all.10.stats_ref = f32[32,8,256]{2,1,0:T(8,128)S(1)} all-to-all(f32[32,8,256]{2,1,0:T(8,128)S(1)} %get-tuple-element.14), channel_id=1, replica_groups=mesh['rep'=32,'fsdp'=32] {'fsdp'}, dimensions={0} | all-to-all | bytes 524288 | tf_op jit(solution)/shard_map/all_to_all | solution.py:233
  79.9 4.2 %second.1 = (bf16[8,256,128]{2,1,0:T(8,128)(2,1)S(1)}, bf16[8,256,128]{2,1,0:T(8,128)(2,1)S(1)}, bf16[8,256,128]{2,1,0:T(8,128)(2,1)S(1)}, bf16[4,256,128]{2,1,0:T(8,128)(2,1)S(1)}, bf16[4,256,128]{2,1,0:T(8,128)(2,1)S(1)}) custom-call(s32[2]{0:T(128)S(1)} %pad_add_fusion.me_ref.ids_ref, s32[1]{0:T(128)S(6)} %copy.11.len_ref, ...), custom_call_target="tpu_custom_call" | custom-call | tf_op jit(solution)/shard_map/second/pallas_call | solution.py:237
  84.1 4.7 %collective-permute-start.10 = (bf16[8,256,128]{2,1,0:T(8,128)(2,1)S(1)}, bf16[8,256,128]{2,1,0:T(8,128)(2,1)S(1)}, u32[]{:S(2)}, u32[]{:S(2)}) collective-permute-start(bf16[8,256,128]{2,1,0:T(8,128)(2,1)S(1)} %get-tuple-element.19), channel_id=1, source_target_pairs={{0,128},{32,160},{64,192},{96,224},{128,256},{160,288},{192,320},{... | collective-permute-start | bytes 1572872 | tf_op jit(solution)/shard_map/ppermute | solution.py:247
  88.9 11.4 %collective-permute-start.11 = (bf16[8,256,128]{2,1,0:T(8,128)(2,1)S(1)}, bf16[8,256,128]{2,1,0:T(8,128)(2,1)S(1)}, u32[]{:S(2)}, u32[]{:S(2)}) collective-permute-start(bf16[8,256,128]{2,1,0:T(8,128)(2,1)S(1)} %get-tuple-element.20), channel_id=1, source_target_pairs={{0,896},{32,928},{64,960},{96,992},{128,0},{160,32},{192,64},{224,... | collective-permute-start | bytes 1572872 | tf_op jit(solution)/shard_map/ppermute | solution.py:248
  100.2 3.0 %collective-permute-start.12 = (bf16[4,256,128]{2,1,0:T(8,128)(2,1)S(1)}, bf16[4,256,128]{2,1,0:T(8,128)(2,1)S(1)}, u32[]{:S(2)}, u32[]{:S(2)}) collective-permute-start(bf16[4,256,128]{2,1,0:T(8,128)(2,1)S(1)} %get-tuple-element.21), channel_id=1, source_target_pairs={{0,32},{32,64},{64,96},{96,0},{128,160},{160,192},{192,224},{224,1... | collective-permute-start | bytes 786440 | tf_op jit(solution)/shard_map/ppermute | solution.py:249
  103.3 4.4 %collective-permute-start.13 = (bf16[4,256,128]{2,1,0:T(8,128)(2,1)S(1)}, bf16[4,256,128]{2,1,0:T(8,128)(2,1)S(1)}, u32[]{:S(2)}, u32[]{:S(2)}) collective-permute-start(bf16[4,256,128]{2,1,0:T(8,128)(2,1)S(1)} %get-tuple-element.22), channel_id=1, source_target_pairs={{0,96},{32,0},{64,32},{96,64},{128,224},{160,128},{192,160},{224,1... | collective-permute-start | bytes 786440 | tf_op jit(solution)/shard_map/ppermute | solution.py:250
  107.6 5.5 %collective-permute-done.12.left_ref = bf16[4,256,128]{2,1,0:T(8,128)(2,1)S(1)} collective-permute-done((bf16[4,256,128]{2,1,0:T(8,128)(2,1)S(1)}, bf16[4,256,128]{2,1,0:T(8,128)(2,1)S(1)}, u32[]{:S(2)}, u32[]{:S(2)}) %collective-permute-start.12) | collective-permute-done | bytes 262176 | tf_op jit(solution)/shard_map/ppermute | solution.py:249
  113.1 6.3 %collective-permute-done.13.right_ref = bf16[4,256,128]{2,1,0:T(8,128)(2,1)S(1)} collective-permute-done((bf16[4,256,128]{2,1,0:T(8,128)(2,1)S(1)}, bf16[4,256,128]{2,1,0:T(8,128)(2,1)S(1)}, u32[]{:S(2)}, u32[]{:S(2)}) %collective-permute-start.13) | collective-permute-done | bytes 262176 | tf_op jit(solution)/shard_map/ppermute | solution.py:250
  119.5 0.0 collective-permute-done.10.below_ref
  119.5 0.0 collective-permute-done.11.above_ref
  119.5 0.3 third.1
  119.7 25.5 %all_to_all.11.parts_ref = bf16[8,256,128]{2,1,0:T(8,128)(2,1)S(1)} all-to-all(bf16[8,256,128]{2,1,0:T(8,128)(2,1)S(1)} %third.1), channel_id=1, replica_groups={{0,64,288,352,512,576,800,864},{128,192,416,480,640,704,928,992},{32,96..., dimensions={0} | all-to-all | bytes 1048576 | tf_op jit(solution)/shard_map/all_to_all | solution.py:259
  145.3 0.8 last.1
  (3 shorter events, 0.0 us)
Async XLA Ops:
  0.0 19.1 %collective-permute-start.1 = (bf16[16,4096]{1,0:T(8,128)(2,1)}, bf16[16,4096]{1,0:T(8,128)(2,1)S(1)}, u32[]{:S(2)}, u32[]{:S(2)}) collective-permute-start(bf16[16,4096]{1,0:T(8,128)(2,1)} %param.7), channel_id=1, source_target_pairs={{0,20},{1,21},{2,22},{3,23},{4,24},{5,25},{6,26},{7,27},{8,28},{9,... | collective-permute-start | bytes 393224 | tf_op jit(solution)/shard_map/ppermute | solution.py:204
  6.2 12.9 %collective-permute-start = (bf16[16,4096]{1,0:T(8,128)(2,1)}, bf16[16,4096]{1,0:T(8,128)(2,1)S(1)}, u32[]{:S(2)}, u32[]{:S(2)}) collective-permute-start(bf16[16,4096]{1,0:T(8,128)(2,1)} %param.7), channel_id=1, source_target_pairs={{0,8},{1,9},{2,10},{3,11},{4,12},{5,13},{6,14},{7,15},{8,0},{9,1},... | collective-permute-start | bytes 393224 | tf_op jit(solution)/shard_map/ppermute | solution.py:204
  12.3 9.2 %collective-permute-start.2 = (bf16[16,4096]{1,0:T(8,128)(2,1)}, bf16[16,4096]{1,0:T(8,128)(2,1)S(1)}, u32[]{:S(2)}, u32[]{:S(2)}) collective-permute-start(bf16[16,4096]{1,0:T(8,128)(2,1)} %param.7), channel_id=1, source_target_pairs={{0,28},{1,29},{2,30},{3,31},{4,16},{5,17},{6,18},{7,19},{8,20},{9,... | collective-permute-start | bytes 393224 | tf_op jit(solution)/shard_map/ppermute | solution.py:204
  21.6 20.0 %collective-permute-start.5 = (bf16[64,4096]{1,0:T(8,128)(2,1)S(1)}, bf16[64,4096]{1,0:T(8,128)(2,1)S(1)}, u32[]{:S(2)}, u32[]{:S(2)}) collective-permute-start(bf16[64,4096]{1,0:T(8,128)(2,1)S(1)} %constant_dynamic-update-slice_fusion.refs_0_), channel_id=1, source_target_pairs={{0,16},{1,17},{2,18},{3,19},{4,20},{5,21},{6,22},{7,23},{8,24},{9,... | collective-permute-start | bytes 1572872 | tf_op jit(solution)/shard_map/ppermute | solution.py:204
  25.2 19.6 %collective-permute-start.4 = (bf16[64,4096]{1,0:T(8,128)(2,1)S(1)}, bf16[64,4096]{1,0:T(8,128)(2,1)S(1)}, u32[]{:S(2)}, u32[]{:S(2)}) collective-permute-start(bf16[64,4096]{1,0:T(8,128)(2,1)S(1)} %constant_dynamic-update-slice_fusion.refs_0_), channel_id=1, source_target_pairs={{0,14},{1,15},{2,0},{3,1},{4,2},{5,3},{6,4},{7,5},{8,6},{9,7},{10,... | collective-permute-start | bytes 1572872 | tf_op jit(solution)/shard_map/ppermute | solution.py:204
  30.0 16.7 %collective-permute-start.3 = (bf16[64,4096]{1,0:T(8,128)(2,1)S(1)}, bf16[64,4096]{1,0:T(8,128)(2,1)S(1)}, u32[]{:S(2)}, u32[]{:S(2)}) collective-permute-start(bf16[64,4096]{1,0:T(8,128)(2,1)S(1)} %constant_dynamic-update-slice_fusion.refs_0_), channel_id=1, source_target_pairs={{0,2},{1,3},{2,4},{3,5},{4,6},{5,7},{6,8},{7,9},{8,10},{9,11},{10,... | collective-permute-start | bytes 1572872 | tf_op jit(solution)/shard_map/ppermute | solution.py:204
  31.9 19.9 %collective-permute-start.6 = (bf16[64,4096]{1,0:T(8,128)(2,1)S(1)}, bf16[64,4096]{1,0:T(8,128)(2,1)S(1)}, u32[]{:S(2)}, u32[]{:S(2)}) collective-permute-start(bf16[64,4096]{1,0:T(8,128)(2,1)S(1)} %constant_dynamic-update-slice_fusion.refs_0_), channel_id=1, source_target_pairs={{0,1},{1,0},{2,3},{3,2},{4,5},{5,4},{6,7},{7,6},{8,9},{9,8},{10,11... | collective-permute-start | bytes 1572872 | tf_op jit(solution)/shard_map/ppermute | solution.py:204
  41.5 10.3 %collective-permute-start.9 = (bf16[64,4096]{1,0:T(8,128)(2,1)S(1)}, bf16[64,4096]{1,0:T(8,128)(2,1)S(1)}, u32[]{:S(2)}, u32[]{:S(2)}) collective-permute-start(bf16[64,4096]{1,0:T(8,128)(2,1)S(1)} %collective-permute-done.5.refs_3_), channel_id=1, source_target_pairs={{0,1},{1,0},{2,3},{3,2},{4,5},{5,4},{6,7},{7,6},{8,9},{9,8},{10,11... | collective-permute-start | bytes 1572872 | tf_op jit(solution)/shard_map/ppermute | solution.py:204
  44.8 7.1 %collective-permute-start.8 = (bf16[64,4096]{1,0:T(8,128)(2,1)S(1)}, bf16[64,4096]{1,0:T(8,128)(2,1)}, u32[]{:S(2)}, u32[]{:S(2)}) collective-permute-start(bf16[64,4096]{1,0:T(8,128)(2,1)S(1)} %collective-permute-done.4.refs_2_), channel_id=1, source_target_pairs={{0,1},{1,0},{2,3},{3,2},{4,5},{5,4},{6,7},{7,6},{8,9},{9,8},{10,11... | collective-permute-start | bytes 1572872 | tf_op jit(solution)/shard_map/ppermute | solution.py:204
  46.8 5.3 %collective-permute-start.7 = (bf16[64,4096]{1,0:T(8,128)(2,1)S(1)}, bf16[64,4096]{1,0:T(8,128)(2,1)}, u32[]{:S(2)}, u32[]{:S(2)}) collective-permute-start(bf16[64,4096]{1,0:T(8,128)(2,1)S(1)} %collective-permute-done.3.refs_1_), channel_id=1, source_target_pairs={{0,1},{1,0},{2,3},{3,2},{4,5},{5,4},{6,7},{7,6},{8,9},{9,8},{10,11... | collective-permute-start | bytes 1572872 | tf_op jit(solution)/shard_map/ppermute | solution.py:204
  52.1 0.9 copy-start
  53.0 0.9 copy-start.1
  84.1 35.4 %collective-permute-start.10 = (bf16[8,256,128]{2,1,0:T(8,128)(2,1)S(1)}, bf16[8,256,128]{2,1,0:T(8,128)(2,1)S(1)}, u32[]{:S(2)}, u32[]{:S(2)}) collective-permute-start(bf16[8,256,128]{2,1,0:T(8,128)(2,1)S(1)} %get-tuple-element.19), channel_id=1, source_target_pairs={{0,128},{32,160},{64,192},{96,224},{128,256},{160,288},{192,320},{... | collective-permute-start | bytes 1572872 | tf_op jit(solution)/shard_map/ppermute | solution.py:247
  88.9 30.6 %collective-permute-start.11 = (bf16[8,256,128]{2,1,0:T(8,128)(2,1)S(1)}, bf16[8,256,128]{2,1,0:T(8,128)(2,1)S(1)}, u32[]{:S(2)}, u32[]{:S(2)}) collective-permute-start(bf16[8,256,128]{2,1,0:T(8,128)(2,1)S(1)} %get-tuple-element.20), channel_id=1, source_target_pairs={{0,896},{32,928},{64,960},{96,992},{128,0},{160,32},{192,64},{224,... | collective-permute-start | bytes 1572872 | tf_op jit(solution)/shard_map/ppermute | solution.py:248
  100.2 12.9 %collective-permute-start.12 = (bf16[4,256,128]{2,1,0:T(8,128)(2,1)S(1)}, bf16[4,256,128]{2,1,0:T(8,128)(2,1)S(1)}, u32[]{:S(2)}, u32[]{:S(2)}) collective-permute-start(bf16[4,256,128]{2,1,0:T(8,128)(2,1)S(1)} %get-tuple-element.21), channel_id=1, source_target_pairs={{0,32},{32,64},{64,96},{96,0},{128,160},{160,192},{192,224},{224,1... | collective-permute-start | bytes 786440 | tf_op jit(solution)/shard_map/ppermute | solution.py:249
  103.3 16.2 %collective-permute-start.13 = (bf16[4,256,128]{2,1,0:T(8,128)(2,1)S(1)}, bf16[4,256,128]{2,1,0:T(8,128)(2,1)S(1)}, u32[]{:S(2)}, u32[]{:S(2)}) collective-permute-start(bf16[4,256,128]{2,1,0:T(8,128)(2,1)S(1)} %get-tuple-element.22), channel_id=1, source_target_pairs={{0,96},{32,0},{64,32},{96,64},{128,224},{160,128},{192,160},{224,1... | collective-permute-start | bytes 786440 | tf_op jit(solution)/shard_map/ppermute | solution.py:250

commit v2 on v1

v2 whole, which is shorter than its diff:
```python
import jax
import jax.numpy as jnp
from jax import lax
from jax.experimental import pallas as pl
from jax.experimental.pallas import tpu as pltpu
from jax.sharding import PartitionSpec as P

D = 8192
EPS = 1e-05
NX, NY, NC = 2, 8, 2
NZ, NH = 8, 4
SHARD = 16
PIECE = 64
HALF = 256
VMEM = pl.BlockSpec(memory_space=pltpu.VMEM)
SMEM = pl.BlockSpec(memory_space=pltpu.SMEM)
ANY = pl.BlockSpec(memory_space=pl.ANY)
PARAMS = pltpu.CompilerParams(vmem_limit_bytes=16 * 1024 * 1024)


def fsdp_of(x, y, c):
    return (x % NX * NY + y % NY) * NC + c % NC


def fsdp_perm(step):
    return [
        (fsdp_of(x, y, c), fsdp_of(*step(x, y, c)))
        for x in range(NX)
        for y in range(NY)
        for c in range(NC)
    ]


def rep_of(z, h):
    return z % NZ * NH + h % NH


def rep_perm(step):
    return [(rep_of(z, h), rep_of(*step(z, h))) for z in range(NZ) for h in range(NH)]


def even_partner(i):
    return i ^ 1


def odd_partner(i):
    return ((i + 1) ^ 1) - 1


def chip_of(q, j):
    x = j // 2
    return x, (q + 2 * x) % 4 + 4 * (j % 2)


TEAMS = [[fsdp_of(*chip_of(q, j), c) for j in range(4)] for q in range(4) for c in range(NC)]
CLASSES = [
    [rep_of(z, h) for z in range(NZ) for h in range(NH) if (z + 2 * h) % 4 == q]
    for q in range(4)
]
BLOCKS = [fsdp_of(*chip_of(q, j), c) for c in range(NC) for q in range(4) for j in range(4)]


def piece_colors(me):
    x, y = me // (NY * NC), (me // NC) % NY
    own = (y + 2 * x) % 4
    to_even = 1 + 2 * (y % 2)
    return [own, (own + to_even) % 4, (own + 4 - to_even) % 4, (own + 2) % 4]


def piece_rows(first, color):
    return pl.ds(pl.multiple_of(first + color * PIECE, PIECE), PIECE)


def prep_kernel(len_ref, after_ref, res_ref, cot_ref, gain_ref, res_out, weighted_ref):
    gain = gain_ref[...].astype(jnp.float32)
    for i, block in enumerate(BLOCKS):
        token = block * SHARD + lax.broadcasted_iota(jnp.int32, (SHARD, 1), 0)
        live = (token < len_ref[0]).astype(jnp.float32)
        there = pl.ds(i * SHARD, SHARD)
        here = pl.ds(block * SHARD, SHARD)
        weighted_ref[there, :] = cot_ref[here, :].astype(jnp.float32) * gain * live
        res_out[there, :] = res_ref[here, :].astype(jnp.float32)


def products(pieces, w_ref, t_ref):
    a = jnp.concatenate([piece[...] for piece in pieces], axis=0)
    return (
        jnp.dot(a, w_ref[...], preferred_element_type=jnp.float32),
        jnp.dot(a, t_ref[...], preferred_element_type=jnp.float32),
    )


def near_kernel(p0, p1, p2, p3, w_ref, t_ref, s_ref, m_ref):
    s_ref[...], m_ref[...] = products((p0, p1, p2, p3), w_ref, t_ref)


def far_kernel(
    me_ref, p0, p1, p2, p3, w_ref, t_ref, near_s_ref, near_m_ref, res_ref, weighted_ref,
    stream_ref, moved_ref, stats_ref,
):
    me = me_ref[0]
    core = me % NC
    s, m = products((p0, p1, p2, p3), w_ref, t_ref)
    for i, color in enumerate(piece_colors(me)):
        here = slice(i * PIECE, (i + 1) * PIECE)
        near = piece_rows(core * HALF, color)
        far = piece_rows((1 - core) * HALF, color)
        stream_ref[near, :] = near_s_ref[here, :]
        moved_ref[near, :] = near_m_ref[here, :]
        stream_ref[far, :] = s[here]
        moved_ref[far, :] = m[here]
    stream = stream_ref[...] + res_ref[...]
    stream_ref[...] = stream
    moved = moved_ref[...]
    weighted = weighted_ref[...]
    sums = [
        jnp.sum(stream * stream, axis=1, keepdims=True),
        jnp.sum(weighted * stream, axis=1, keepdims=True),
        jnp.sum(weighted * moved, axis=1, keepdims=True),
        jnp.sum(stream * moved, axis=1, keepdims=True),
    ]
    lane = lax.broadcasted_iota(jnp.int32, (2 * HALF, 128), 1)
    table = jnp.zeros((2 * HALF, 128), jnp.float32)
    for i, value in enumerate(sums):
        table = jnp.where(lane == i, value, table)
    turned = table.T
    packed = jnp.concatenate([turned[:4, :HALF], turned[:4, HALF:]], axis=0)
    for i in range(stats_ref.shape[0]):
        stats_ref[i] = packed


def second_kernel(
    ids_ref, stats_ref, stream_ref, moved_ref, weighted_ref,
    n0, n1, n2, n3, f0, f1, f2, f3,
    own_ref, even_ref, odd_ref, first_ref, later_ref, curv_ref,
):
    total = jnp.sum(stats_ref[...], axis=0)
    coefs = []
    for h in range(2):
        sum_sq, along_c, tangent_c, cross = (
            total[4 * h + i : 4 * h + i + 1] for i in range(4)
        )
        inv = lax.rsqrt(sum_sq / D + EPS)
        inv3 = inv * inv * inv
        inv5 = inv3 * inv * inv
        share = cross / D
        coefs.append(-inv3 * share)
        coefs.append((3.0 * inv5 * share * along_c - inv3 * tangent_c) / D)
        coefs.append(-inv3 * along_c / D)
    coefs.append(jnp.zeros((128 - len(coefs), HALF), jnp.float32))
    turned = jnp.concatenate(coefs, axis=0).T
    for h in range(2):
        rows = pl.ds(h * HALF, HALF)
        curv_ref[rows, :] = (
            turned[:, 3 * h : 3 * h + 1] * weighted_ref[rows, :]
            + turned[:, 3 * h + 1 : 3 * h + 2] * stream_ref[rows, :]
            + turned[:, 3 * h + 2 : 3 * h + 3] * moved_ref[rows, :]
        )
    me = ids_ref[0]
    core = me % NC
    colors = piece_colors(me)
    curv = jnp.concatenate(
        [curv_ref[piece_rows(core * HALF, q), :] for q in colors]
        + [curv_ref[piece_rows((1 - core) * HALF, q), :] for q in colors],
        axis=0,
    )
    curv_t = curv.T.astype(jnp.bfloat16)
    pieces = (n0, n1, n2, n3, f0, f1, f2, f3)
    color = ids_ref[1]
    to_even = 1 + 2 * (color % 2)
    for what, step in (("even", to_even), ("odd", 4 - to_even), ("side", 2), ("own", 0)):
        q = (color + step) % 4
        for pair in range(4):
            z = 2 * pair + q % 2
            h = ((z - q + 8) % 4) // 2
            columns = []
            for k in range(2):
                at = pl.ds(pl.multiple_of((z * NH + h + 2 * k) * 128, 128), 128)
                columns.append(jnp.concatenate([p[:, at] for p in pieces], axis=0))
            out = jnp.dot(
                curv_t,
                jnp.concatenate(columns, axis=1),
                preferred_element_type=jnp.float32,
            ).astype(jnp.bfloat16)
            for k in range(2):
                i = 2 * pair + k
                value = out[:, 128 * k : 128 * k + 128]
                if what == "own":
                    own_ref[i] = value
                elif what == "even":
                    even_ref[i] = value
                elif what == "odd":
                    odd_ref[i] = value
                elif i < 4:
                    first_ref[i] = value
                else:
                    later_ref[i - 4] = value


def third_kernel(own_ref, even_ref, odd_ref, first_ref, later_ref, out_ref):
    f32 = jnp.float32
    for i in range(8):
        side = first_ref[i] if i < 4 else later_ref[i - 4]
        out_ref[i] = (
            own_ref[i].astype(f32)
            + even_ref[i].astype(f32)
            + odd_ref[i].astype(f32)
            + side.astype(f32)
        ).astype(out_ref.dtype)


def last_kernel(parts_ref, out_ref):
    total = parts_ref[0].astype(jnp.float32)
    for i in range(1, parts_ref.shape[0]):
        total = total + parts_ref[i].astype(jnp.float32)
    out_ref[...] = total.T.astype(out_ref.dtype)


def local(attn_out, residual, out_weight, tangent, norm_gain, cotangent, seq_len):
    f32, bf16 = jnp.float32, jnp.bfloat16
    rows, columns = residual.shape
    features = attn_out.shape[1]
    me = lax.axis_index("fsdp")
    rep = lax.axis_index("rep")
    color = (rep // NH + 2 * (rep % NH)) % 4
    ids = jnp.stack([me, color]).astype(jnp.int32)
    gain = norm_gain[None, :]

    def in_group(x, step):
        return lax.ppermute(x, "fsdp", fsdp_perm(step))

    def of_groups(x, step):
        return lax.ppermute(x, "rep", rep_perm(step))

    def shape(*dims, dtype=f32):
        return jax.ShapeDtypeStruct(dims, dtype)

    own = lax.all_to_all(
        jnp.broadcast_to(attn_out[None], (4, SHARD, features)),
        "fsdp", 0, 0, axis_index_groups=TEAMS,
    ).reshape(PIECE, features)
    near = [
        own,
        in_group(own, lambda x, y, c: (x, even_partner(y), c)),
        in_group(own, lambda x, y, c: (x, odd_partner(y), c)),
        in_group(own, lambda x, y, c: (x + 1, y, c)),
    ]
    res, weighted = pl.pallas_call(
        prep_kernel,
        out_shape=(shape(rows, columns), shape(rows, columns)),
        in_specs=[SMEM, ANY, VMEM, VMEM, VMEM],
        out_specs=(VMEM,) * 2,
        compiler_params=PARAMS,
        name="prep",
    )(seq_len, own, residual, cotangent, gain)
    near[3], res = lax.optimization_barrier((near[3], res))

    far = [in_group(piece, lambda x, y, c: (x, y, c + 1)) for piece in near]

    near_s, near_m = pl.pallas_call(
        near_kernel,
        out_shape=(shape(HALF, columns), shape(HALF, columns)),
        in_specs=[VMEM] * 6,
        out_specs=(VMEM,) * 2,
        compiler_params=PARAMS,
        name="near",
    )(*near, out_weight, tangent)

    stream, moved, stats = pl.pallas_call(
        far_kernel,
        out_shape=(shape(rows, columns), shape(rows, columns), shape(32, 8, HALF)),
        in_specs=[SMEM] + [VMEM] * 10,
        out_specs=(VMEM,) * 3,
        compiler_params=PARAMS,
        name="far",
    )(ids, *far, out_weight, tangent, near_s, near_m, res, weighted)

    stats = lax.all_to_all(stats, "fsdp", 0, 0)

    whole = shape(8, columns, 128, dtype=bf16)
    part = shape(4, columns, 128, dtype=bf16)
    mine, even, odd, first, later = pl.pallas_call(
        second_kernel,
        out_shape=(whole, whole, whole, part, part),
        in_specs=[SMEM] + [VMEM] * 12,
        out_specs=(VMEM,) * 5,
        scratch_shapes=[pltpu.VMEM((rows, columns), f32)],
        compiler_params=PARAMS,
        name="second",
    )(ids, stats, stream, moved, weighted, *near, *far)

    even = of_groups(even, lambda z, h: (even_partner(z), h))
    odd = of_groups(odd, lambda z, h: (odd_partner(z), h))
    first = of_groups(first, lambda z, h: (z, even_partner(h)))
    later = of_groups(later, lambda z, h: (z, odd_partner(h)))
    four = pl.pallas_call(
        third_kernel,
        out_shape=whole,
        in_specs=[VMEM] * 5,
        out_specs=VMEM,
        compiler_params=PARAMS,
        name="third",
    )(mine, even, odd, first, later)
    parts = lax.all_to_all(four, "rep", 0, 0, axis_index_groups=CLASSES)
    return pl.pallas_call(
        last_kernel,
        out_shape=shape(128, columns, dtype=bf16),
        in_specs=[VMEM],
        out_specs=VMEM,
        compiler_params=PARAMS,
        name="last",
    )(parts)


def solution(mesh):
    in_specs = (
        P(("rep", "fsdp"), None),
        P("rep", "fsdp"),
        P(None, "fsdp"),
        P(None, "fsdp"),
        P("fsdp"),
        P("rep", "fsdp"),
        P("rep"),
    )
    out_specs = P("rep", "fsdp")
    return jax.shard_map(local, mesh=mesh, in_specs=in_specs, out_specs=out_specs, check_vma=False)
```

time: 147 us -> 148 us (level)
  blocking collectives: 44.1 us -> 66.6 us
  starting transfers between devices: 69.3 us -> 51.2 us
  waiting for transfers between devices: 15.6 us -> 11.2 us
  local copies, waits for them, and re-layouts: 3.51 us -> 6.83 us
  Pallas kernels: 12.5 us -> 10.9 us
    all_to_all x0 -> x1, blocking collectives: none -> 23.6 us  [local(): lax.all_to_all(jnp.broadcast_to(attn_out[None], (4, SHARD, features)), 'f...]
    ppermute x14 -> x11, starting transfers between devices: 69.3 us -> 51.2 us  [the longest x4 30.1 us: of_groups(): return lax.ppermute(x, 'rep', rep_perm(step))]
    ppermute x14 -> x11, waiting for transfers between devices: 15.6 us -> 11.2 us  [the longest x4 11.2 us: of_groups(): return lax.ppermute(x, 'rep', rep_perm(step))]
    unnamed x7 -> x16, local copies, waits for them, and re-layouts: 2.84 us -> 5.08 us
    all_to_all x1, blocking collectives: 18.6 us -> 16.9 us  [local(): stats = lax.all_to_all(stats, 'fsdp', 0, 0)]
    pallas_call x2 -> x4, Pallas kernels: 8.05 us -> 6.72 us  [the longest x1 3.32 us: local(): pl.pallas_call(far_kernel, out_shape=(shape(rows, columns), shape(rows, c...]
  transfers between devices with their start and end apart: 14 -> 11, of which waited for: 5 -> 2; matrix products, arithmetic and copies ran while one was open for 1% -> 0% of each run, Pallas kernels for 0% -> 2%
where the time goes in v2:
time: 148 us
  blocking collectives  66.6 us (45%)
  starting transfers between devices  51.2 us (35%)
  waiting for transfers between devices  11.2 us (8%)
  Pallas kernels  10.9 us (7%)
  local copies, waits for them, and re-layouts  6.83 us (5%)
    ppermute x4, starting transfers between devices, of_groups(): return lax.ppermute(x, 'rep', rep_perm(step))  30.1 us
    all_to_all x1, blocking collectives, local(): parts = lax.all_to_all(four, 'rep', 0, 0, axis_index_groups=CLASSES)  26 us
    all_to_all x1, blocking collectives, local(): lax.all_to_all(jnp.broadcast_to(attn_out[None], (4, SHARD, features)), 'f...  23.6 us
    ppermute x7, starting transfers between devices, in_group(): return lax.ppermute(x, 'fsdp', fsdp_perm(step))  21.1 us
    all_to_all x1, blocking collectives, local(): stats = lax.all_to_all(stats, 'fsdp', 0, 0)  16.9 us
    ppermute x4, waiting for transfers between devices, of_groups(): return lax.ppermute(x, 'rep', rep_perm(step))  11.2 us
    unnamed x16, local copies, waits for them, and re-layouts  5.08 us
    pallas_call x1, Pallas kernels, local(): pl.pallas_call(second_kernel, out_shape=(whole, whole, whole, part, part)...  3.96 us
  transfers between devices with their start and end apart: 11, of which 2 were waited for; matrix products, arithmetic and copies ran while one was open for 0% of the time, Pallas kernels for 2%

profile of v2, /device:TPU:1, one launch (start us, length us, event | category | flops | bytes accessed | tf_op | source)
XLA Modules:
  0.0 147.8 jit_solution(7642971136992991188)
XLA Ops:
  0.0 0.0 copy-start
  0.0 1.1 broadcast_in_dim.4
  1.1 23.6 %all_to_all.15 = bf16[4,16,4096]{2,1,0:T(8,128)(2,1)S(1)} all-to-all(bf16[4,16,4096]{2,1,0:T(8,128)(2,1)S(1)} %broadcast_in_dim.4), channel_id=1, replica_groups={{0,8,20,28},{1,9,21,29},{2,10,22,30},{3,11,23,31},{4,12,16,24},{5,13,17..., dimensions={0} | all-to-all | bytes 1048576 | tf_op jit(solution)/shard_map/all_to_all | solution.py:238
  24.7 1.9 %collective-permute-start.5 = (bf16[64,4096]{1,0:T(8,128)(2,1)S(1)}, bf16[64,4096]{1,0:T(8,128)(2,1)S(1)}, u32[]{:S(2)}, u32[]{:S(2)}) collective-permute-start(bf16[64,4096]{1,0:T(8,128)(2,1)S(1)} %bitcast.3), channel_id=1, source_target_pairs={{0,16},{1,17},{2,18},{3,19},{4,20},{5,21},{6,22},{7,23},{8,24},{9,... | collective-permute-start | bytes 1572872 | tf_op jit(solution)/shard_map/ppermute | solution.py:230
  26.6 1.9 %collective-permute-start.3 = (bf16[64,4096]{1,0:T(8,128)(2,1)S(1)}, bf16[64,4096]{1,0:T(8,128)(2,1)}, u32[]{:S(2)}, u32[]{:S(2)}) collective-permute-start(bf16[64,4096]{1,0:T(8,128)(2,1)S(1)} %bitcast.4), channel_id=1, source_target_pairs={{0,14},{1,15},{2,4},{3,5},{4,2},{5,3},{6,8},{7,9},{8,6},{9,7},{10,... | collective-permute-start | bytes 1572872 | tf_op jit(solution)/shard_map/ppermute | solution.py:230
  28.6 5.4 %collective-permute-start.1 = (bf16[64,4096]{1,0:T(8,128)(2,1)S(1)}, bf16[64,4096]{1,0:T(8,128)(2,1)}, u32[]{:S(2)}, u32[]{:S(2)}) collective-permute-start(bf16[64,4096]{1,0:T(8,128)(2,1)S(1)} %bitcast.5), channel_id=1, source_target_pairs={{0,2},{1,3},{2,0},{3,1},{4,6},{5,7},{6,4},{7,5},{8,10},{9,11},{10,... | collective-permute-start | bytes 1572872 | tf_op jit(solution)/shard_map/ppermute | solution.py:230
  34.6 0.7 broadcast_in_dim.10.gain_ref
  35.3 4.3 %collective-permute-start = (bf16[64,4096]{1,0:T(8,128)(2,1)S(1)}, bf16[64,4096]{1,0:T(8,128)(2,1)}, u32[]{:S(2)}, u32[]{:S(2)}) collective-permute-start(bf16[64,4096]{1,0:T(8,128)(2,1)S(1)} %bitcast.6), channel_id=1, source_target_pairs={{0,1},{1,0},{2,3},{3,2},{4,5},{5,4},{6,7},{7,6},{8,9},{9,8},{10,11... | collective-permute-start | bytes 1572872 | tf_op jit(solution)/shard_map/ppermute | solution.py:230
  39.6 0.0 copy-start.6
  39.6 0.9 copy-done.6
  40.5 0.0 copy-start.7
  40.6 0.9 copy-done.7
  41.5 0.1 prep.1
  41.6 0.0 copy-start.2
  41.6 0.8 copy-done.2
  42.4 0.0 copy-start.4
  42.4 0.8 copy-done.4
  43.2 0.0 collective-permute-done.5.p3.n3
  43.2 0.0 collective-permute-done.3.p2.n2
  43.2 2.9 %collective-permute-start.4 = (bf16[64,4096]{1,0:T(8,128)(2,1)}, bf16[64,4096]{1,0:T(8,128)(2,1)}, u32[]{:S(2)}, u32[]{:S(2)}) collective-permute-start(bf16[64,4096]{1,0:T(8,128)(2,1)} %collective-permute-done.3.p2.n2), channel_id=1, source_target_pairs={{0,1},{1,0},{2,3},{3,2},{4,5},{5,4},{6,7},{7,6},{8,9},{9,8},{10,11... | collective-permute-start | bytes 1572872 | tf_op jit(solution)/shard_map/ppermute | solution.py:230
  46.1 0.0 collective-permute-done.1.p1.n1
  46.1 2.7 %collective-permute-start.2 = (bf16[64,4096]{1,0:T(8,128)(2,1)}, bf16[64,4096]{1,0:T(8,128)(2,1)}, u32[]{:S(2)}, u32[]{:S(2)}) collective-permute-start(bf16[64,4096]{1,0:T(8,128)(2,1)} %collective-permute-done.1.p1.n1), channel_id=1, source_target_pairs={{0,1},{1,0},{2,3},{3,2},{4,5},{5,4},{6,7},{7,6},{8,9},{9,8},{10,11... | collective-permute-start | bytes 1572872 | tf_op jit(solution)/shard_map/ppermute | solution.py:230
  48.8 1.9 %collective-permute-start.6 = (bf16[64,4096]{1,0:T(8,128)(2,1)S(1)}, bf16[64,4096]{1,0:T(8,128)(2,1)}, u32[]{:S(2)}, u32[]{:S(2)}) collective-permute-start(bf16[64,4096]{1,0:T(8,128)(2,1)S(1)} %collective-permute-done.5.p3.n3), channel_id=1, source_target_pairs={{0,1},{1,0},{2,3},{3,2},{4,5},{5,4},{6,7},{7,6},{8,9},{9,8},{10,11... | collective-permute-start | bytes 1572872 | tf_op jit(solution)/shard_map/ppermute | solution.py:230
  50.8 0.1 pad_add_fusion.me_ref.ids_ref
  50.9 0.0 copy-done
  50.9 0.0 copy-start.1
  50.9 1.6 %copy-done.1 = bf16[4096,256]{1,0:T(8,128)(2,1)S(1)} copy-done((bf16[4096,256]{1,0:T(8,128)(2,1)S(1)}, bf16[4096,256]{1,0:T(8,128)(2,1)}, u32[]{:S(2)}) %copy-start.1) | copy-done | bytes 2097176
  52.5 0.0 copy-start.3
  52.5 0.0 copy-start.5
  52.5 2.5 %near.1 = (f32[256,256]{1,0:T(8,128)S(1)}, f32[256,256]{1,0:T(8,128)S(1)}) custom-call(bf16[64,4096]{1,0:T(8,128)(2,1)S(1)} %bitcast.8, bf16[64,4096]{1,0:T(8,128)(2,1)} %collective-permute-done.1.p1.n1, bf16[64,4096]{1,0:T(8,128)(2,1)} %collective-permute-done.3.p2.n2, bf16[64,4096]{1,0:T(8,128)(2,1)S(1)} %collective-permute-done.5.p3.n3, ...), custom_call_target="tpu_custom_call" | custom-call | tf_op jit(solution)/shard_map/near/pallas_call | solution.py:260
  55.0 0.0 collective-permute-done.p0.f0
  55.0 0.0 collective-permute-done.4.p2.f2
  55.0 0.0 collective-permute-done.2.p1.f1
  55.0 0.0 collective-permute-done.6.p3.f3
  55.1 0.0 copy-done.3
  55.1 0.0 copy-done.5
  55.1 3.3 %far.1 = (f32[512,256]{1,0:T(8,128)S(1)}, f32[512,256]{1,0:T(8,128)S(1)}, f32[32,8,256]{2,1,0:T(8,128)S(1)}) custom-call(s32[2]{0:T(128)S(1)} %pad_add_fusion.me_ref.ids_ref, bf16[64,4096]{1,0:T(8,128)(2,1)} %collective-permute-done.p0.f0, bf16[64,4096]{1,0:T(8,128)(2,1)} %collective-permute-done.2.p1.f1, bf16[64,4096]{1,0:T(8,128)(2,1)} %collective-permute-done.4.p2.f2, ...), custom_call_target="tpu_custom_call" | custom-call | tf_op jit(solution)/shard_map/far/pallas_call | solution.py:269
  58.4 16.9 %all_to_all.16.stats_ref = f32[32,8,256]{2,1,0:T(8,128)S(1)} all-to-all(f32[32,8,256]{2,1,0:T(8,128)S(1)} %get-tuple-element.25), channel_id=1, replica_groups=mesh['rep'=32,'fsdp'=32] {'fsdp'}, dimensions={0} | all-to-all | bytes 524288 | tf_op jit(solution)/shard_map/all_to_all | solution.py:278
  75.4 4.0 %second.1 = (bf16[8,256,128]{2,1,0:T(8,128)(2,1)S(1)}, bf16[8,256,128]{2,1,0:T(8,128)(2,1)S(1)}, bf16[8,256,128]{2,1,0:T(8,128)(2,1)S(1)}, bf16[4,256,128]{2,1,0:T(8,128)(2,1)S(1)}, bf16[4,256,128]{2,1,0:T(8,128)(2,1)S(1)}) custom-call(s32[2]{0:T(128)S(1)} %pad_add_fusion.me_ref.ids_ref, f32[32,8,256]{2,1,0:T(8,128)S(1)} %all_to_all.16.stats_ref, ...), custom_call_target="tpu_custom_call" | custom-call | tf_op jit(solution)/shard_map/second/pallas_call | solution.py:282
  79.3 4.8 %collective-permute-start.7 = (bf16[8,256,128]{2,1,0:T(8,128)(2,1)S(1)}, bf16[8,256,128]{2,1,0:T(8,128)(2,1)S(1)}, u32[]{:S(2)}, u32[]{:S(2)}) collective-permute-start(bf16[8,256,128]{2,1,0:T(8,128)(2,1)S(1)} %get-tuple-element.29), channel_id=1, source_target_pairs={{0,128},{32,160},{64,192},{96,224},{128,0},{160,32},{192,64},{224,... | collective-permute-start | bytes 1572872 | tf_op jit(solution)/shard_map/ppermute | solution.py:233
  84.1 14.9 %collective-permute-start.8 = (bf16[8,256,128]{2,1,0:T(8,128)(2,1)S(1)}, bf16[8,256,128]{2,1,0:T(8,128)(2,1)S(1)}, u32[]{:S(2)}, u32[]{:S(2)}) collective-permute-start(bf16[8,256,128]{2,1,0:T(8,128)(2,1)S(1)} %get-tuple-element.30), channel_id=1, source_target_pairs={{0,896},{32,928},{64,960},{96,992},{128,256},{160,288},{192,320},{... | collective-permute-start | bytes 1572872 | tf_op jit(solution)/shard_map/ppermute | solution.py:233
  99.0 4.8 %collective-permute-start.9 = (bf16[4,256,128]{2,1,0:T(8,128)(2,1)S(1)}, bf16[4,256,128]{2,1,0:T(8,128)(2,1)S(1)}, u32[]{:S(2)}, u32[]{:S(2)}) collective-permute-start(bf16[4,256,128]{2,1,0:T(8,128)(2,1)S(1)} %get-tuple-element.31), channel_id=1, source_target_pairs={{0,32},{32,0},{64,96},{96,64},{128,160},{160,128},{192,224},{224,1... | collective-permute-start | bytes 786440 | tf_op jit(solution)/shard_map/ppermute | solution.py:233
  103.8 5.7 %collective-permute-start.10 = (bf16[4,256,128]{2,1,0:T(8,128)(2,1)S(1)}, bf16[4,256,128]{2,1,0:T(8,128)(2,1)S(1)}, u32[]{:S(2)}, u32[]{:S(2)}) collective-permute-start(bf16[4,256,128]{2,1,0:T(8,128)(2,1)S(1)} %get-tuple-element.32), channel_id=1, source_target_pairs={{0,96},{32,64},{64,32},{96,0},{128,224},{160,192},{192,160},{224,1... | collective-permute-start | bytes 786440 | tf_op jit(solution)/shard_map/ppermute | solution.py:233
  109.5 6.4 %collective-permute-done.9.first_ref = bf16[4,256,128]{2,1,0:T(8,128)(2,1)S(1)} collective-permute-done((bf16[4,256,128]{2,1,0:T(8,128)(2,1)S(1)}, bf16[4,256,128]{2,1,0:T(8,128)(2,1)S(1)}, u32[]{:S(2)}, u32[]{:S(2)}) %collective-permute-start.9) | collective-permute-done | bytes 262176 | tf_op jit(solution)/shard_map/ppermute | solution.py:233
  115.9 4.8 %collective-permute-done.10.later_ref = bf16[4,256,128]{2,1,0:T(8,128)(2,1)S(1)} collective-permute-done((bf16[4,256,128]{2,1,0:T(8,128)(2,1)S(1)}, bf16[4,256,128]{2,1,0:T(8,128)(2,1)S(1)}, u32[]{:S(2)}, u32[]{:S(2)}) %collective-permute-start.10) | collective-permute-done | bytes 262176 | tf_op jit(solution)/shard_map/ppermute | solution.py:233
  120.7 0.0 collective-permute-done.7.even_ref
  120.7 0.0 collective-permute-done.8.odd_ref
  120.7 0.3 third.1
  121.0 26.0 %all_to_all.17.parts_ref = bf16[8,256,128]{2,1,0:T(8,128)(2,1)S(1)} all-to-all(bf16[8,256,128]{2,1,0:T(8,128)(2,1)S(1)} %third.1), channel_id=1, replica_groups={{0,64,288,352,512,576,800,864},{128,192,416,480,640,704,928,992},{32,96..., dimensions={0} | all-to-all | bytes 1048576 | tf_op jit(solution)/shard_map/all_to_all | solution.py:304
  147.0 0.8 last.1
Async XLA Ops:
  0.0 50.9 %copy-start = (bf16[4096,256]{1,0:T(8,128)(2,1)S(1)}, bf16[4096,256]{1,0:T(8,128)(2,1)}, u32[]{:S(2)}) copy-start(bf16[4096,256]{1,0:T(8,128)(2,1)} %w_ref.3) | copy-start | bytes 6291460
  24.7 18.5 %collective-permute-start.5 = (bf16[64,4096]{1,0:T(8,128)(2,1)S(1)}, bf16[64,4096]{1,0:T(8,128)(2,1)S(1)}, u32[]{:S(2)}, u32[]{:S(2)}) collective-permute-start(bf16[64,4096]{1,0:T(8,128)(2,1)S(1)} %bitcast.3), channel_id=1, source_target_pairs={{0,16},{1,17},{2,18},{3,19},{4,20},{5,21},{6,22},{7,23},{8,24},{9,... | collective-permute-start | bytes 1572872 | tf_op jit(solution)/shard_map/ppermute | solution.py:230
  26.6 16.6 %collective-permute-start.3 = (bf16[64,4096]{1,0:T(8,128)(2,1)S(1)}, bf16[64,4096]{1,0:T(8,128)(2,1)}, u32[]{:S(2)}, u32[]{:S(2)}) collective-permute-start(bf16[64,4096]{1,0:T(8,128)(2,1)S(1)} %bitcast.4), channel_id=1, source_target_pairs={{0,14},{1,15},{2,4},{3,5},{4,2},{5,3},{6,8},{7,9},{8,6},{9,7},{10,... | collective-permute-start | bytes 1572872 | tf_op jit(solution)/shard_map/ppermute | solution.py:230
  28.6 17.5 %collective-permute-start.1 = (bf16[64,4096]{1,0:T(8,128)(2,1)S(1)}, bf16[64,4096]{1,0:T(8,128)(2,1)}, u32[]{:S(2)}, u32[]{:S(2)}) collective-permute-start(bf16[64,4096]{1,0:T(8,128)(2,1)S(1)} %bitcast.5), channel_id=1, source_target_pairs={{0,2},{1,3},{2,0},{3,1},{4,6},{5,7},{6,4},{7,5},{8,10},{9,11},{10,... | collective-permute-start | bytes 1572872 | tf_op jit(solution)/shard_map/ppermute | solution.py:230
  35.3 19.7 %collective-permute-start = (bf16[64,4096]{1,0:T(8,128)(2,1)S(1)}, bf16[64,4096]{1,0:T(8,128)(2,1)}, u32[]{:S(2)}, u32[]{:S(2)}) collective-permute-start(bf16[64,4096]{1,0:T(8,128)(2,1)S(1)} %bitcast.6), channel_id=1, source_target_pairs={{0,1},{1,0},{2,3},{3,2},{4,5},{5,4},{6,7},{7,6},{8,9},{9,8},{10,11... | collective-permute-start | bytes 1572872 | tf_op jit(solution)/shard_map/ppermute | solution.py:230
  39.6 1.0 copy-start.6
  40.5 0.9 copy-start.7
  41.6 0.8 copy-start.2
  42.4 0.8 copy-start.4
  43.2 11.8 %collective-permute-start.4 = (bf16[64,4096]{1,0:T(8,128)(2,1)}, bf16[64,4096]{1,0:T(8,128)(2,1)}, u32[]{:S(2)}, u32[]{:S(2)}) collective-permute-start(bf16[64,4096]{1,0:T(8,128)(2,1)} %collective-permute-done.3.p2.n2), channel_id=1, source_target_pairs={{0,1},{1,0},{2,3},{3,2},{4,5},{5,4},{6,7},{7,6},{8,9},{9,8},{10,11... | collective-permute-start | bytes 1572872 | tf_op jit(solution)/shard_map/ppermute | solution.py:230
  46.1 8.9 %collective-permute-start.2 = (bf16[64,4096]{1,0:T(8,128)(2,1)}, bf16[64,4096]{1,0:T(8,128)(2,1)}, u32[]{:S(2)}, u32[]{:S(2)}) collective-permute-start(bf16[64,4096]{1,0:T(8,128)(2,1)} %collective-permute-done.1.p1.n1), channel_id=1, source_target_pairs={{0,1},{1,0},{2,3},{3,2},{4,5},{5,4},{6,7},{7,6},{8,9},{9,8},{10,11... | collective-permute-start | bytes 1572872 | tf_op jit(solution)/shard_map/ppermute | solution.py:230
  48.8 6.2 %collective-permute-start.6 = (bf16[64,4096]{1,0:T(8,128)(2,1)S(1)}, bf16[64,4096]{1,0:T(8,128)(2,1)}, u32[]{:S(2)}, u32[]{:S(2)}) collective-permute-start(bf16[64,4096]{1,0:T(8,128)(2,1)S(1)} %collective-permute-done.5.p3.n3), channel_id=1, source_target_pairs={{0,1},{1,0},{2,3},{3,2},{4,5},{5,4},{6,7},{7,6},{8,9},{9,8},{10,11... | collective-permute-start | bytes 1572872 | tf_op jit(solution)/shard_map/ppermute | solution.py:230
  50.9 1.6 %copy-start.1 = (bf16[4096,256]{1,0:T(8,128)(2,1)S(1)}, bf16[4096,256]{1,0:T(8,128)(2,1)}, u32[]{:S(2)}) copy-start(bf16[4096,256]{1,0:T(8,128)(2,1)} %t_ref.3) | copy-start | bytes 6291460
  52.5 2.6 %copy-start.3 = (f32[512,256]{1,0:T(8,128)S(1)}, f32[512,256]{1,0:T(8,128)}, u32[]{:S(2)}) copy-start(f32[512,256]{1,0:T(8,128)} %copy-done.2) | copy-start | bytes 1572868
  52.5 2.6 %copy-start.5 = (f32[512,256]{1,0:T(8,128)S(1)}, f32[512,256]{1,0:T(8,128)}, u32[]{:S(2)}) copy-start(f32[512,256]{1,0:T(8,128)} %copy-done.4) | copy-start | bytes 1572868
  79.3 41.4 %collective-permute-start.7 = (bf16[8,256,128]{2,1,0:T(8,128)(2,1)S(1)}, bf16[8,256,128]{2,1,0:T(8,128)(2,1)S(1)}, u32[]{:S(2)}, u32[]{:S(2)}) collective-permute-start(bf16[8,256,128]{2,1,0:T(8,128)(2,1)S(1)} %get-tuple-element.29), channel_id=1, source_target_pairs={{0,128},{32,160},{64,192},{96,224},{128,0},{160,32},{192,64},{224,... | collective-permute-start | bytes 1572872 | tf_op jit(solution)/shard_map/ppermute | solution.py:233
  84.1 36.6 %collective-permute-start.8 = (bf16[8,256,128]{2,1,0:T(8,128)(2,1)S(1)}, bf16[8,256,128]{2,1,0:T(8,128)(2,1)S(1)}, u32[]{:S(2)}, u32[]{:S(2)}) collective-permute-start(bf16[8,256,128]{2,1,0:T(8,128)(2,1)S(1)} %get-tuple-element.30), channel_id=1, source_target_pairs={{0,896},{32,928},{64,960},{96,992},{128,256},{160,288},{192,320},{... | collective-permute-start | bytes 1572872 | tf_op jit(solution)/shard_map/ppermute | solution.py:233
  99.0 16.9 %collective-permute-start.9 = (bf16[4,256,128]{2,1,0:T(8,128)(2,1)S(1)}, bf16[4,256,128]{2,1,0:T(8,128)(2,1)S(1)}, u32[]{:S(2)}, u32[]{:S(2)}) collective-permute-start(bf16[4,256,128]{2,1,0:T(8,128)(2,1)S(1)} %get-tuple-element.31), channel_id=1, source_target_pairs={{0,32},{32,0},{64,96},{96,64},{128,160},{160,128},{192,224},{224,1... | collective-permute-start | bytes 786440 | tf_op jit(solution)/shard_map/ppermute | solution.py:233
  103.8 16.9 %collective-permute-start.10 = (bf16[4,256,128]{2,1,0:T(8,128)(2,1)S(1)}, bf16[4,256,128]{2,1,0:T(8,128)(2,1)S(1)}, u32[]{:S(2)}, u32[]{:S(2)}) collective-permute-start(bf16[4,256,128]{2,1,0:T(8,128)(2,1)S(1)} %get-tuple-element.32), channel_id=1, source_target_pairs={{0,96},{32,64},{64,32},{96,0},{128,224},{160,192},{192,160},{224,1... | collective-permute-start | bytes 786440 | tf_op jit(solution)/shard_map/ppermute | solution.py:233

commit v3 on v2

--- a/solution.py
+++ b/solution.py
@@ -82,16 +82,13 @@
         res_out[there, :] = res_ref[here, :].astype(jnp.float32)
 
 
-def products(pieces, w_ref, t_ref):
+def product(pieces, w_ref):
     a = jnp.concatenate([piece[...] for piece in pieces], axis=0)
-    return (
-        jnp.dot(a, w_ref[...], preferred_element_type=jnp.float32),
-        jnp.dot(a, t_ref[...], preferred_element_type=jnp.float32),
-    )
-
-
-def near_kernel(p0, p1, p2, p3, w_ref, t_ref, s_ref, m_ref):
-    s_ref[...], m_ref[...] = products((p0, p1, p2, p3), w_ref, t_ref)
+    return jnp.dot(a, w_ref[...], preferred_element_type=jnp.float32)
+
+
+def near_kernel(p0, p1, p2, p3, w_ref, s_ref):
+    s_ref[...] = product((p0, p1, p2, p3), w_ref)
 
 
 def far_kernel(
@@ -100,7 +97,8 @@
 ):
     me = me_ref[0]
     core = me % NC
-    s, m = products((p0, p1, p2, p3), w_ref, t_ref)
+    pieces = (p0, p1, p2, p3)
+    s, m = product(pieces, w_ref), product(pieces, t_ref)
     for i, color in enumerate(piece_colors(me)):
         here = slice(i * PIECE, (i + 1) * PIECE)
         near = piece_rows(core * HALF, color)
@@ -132,8 +130,14 @@
 def second_kernel(
     ids_ref, stats_ref, stream_ref, moved_ref, weighted_ref,
     n0, n1, n2, n3, f0, f1, f2, f3,
-    own_ref, even_ref, odd_ref, first_ref, later_ref, curv_ref,
+    own_ref, even_ref, odd_ref, first_ref, later_ref, curv_ref, a_ref, sems,
 ):
+    copies = [
+        pltpu.make_async_copy(piece, a_ref.at[pl.ds(i * PIECE, PIECE)], sems.at[i])
+        for i, piece in enumerate((n0, n1, n2, n3, f0, f1, f2, f3))
+    ]
+    for copy in copies:
+        copy.start()
     total = jnp.sum(stats_ref[...], axis=0)
     coefs = []
     for h in range(2):
@@ -165,10 +169,11 @@
         axis=0,
     )
     curv_t = curv.T.astype(jnp.bfloat16)
-    pieces = (n0, n1, n2, n3, f0, f1, f2, f3)
+    for copy in copies:
+        copy.wait()
     color = ids_ref[1]
     to_even = 1 + 2 * (color % 2)
-    for what, step in (("even", to_even), ("odd", 4 - to_even), ("side", 2), ("own", 0)):
+    for what, step in (("side", 2), ("even", to_even), ("odd", 4 - to_even), ("own", 0)):
         q = (color + step) % 4
         for pair in range(4):
             z = 2 * pair + q % 2
@@ -176,7 +181,7 @@
             columns = []
             for k in range(2):
                 at = pl.ds(pl.multiple_of((z * NH + h + 2 * k) * 128, 128), 128)
-                columns.append(jnp.concatenate([p[:, at] for p in pieces], axis=0))
+                columns.append(a_ref[:, at])
             out = jnp.dot(
                 curv_t,
                 jnp.concatenate(columns, axis=1),
@@ -253,18 +258,21 @@
         compiler_params=PARAMS,
         name="prep",
     )(seq_len, own, residual, cotangent, gain)
-    near[3], res = lax.optimization_barrier((near[3], res))
-
-    far = [in_group(piece, lambda x, y, c: (x, y, c + 1)) for piece in near]
-
-    near_s, near_m = pl.pallas_call(
-        near_kernel,
-        out_shape=(shape(HALF, columns), shape(HALF, columns)),
-        in_specs=[VMEM] * 6,
-        out_specs=(VMEM,) * 2,
-        compiler_params=PARAMS,
-        name="near",
-    )(*near, out_weight, tangent)
+    ready, res = lax.optimization_barrier((own, res))
+
+    far = [in_group(piece, lambda x, y, c: (x, y, c + 1)) for piece in [ready] + near[1:]]
+
+    near_s, near_m = (
+        pl.pallas_call(
+            near_kernel,
+            out_shape=shape(HALF, columns),
+            in_specs=[VMEM] * 5,
+            out_specs=VMEM,
+            compiler_params=PARAMS,
+            name=name,
+        )(*near, w)
+        for name, w in (("near_s", out_weight), ("near_m", tangent))
+    )
 
     stream, moved, stats = pl.pallas_call(
         far_kernel,
@@ -282,17 +290,21 @@
     mine, even, odd, first, later = pl.pallas_call(
         second_kernel,
         out_shape=(whole, whole, whole, part, part),
-        in_specs=[SMEM] + [VMEM] * 12,
+        in_specs=[SMEM] + [VMEM] * 4 + [ANY] * 8,
         out_specs=(VMEM,) * 5,
-        scratch_shapes=[pltpu.VMEM((rows, columns), f32)],
+        scratch_shapes=[
+            pltpu.VMEM((rows, columns), f32),
+            pltpu.VMEM((rows, features), bf16),
+            pltpu.SemaphoreType.DMA((8,)),
+        ],
         compiler_params=PARAMS,
         name="second",
     )(ids, stats, stream, moved, weighted, *near, *far)
 
+    first = of_groups(first, lambda z, h: (z, even_partner(h)))
+    later = of_groups(later, lambda z, h: (z, odd_partner(h)))
     even = of_groups(even, lambda z, h: (even_partner(z), h))
     odd = of_groups(odd, lambda z, h: (odd_partner(z), h))
-    first = of_groups(first, lambda z, h: (z, even_partner(h)))
-    later = of_groups(later, lambda z, h: (z, odd_partner(h)))
     four = pl.pallas_call(
         third_kernel,
         out_shape=whole,

time: 148 us -> 146 us (0.986)
  the two profiles are of different devices: /device:TPU:1 before, /device:TPU:2 now
where the time goes in v3:
time: 146 us; the launch traced here: 145 us
  blocking collectives  68 us (47%)
  starting transfers between devices  48.7 us (33%)
  Pallas kernels  12.8 us (9%)
  waiting for transfers between devices  9.64 us (7%)
  local copies, waits for them, and re-layouts  5.23 us (4%)
    ppermute x4, starting transfers between devices, of_groups(): return lax.ppermute(x, 'rep', rep_perm(step))  29.9 us
    all_to_all x1, blocking collectives, local(): parts = lax.all_to_all(four, 'rep', 0, 0, axis_index_groups=CLASSES)  27.5 us
    all_to_all x1, blocking collectives, local(): lax.all_to_all(jnp.broadcast_to(attn_out[None], (4, SHARD, features)), 'f...  22.1 us
    ppermute x7, starting transfers between devices, in_group(): return lax.ppermute(x, 'fsdp', fsdp_perm(step))  18.9 us
    all_to_all x1, blocking collectives, local(): stats = lax.all_to_all(stats, 'fsdp', 0, 0)  18.4 us
    ppermute x4, waiting for transfers between devices, of_groups(): return lax.ppermute(x, 'rep', rep_perm(step))  9.32 us
    pallas_call x1, Pallas kernels, local(): pl.pallas_call(second_kernel, out_shape=(whole, whole, whole, part, part)...  4.24 us
    pallas_call x2, Pallas kernels, local(): pl.pallas_call(near_kernel, out_shape=shape(HALF, columns), in_specs=[VME...  4.07 us
  transfers between devices with their start and end apart: 11, of which 3 were waited for; matrix products, arithmetic and copies ran while one was open for 1% of the time, Pallas kernels for 3%

profile of v3, /device:TPU:2, one launch (start us, length us, event | category | flops | bytes accessed | tf_op | source)
XLA Modules:
  0.0 145.4 jit_solution(1856157606859599410)
XLA Ops:
  0.0 0.0 copy-start.1
  0.0 1.1 broadcast_in_dim.4
  1.1 22.1 %all_to_all.15 = bf16[4,16,4096]{2,1,0:T(8,128)(2,1)S(1)} all-to-all(bf16[4,16,4096]{2,1,0:T(8,128)(2,1)S(1)} %broadcast_in_dim.4), channel_id=1, replica_groups={{0,8,20,28},{1,9,21,29},{2,10,22,30},{3,11,23,31},{4,12,16,24},{5,13,17..., dimensions={0} | all-to-all | bytes 1048576 | tf_op jit(solution)/shard_map/all_to_all | solution.py:243
  23.2 5.6 %collective-permute-start.5 = (bf16[64,4096]{1,0:T(8,128)(2,1)S(1)}, bf16[64,4096]{1,0:T(8,128)(2,1)S(1)}, u32[]{:S(2)}, u32[]{:S(2)}) collective-permute-start(bf16[64,4096]{1,0:T(8,128)(2,1)S(1)} %bitcast.3), channel_id=1, source_target_pairs={{0,16},{1,17},{2,18},{3,19},{4,20},{5,21},{6,22},{7,23},{8,24},{9,... | collective-permute-start | bytes 1572872 | tf_op jit(solution)/shard_map/ppermute | solution.py:235
  28.8 1.9 %collective-permute-start.3 = (bf16[64,4096]{1,0:T(8,128)(2,1)S(1)}, bf16[64,4096]{1,0:T(8,128)(2,1)}, u32[]{:S(2)}, u32[]{:S(2)}) collective-permute-start(bf16[64,4096]{1,0:T(8,128)(2,1)S(1)} %bitcast.4), channel_id=1, source_target_pairs={{0,14},{1,15},{2,4},{3,5},{4,2},{5,3},{6,8},{7,9},{8,6},{9,7},{10,... | collective-permute-start | bytes 1572872 | tf_op jit(solution)/shard_map/ppermute | solution.py:235
  30.7 2.7 %collective-permute-start.1 = (bf16[64,4096]{1,0:T(8,128)(2,1)S(1)}, bf16[64,4096]{1,0:T(8,128)(2,1)}, u32[]{:S(2)}, u32[]{:S(2)}) collective-permute-start(bf16[64,4096]{1,0:T(8,128)(2,1)S(1)} %bitcast.5), channel_id=1, source_target_pairs={{0,2},{1,3},{2,0},{3,1},{4,6},{5,7},{6,4},{7,5},{8,10},{9,11},{10,... | collective-permute-start | bytes 1572872 | tf_op jit(solution)/shard_map/ppermute | solution.py:235
  34.0 0.7 broadcast_in_dim.10.gain_ref
  34.7 0.0 copy-start.6
  34.7 0.9 copy-done.6
  35.7 0.0 copy-start.7
  35.7 0.9 copy-done.7
  36.6 0.1 prep.1
  36.7 0.0 copy-start.2
  36.7 0.8 copy-done.2
  37.5 0.0 copy-start.4
  37.5 0.8 copy-done.4
  38.3 1.9 %collective-permute-start = (bf16[64,4096]{1,0:T(8,128)(2,1)S(1)}, bf16[64,4096]{1,0:T(8,128)(2,1)}, u32[]{:S(2)}, u32[]{:S(2)}) collective-permute-start(bf16[64,4096]{1,0:T(8,128)(2,1)S(1)} %bitcast.7), channel_id=1, source_target_pairs={{0,1},{1,0},{2,3},{3,2},{4,5},{5,4},{6,7},{7,6},{8,9},{9,8},{10,11... | collective-permute-start | bytes 1572872 | tf_op jit(solution)/shard_map/ppermute | solution.py:235
  40.2 0.0 collective-permute-done.5.p3.n3
  40.2 2.4 %collective-permute-start.6 = (bf16[64,4096]{1,0:T(8,128)(2,1)S(1)}, bf16[64,4096]{1,0:T(8,128)(2,1)}, u32[]{:S(2)}, u32[]{:S(2)}) collective-permute-start(bf16[64,4096]{1,0:T(8,128)(2,1)S(1)} %collective-permute-done.5.p3.n3), channel_id=1, source_target_pairs={{0,1},{1,0},{2,3},{3,2},{4,5},{5,4},{6,7},{7,6},{8,9},{9,8},{10,11... | collective-permute-start | bytes 1572872 | tf_op jit(solution)/shard_map/ppermute | solution.py:235
  42.6 0.3 collective-permute-done.3.p2.n2
  42.9 1.9 %collective-permute-start.4 = (bf16[64,4096]{1,0:T(8,128)(2,1)}, bf16[64,4096]{1,0:T(8,128)(2,1)}, u32[]{:S(2)}, u32[]{:S(2)}) collective-permute-start(bf16[64,4096]{1,0:T(8,128)(2,1)} %collective-permute-done.3.p2.n2), channel_id=1, source_target_pairs={{0,1},{1,0},{2,3},{3,2},{4,5},{5,4},{6,7},{7,6},{8,9},{9,8},{10,11... | collective-permute-start | bytes 1572872 | tf_op jit(solution)/shard_map/ppermute | solution.py:235
  44.8 0.0 collective-permute-done.1.p1.n1
  44.9 2.4 %collective-permute-start.2 = (bf16[64,4096]{1,0:T(8,128)(2,1)}, bf16[64,4096]{1,0:T(8,128)(2,1)}, u32[]{:S(2)}, u32[]{:S(2)}) collective-permute-start(bf16[64,4096]{1,0:T(8,128)(2,1)} %collective-permute-done.1.p1.n1), channel_id=1, source_target_pairs={{0,1},{1,0},{2,3},{3,2},{4,5},{5,4},{6,7},{7,6},{8,9},{9,8},{10,11... | collective-permute-start | bytes 1572872 | tf_op jit(solution)/shard_map/ppermute | solution.py:235
  47.3 0.1 pad_add_fusion.me_ref.ids_ref
  47.4 0.0 copy-done.1
  47.4 0.0 copy-start
  47.4 2.1 %near_m.1.near_m_ref = f32[256,256]{1,0:T(8,128)S(1)} custom-call(bf16[64,4096]{1,0:T(8,128)(2,1)S(1)} %bitcast.8, bf16[64,4096]{1,0:T(8,128)(2,1)} %collective-permute-done.1.p1.n1, bf16[64,4096]{1,0:T(8,128)(2,1)} %collective-permute-done.3.p2.n2, bf16[64,4096]{1,0:T(8,128)(2,1)S(1)} %collective-permute-done.5.p3.n3, bf16[4096,256]{1,0:T(8,128)(2,1)S(1)} %copy-done.1), custom_call_target="tpu_custom_call" | custom-call | tf_op jit(solution)/shard_map/near_m/pallas_call | solution.py:266
  49.5 0.0 copy-done
  49.5 0.0 copy-start.3
  49.5 0.0 copy-start.5
  49.5 2.0 %near_s.1.near_s_ref = f32[256,256]{1,0:T(8,128)S(1)} custom-call(bf16[64,4096]{1,0:T(8,128)(2,1)S(1)} %bitcast.9, bf16[64,4096]{1,0:T(8,128)(2,1)} %collective-permute-done.1.p1.n1, bf16[64,4096]{1,0:T(8,128)(2,1)} %collective-permute-done.3.p2.n2, bf16[64,4096]{1,0:T(8,128)(2,1)S(1)} %collective-permute-done.5.p3.n3, bf16[4096,256]{1,0:T(8,128)(2,1)S(1)} %copy-done), custom_call_target="tpu_custom_call" | custom-call | tf_op jit(solution)/shard_map/near_s/pallas_call | solution.py:266
  51.5 0.0 collective-permute-done.p0.f0
  51.5 0.0 collective-permute-done.6.p3.f3
  51.5 0.0 collective-permute-done.4.p2.f2
  51.5 0.0 collective-permute-done.2.p1.f1
  51.6 0.0 copy-done.3
  51.6 0.0 copy-done.5
  51.6 3.3 %far.1 = (f32[512,256]{1,0:T(8,128)S(1)}, f32[512,256]{1,0:T(8,128)S(1)}, f32[32,8,256]{2,1,0:T(8,128)S(1)}) custom-call(s32[2]{0:T(128)S(1)} %pad_add_fusion.me_ref.ids_ref, bf16[64,4096]{1,0:T(8,128)(2,1)} %collective-permute-done.p0.f0, bf16[64,4096]{1,0:T(8,128)(2,1)} %collective-permute-done.2.p1.f1, bf16[64,4096]{1,0:T(8,128)(2,1)} %collective-permute-done.4.p2.f2, ...), custom_call_target="tpu_custom_call" | custom-call | tf_op jit(solution)/shard_map/far/pallas_call | solution.py:277
  54.9 18.4 %all_to_all.16.stats_ref = f32[32,8,256]{2,1,0:T(8,128)S(1)} all-to-all(f32[32,8,256]{2,1,0:T(8,128)S(1)} %get-tuple-element.21), channel_id=1, replica_groups=mesh['rep'=32,'fsdp'=32] {'fsdp'}, dimensions={0} | all-to-all | bytes 524288 | tf_op jit(solution)/shard_map/all_to_all | solution.py:286
  73.3 4.2 %second.1 = (bf16[8,256,128]{2,1,0:T(8,128)(2,1)S(1)}, bf16[8,256,128]{2,1,0:T(8,128)(2,1)S(1)}, bf16[8,256,128]{2,1,0:T(8,128)(2,1)S(1)}, bf16[4,256,128]{2,1,0:T(8,128)(2,1)S(1)}, bf16[4,256,128]{2,1,0:T(8,128)(2,1)S(1)}) custom-call(s32[2]{0:T(128)S(1)} %pad_add_fusion.me_ref.ids_ref, f32[32,8,256]{2,1,0:T(8,128)S(1)} %all_to_all.16.stats_ref, ...), custom_call_target="tpu_custom_call" | custom-call | tf_op jit(solution)/shard_map/second/pallas_call | solution.py:290
  77.6 4.0 %collective-permute-start.7 = (bf16[8,256,128]{2,1,0:T(8,128)(2,1)S(1)}, bf16[8,256,128]{2,1,0:T(8,128)(2,1)S(1)}, u32[]{:S(2)}, u32[]{:S(2)}) collective-permute-start(bf16[8,256,128]{2,1,0:T(8,128)(2,1)S(1)} %get-tuple-element.25), channel_id=1, source_target_pairs={{0,128},{32,160},{64,192},{96,224},{128,0},{160,32},{192,64},{224,... | collective-permute-start | bytes 1572872 | tf_op jit(solution)/shard_map/ppermute | solution.py:238
  81.5 14.9 %collective-permute-start.8 = (bf16[8,256,128]{2,1,0:T(8,128)(2,1)S(1)}, bf16[8,256,128]{2,1,0:T(8,128)(2,1)S(1)}, u32[]{:S(2)}, u32[]{:S(2)}) collective-permute-start(bf16[8,256,128]{2,1,0:T(8,128)(2,1)S(1)} %get-tuple-element.26), channel_id=1, source_target_pairs={{0,896},{32,928},{64,960},{96,992},{128,256},{160,288},{192,320},{... | collective-permute-start | bytes 1572872 | tf_op jit(solution)/shard_map/ppermute | solution.py:238
  96.4 5.9 %collective-permute-start.9 = (bf16[4,256,128]{2,1,0:T(8,128)(2,1)S(1)}, bf16[4,256,128]{2,1,0:T(8,128)(2,1)S(1)}, u32[]{:S(2)}, u32[]{:S(2)}) collective-permute-start(bf16[4,256,128]{2,1,0:T(8,128)(2,1)S(1)} %get-tuple-element.27), channel_id=1, source_target_pairs={{0,32},{32,0},{64,96},{96,64},{128,160},{160,128},{192,224},{224,1... | collective-permute-start | bytes 786440 | tf_op jit(solution)/shard_map/ppermute | solution.py:238
  102.4 5.1 %collective-permute-start.10 = (bf16[4,256,128]{2,1,0:T(8,128)(2,1)S(1)}, bf16[4,256,128]{2,1,0:T(8,128)(2,1)S(1)}, u32[]{:S(2)}, u32[]{:S(2)}) collective-permute-start(bf16[4,256,128]{2,1,0:T(8,128)(2,1)S(1)} %get-tuple-element.28), channel_id=1, source_target_pairs={{0,96},{32,64},{64,32},{96,0},{128,224},{160,192},{192,160},{224,1... | collective-permute-start | bytes 786440 | tf_op jit(solution)/shard_map/ppermute | solution.py:238
  107.5 5.4 %collective-permute-done.9.first_ref = bf16[4,256,128]{2,1,0:T(8,128)(2,1)S(1)} collective-permute-done((bf16[4,256,128]{2,1,0:T(8,128)(2,1)S(1)}, bf16[4,256,128]{2,1,0:T(8,128)(2,1)S(1)}, u32[]{:S(2)}, u32[]{:S(2)}) %collective-permute-start.9) | collective-permute-done | bytes 262176 | tf_op jit(solution)/shard_map/ppermute | solution.py:238
  112.8 4.0 %collective-permute-done.10.later_ref = bf16[4,256,128]{2,1,0:T(8,128)(2,1)S(1)} collective-permute-done((bf16[4,256,128]{2,1,0:T(8,128)(2,1)S(1)}, bf16[4,256,128]{2,1,0:T(8,128)(2,1)S(1)}, u32[]{:S(2)}, u32[]{:S(2)}) %collective-permute-start.10) | collective-permute-done | bytes 262176 | tf_op jit(solution)/shard_map/ppermute | solution.py:238
  116.8 0.0 collective-permute-done.7.even_ref
  116.8 0.0 collective-permute-done.8.odd_ref
  116.8 0.3 third.1
  117.1 27.5 %all_to_all.17.parts_ref = bf16[8,256,128]{2,1,0:T(8,128)(2,1)S(1)} all-to-all(bf16[8,256,128]{2,1,0:T(8,128)(2,1)S(1)} %third.1), channel_id=1, replica_groups={{0,64,288,352,512,576,800,864},{128,192,416,480,640,704,928,992},{32,96..., dimensions={0} | all-to-all | bytes 1048576 | tf_op jit(solution)/shard_map/all_to_all | solution.py:316
  144.6 0.8 last.1
Async XLA Ops:
  0.0 47.4 %copy-start.1 = (bf16[4096,256]{1,0:T(8,128)(2,1)S(1)}, bf16[4096,256]{1,0:T(8,128)(2,1)}, u32[]{:S(2)}) copy-start(bf16[4096,256]{1,0:T(8,128)(2,1)} %t_ref.1) | copy-start | bytes 6291460
  23.2 17.0 %collective-permute-start.5 = (bf16[64,4096]{1,0:T(8,128)(2,1)S(1)}, bf16[64,4096]{1,0:T(8,128)(2,1)S(1)}, u32[]{:S(2)}, u32[]{:S(2)}) collective-permute-start(bf16[64,4096]{1,0:T(8,128)(2,1)S(1)} %bitcast.3), channel_id=1, source_target_pairs={{0,16},{1,17},{2,18},{3,19},{4,20},{5,21},{6,22},{7,23},{8,24},{9,... | collective-permute-start | bytes 1572872 | tf_op jit(solution)/shard_map/ppermute | solution.py:235
  28.8 14.1 %collective-permute-start.3 = (bf16[64,4096]{1,0:T(8,128)(2,1)S(1)}, bf16[64,4096]{1,0:T(8,128)(2,1)}, u32[]{:S(2)}, u32[]{:S(2)}) collective-permute-start(bf16[64,4096]{1,0:T(8,128)(2,1)S(1)} %bitcast.4), channel_id=1, source_target_pairs={{0,14},{1,15},{2,4},{3,5},{4,2},{5,3},{6,8},{7,9},{8,6},{9,7},{10,... | collective-permute-start | bytes 1572872 | tf_op jit(solution)/shard_map/ppermute | solution.py:235
  30.7 14.1 %collective-permute-start.1 = (bf16[64,4096]{1,0:T(8,128)(2,1)S(1)}, bf16[64,4096]{1,0:T(8,128)(2,1)}, u32[]{:S(2)}, u32[]{:S(2)}) collective-permute-start(bf16[64,4096]{1,0:T(8,128)(2,1)S(1)} %bitcast.5), channel_id=1, source_target_pairs={{0,2},{1,3},{2,0},{3,1},{4,6},{5,7},{6,4},{7,5},{8,10},{9,11},{10,... | collective-permute-start | bytes 1572872 | tf_op jit(solution)/shard_map/ppermute | solution.py:235
  34.7 0.9 copy-start.6
  35.7 0.9 copy-start.7
  36.7 0.8 copy-start.2
  37.5 0.8 copy-start.4
  38.3 13.2 %collective-permute-start = (bf16[64,4096]{1,0:T(8,128)(2,1)S(1)}, bf16[64,4096]{1,0:T(8,128)(2,1)}, u32[]{:S(2)}, u32[]{:S(2)}) collective-permute-start(bf16[64,4096]{1,0:T(8,128)(2,1)S(1)} %bitcast.7), channel_id=1, source_target_pairs={{0,1},{1,0},{2,3},{3,2},{4,5},{5,4},{6,7},{7,6},{8,9},{9,8},{10,11... | collective-permute-start | bytes 1572872 | tf_op jit(solution)/shard_map/ppermute | solution.py:235
  40.2 11.3 %collective-permute-start.6 = (bf16[64,4096]{1,0:T(8,128)(2,1)S(1)}, bf16[64,4096]{1,0:T(8,128)(2,1)}, u32[]{:S(2)}, u32[]{:S(2)}) collective-permute-start(bf16[64,4096]{1,0:T(8,128)(2,1)S(1)} %collective-permute-done.5.p3.n3), channel_id=1, source_target_pairs={{0,1},{1,0},{2,3},{3,2},{4,5},{5,4},{6,7},{7,6},{8,9},{9,8},{10,11... | collective-permute-start | bytes 1572872 | tf_op jit(solution)/shard_map/ppermute | solution.py:235
  42.9 8.6 %collective-permute-start.4 = (bf16[64,4096]{1,0:T(8,128)(2,1)}, bf16[64,4096]{1,0:T(8,128)(2,1)}, u32[]{:S(2)}, u32[]{:S(2)}) collective-permute-start(bf16[64,4096]{1,0:T(8,128)(2,1)} %collective-permute-done.3.p2.n2), channel_id=1, source_target_pairs={{0,1},{1,0},{2,3},{3,2},{4,5},{5,4},{6,7},{7,6},{8,9},{9,8},{10,11... | collective-permute-start | bytes 1572872 | tf_op jit(solution)/shard_map/ppermute | solution.py:235
  44.9 6.7 %collective-permute-start.2 = (bf16[64,4096]{1,0:T(8,128)(2,1)}, bf16[64,4096]{1,0:T(8,128)(2,1)}, u32[]{:S(2)}, u32[]{:S(2)}) collective-permute-start(bf16[64,4096]{1,0:T(8,128)(2,1)} %collective-permute-done.1.p1.n1), channel_id=1, source_target_pairs={{0,1},{1,0},{2,3},{3,2},{4,5},{5,4},{6,7},{7,6},{8,9},{9,8},{10,11... | collective-permute-start | bytes 1572872 | tf_op jit(solution)/shard_map/ppermute | solution.py:235
  47.4 2.1 %copy-start = (bf16[4096,256]{1,0:T(8,128)(2,1)S(1)}, bf16[4096,256]{1,0:T(8,128)(2,1)}, u32[]{:S(2)}) copy-start(bf16[4096,256]{1,0:T(8,128)(2,1)} %w_ref.5) | copy-start | bytes 6291460
  49.5 2.1 %copy-start.3 = (f32[512,256]{1,0:T(8,128)S(1)}, f32[512,256]{1,0:T(8,128)}, u32[]{:S(2)}) copy-start(f32[512,256]{1,0:T(8,128)} %copy-done.2) | copy-start | bytes 1572868
  49.5 2.1 %copy-start.5 = (f32[512,256]{1,0:T(8,128)S(1)}, f32[512,256]{1,0:T(8,128)}, u32[]{:S(2)}) copy-start(f32[512,256]{1,0:T(8,128)} %copy-done.4) | copy-start | bytes 1572868
  77.6 39.2 %collective-permute-start.7 = (bf16[8,256,128]{2,1,0:T(8,128)(2,1)S(1)}, bf16[8,256,128]{2,1,0:T(8,128)(2,1)S(1)}, u32[]{:S(2)}, u32[]{:S(2)}) collective-permute-start(bf16[8,256,128]{2,1,0:T(8,128)(2,1)S(1)} %get-tuple-element.25), channel_id=1, source_target_pairs={{0,128},{32,160},{64,192},{96,224},{128,0},{160,32},{192,64},{224,... | collective-permute-start | bytes 1572872 | tf_op jit(solution)/shard_map/ppermute | solution.py:238
  81.5 35.3 %collective-permute-start.8 = (bf16[8,256,128]{2,1,0:T(8,128)(2,1)S(1)}, bf16[8,256,128]{2,1,0:T(8,128)(2,1)S(1)}, u32[]{:S(2)}, u32[]{:S(2)}) collective-permute-start(bf16[8,256,128]{2,1,0:T(8,128)(2,1)S(1)} %get-tuple-element.26), channel_id=1, source_target_pairs={{0,896},{32,928},{64,960},{96,992},{128,256},{160,288},{192,320},{... | collective-permute-start | bytes 1572872 | tf_op jit(solution)/shard_map/ppermute | solution.py:238
  96.4 16.4 %collective-permute-start.9 = (bf16[4,256,128]{2,1,0:T(8,128)(2,1)S(1)}, bf16[4,256,128]{2,1,0:T(8,128)(2,1)S(1)}, u32[]{:S(2)}, u32[]{:S(2)}) collective-permute-start(bf16[4,256,128]{2,1,0:T(8,128)(2,1)S(1)} %get-tuple-element.27), channel_id=1, source_target_pairs={{0,32},{32,0},{64,96},{96,64},{128,160},{160,128},{192,224},{224,1... | collective-permute-start | bytes 786440 | tf_op jit(solution)/shard_map/ppermute | solution.py:238
  102.4 14.4 %collective-permute-start.10 = (bf16[4,256,128]{2,1,0:T(8,128)(2,1)S(1)}, bf16[4,256,128]{2,1,0:T(8,128)(2,1)S(1)}, u32[]{:S(2)}, u32[]{:S(2)}) collective-permute-start(bf16[4,256,128]{2,1,0:T(8,128)(2,1)S(1)} %get-tuple-element.28), channel_id=1, source_target_pairs={{0,96},{32,64},{64,32},{96,0},{128,224},{160,192},{192,160},{224,1... | collective-permute-start | bytes 786440 | tf_op jit(solution)/shard_map/ppermute | solution.py:238

commit v4 on v3

--- a/solution.py
+++ b/solution.py
@@ -45,6 +45,17 @@
 
 def odd_partner(i):
     return ((i + 1) ^ 1) - 1
+
+
+def side_perm():
+    moves = []
+    for z in range(NZ):
+        for h in range(NH):
+            for f in range(NX * NY * NC):
+                there = odd_partner(h) if f % NC else even_partner(h)
+                width = NX * NY * NC
+                moves.append((rep_of(z, h) * width + f, rep_of(z, there) * width + f))
+    return moves
 
 
 def chip_of(q, j):
@@ -130,7 +141,7 @@
 def second_kernel(
     ids_ref, stats_ref, stream_ref, moved_ref, weighted_ref,
     n0, n1, n2, n3, f0, f1, f2, f3,
-    own_ref, even_ref, odd_ref, first_ref, later_ref, curv_ref, a_ref, sems,
+    own_ref, side_ref, even_ref, odd_ref, curv_ref, a_ref, sems,
 ):
     copies = [
         pltpu.make_async_copy(piece, a_ref.at[pl.ds(i * PIECE, PIECE)], sems.at[i])
@@ -173,7 +184,9 @@
         copy.wait()
     color = ids_ref[1]
     to_even = 1 + 2 * (color % 2)
-    for what, step in (("side", 2), ("even", to_even), ("odd", 4 - to_even), ("own", 0)):
+    for out_ref, step in (
+        (side_ref, 2), (even_ref, to_even), (odd_ref, 4 - to_even), (own_ref, 0)
+    ):
         q = (color + step) % 4
         for pair in range(4):
             z = 2 * pair + q % 2
@@ -187,30 +200,18 @@
                 jnp.concatenate(columns, axis=1),
                 preferred_element_type=jnp.float32,
             ).astype(jnp.bfloat16)
-            for k in range(2):
-                i = 2 * pair + k
-                value = out[:, 128 * k : 128 * k + 128]
-                if what == "own":
-                    own_ref[i] = value
-                elif what == "even":
-                    even_ref[i] = value
-                elif what == "odd":
-                    odd_ref[i] = value
-                elif i < 4:
-                    first_ref[i] = value
-                else:
-                    later_ref[i - 4] = value
-
-
-def third_kernel(own_ref, even_ref, odd_ref, first_ref, later_ref, out_ref):
+            out_ref[2 * pair] = out[:, :128]
+            out_ref[2 * pair + 1] = out[:, 128:]
+
+
+def third_kernel(side_ref, own_ref, even_ref, odd_ref, out_ref):
     f32 = jnp.float32
-    for i in range(8):
-        side = first_ref[i] if i < 4 else later_ref[i - 4]
+    for i in range(own_ref.shape[0]):
         out_ref[i] = (
             own_ref[i].astype(f32)
             + even_ref[i].astype(f32)
             + odd_ref[i].astype(f32)
-            + side.astype(f32)
+            + side_ref[i].astype(f32)
         ).astype(out_ref.dtype)
 
 
@@ -286,12 +287,11 @@
     stats = lax.all_to_all(stats, "fsdp", 0, 0)
 
     whole = shape(8, columns, 128, dtype=bf16)
-    part = shape(4, columns, 128, dtype=bf16)
-    mine, even, odd, first, later = pl.pallas_call(
+    mine, side, even, odd = pl.pallas_call(
         second_kernel,
-        out_shape=(whole, whole, whole, part, part),
+        out_shape=(whole,) * 4,
         in_specs=[SMEM] + [VMEM] * 4 + [ANY] * 8,
-        out_specs=(VMEM,) * 5,
+        out_specs=(VMEM,) * 4,
         scratch_shapes=[
             pltpu.VMEM((rows, columns), f32),
             pltpu.VMEM((rows, features), bf16),
@@ -301,18 +301,17 @@
         name="second",
     )(ids, stats, stream, moved, weighted, *near, *far)
 
-    first = of_groups(first, lambda z, h: (z, even_partner(h)))
-    later = of_groups(later, lambda z, h: (z, odd_partner(h)))
+    side = lax.ppermute(side, ("rep", "fsdp"), side_perm())
     even = of_groups(even, lambda z, h: (even_partner(z), h))
     odd = of_groups(odd, lambda z, h: (odd_partner(z), h))
     four = pl.pallas_call(
         third_kernel,
         out_shape=whole,
-        in_specs=[VMEM] * 5,
+        in_specs=[VMEM] * 4,
         out_specs=VMEM,
         compiler_params=PARAMS,
         name="third",
-    )(mine, even, odd, first, later)
+    )(side, mine, even, odd)
     parts = lax.all_to_all(four, "rep", 0, 0, axis_index_groups=CLASSES)
     return pl.pallas_call(
         last_kernel,

time: 146 us -> 142 us (0.973)
  the two profiles are of different devices: /device:TPU:2 before, /device:TPU:22 now
where the time goes in v4:
time: 142 us; the launch traced here: 141 us
  blocking collectives  67.8 us (48%)
  starting transfers between devices  41.7 us (29%)
  Pallas kernels  12.8 us (9%)
  waiting for transfers between devices  12.5 us (9%)
  local copies, waits for them, and re-layouts  5.24 us (4%)
    all_to_all x1, blocking collectives, local(): parts = lax.all_to_all(four, 'rep', 0, 0, axis_index_groups=CLASSES)  29.8 us
    all_to_all x1, blocking collectives, local(): lax.all_to_all(jnp.broadcast_to(attn_out[None], (4, SHARD, features)), 'f...  21.5 us
    ppermute x2, starting transfers between devices, of_groups(): return lax.ppermute(x, 'rep', rep_perm(step))  19.9 us
    ppermute x7, starting transfers between devices, in_group(): return lax.ppermute(x, 'fsdp', fsdp_perm(step))  18.1 us
    all_to_all x1, blocking collectives, local(): stats = lax.all_to_all(stats, 'fsdp', 0, 0)  16.5 us
    ppermute x2, waiting for transfers between devices, of_groups(): return lax.ppermute(x, 'rep', rep_perm(step))  10.5 us
    pallas_call x1, Pallas kernels, local(): pl.pallas_call(second_kernel, out_shape=(whole,) * 4, in_specs=[SMEM] + [...  4.24 us
    pallas_call x2, Pallas kernels, local(): pl.pallas_call(near_kernel, out_shape=shape(HALF, columns), in_specs=[VME...  4.07 us
  transfers between devices with their start and end apart: 10, of which 3 were waited for; matrix products, arithmetic and copies ran while one was open for 1% of the time, Pallas kernels for 3%

profile of v4, /device:TPU:22, one launch (start us, length us, event | category | flops | bytes accessed | tf_op | source)
XLA Modules:
  0.0 141.0 jit_solution(18218838860431233996)
XLA Ops:
  0.0 0.0 copy-start.1
  0.0 1.1 broadcast_in_dim.4
  1.1 21.5 %all_to_all.15 = bf16[4,16,4096]{2,1,0:T(8,128)(2,1)S(1)} all-to-all(bf16[4,16,4096]{2,1,0:T(8,128)(2,1)S(1)} %broadcast_in_dim.4), channel_id=1, replica_groups={{0,8,20,28},{1,9,21,29},{2,10,22,30},{3,11,23,31},{4,12,16,24},{5,13,17..., dimensions={0} | all-to-all | bytes 1048576 | tf_op jit(solution)/shard_map/all_to_all | solution.py:244
  22.6 4.9 %collective-permute-start.5 = (bf16[64,4096]{1,0:T(8,128)(2,1)S(1)}, bf16[64,4096]{1,0:T(8,128)(2,1)S(1)}, u32[]{:S(2)}, u32[]{:S(2)}) collective-permute-start(bf16[64,4096]{1,0:T(8,128)(2,1)S(1)} %bitcast.3), channel_id=1, source_target_pairs={{0,16},{1,17},{2,18},{3,19},{4,20},{5,21},{6,22},{7,23},{8,24},{9,... | collective-permute-start | bytes 1572872 | tf_op jit(solution)/shard_map/ppermute | solution.py:236
  27.5 3.2 %collective-permute-start.3 = (bf16[64,4096]{1,0:T(8,128)(2,1)S(1)}, bf16[64,4096]{1,0:T(8,128)(2,1)}, u32[]{:S(2)}, u32[]{:S(2)}) collective-permute-start(bf16[64,4096]{1,0:T(8,128)(2,1)S(1)} %bitcast.4), channel_id=1, source_target_pairs={{0,14},{1,15},{2,4},{3,5},{4,2},{5,3},{6,8},{7,9},{8,6},{9,7},{10,... | collective-permute-start | bytes 1572872 | tf_op jit(solution)/shard_map/ppermute | solution.py:236
  30.6 1.9 %collective-permute-start.1 = (bf16[64,4096]{1,0:T(8,128)(2,1)S(1)}, bf16[64,4096]{1,0:T(8,128)(2,1)}, u32[]{:S(2)}, u32[]{:S(2)}) collective-permute-start(bf16[64,4096]{1,0:T(8,128)(2,1)S(1)} %bitcast.5), channel_id=1, source_target_pairs={{0,2},{1,3},{2,0},{3,1},{4,6},{5,7},{6,4},{7,5},{8,10},{9,11},{10,... | collective-permute-start | bytes 1572872 | tf_op jit(solution)/shard_map/ppermute | solution.py:236
  33.2 0.7 broadcast_in_dim.10.gain_ref
  33.9 0.0 copy-start.6
  33.9 0.9 copy-done.6
  34.8 0.0 copy-start.7
  34.8 0.9 copy-done.7
  35.8 0.1 prep.1
  35.9 0.0 copy-start.2
  35.9 0.8 copy-done.2
  36.7 0.0 copy-start.4
  36.7 0.8 copy-done.4
  37.5 1.9 %collective-permute-start = (bf16[64,4096]{1,0:T(8,128)(2,1)S(1)}, bf16[64,4096]{1,0:T(8,128)(2,1)}, u32[]{:S(2)}, u32[]{:S(2)}) collective-permute-start(bf16[64,4096]{1,0:T(8,128)(2,1)S(1)} %bitcast.7), channel_id=1, source_target_pairs={{0,1},{1,0},{2,3},{3,2},{4,5},{5,4},{6,7},{7,6},{8,9},{9,8},{10,11... | collective-permute-start | bytes 1572872 | tf_op jit(solution)/shard_map/ppermute | solution.py:236
  39.4 0.0 collective-permute-done.5.p3.n3
  39.4 2.4 %collective-permute-start.6 = (bf16[64,4096]{1,0:T(8,128)(2,1)S(1)}, bf16[64,4096]{1,0:T(8,128)(2,1)}, u32[]{:S(2)}, u32[]{:S(2)}) collective-permute-start(bf16[64,4096]{1,0:T(8,128)(2,1)S(1)} %collective-permute-done.5.p3.n3), channel_id=1, source_target_pairs={{0,1},{1,0},{2,3},{3,2},{4,5},{5,4},{6,7},{7,6},{8,9},{9,8},{10,11... | collective-permute-start | bytes 1572872 | tf_op jit(solution)/shard_map/ppermute | solution.py:236
  41.8 0.9 collective-permute-done.3.p2.n2
  42.7 1.9 %collective-permute-start.4 = (bf16[64,4096]{1,0:T(8,128)(2,1)}, bf16[64,4096]{1,0:T(8,128)(2,1)}, u32[]{:S(2)}, u32[]{:S(2)}) collective-permute-start(bf16[64,4096]{1,0:T(8,128)(2,1)} %collective-permute-done.3.p2.n2), channel_id=1, source_target_pairs={{0,1},{1,0},{2,3},{3,2},{4,5},{5,4},{6,7},{7,6},{8,9},{9,8},{10,11... | collective-permute-start | bytes 1572872 | tf_op jit(solution)/shard_map/ppermute | solution.py:236
  44.6 1.1 collective-permute-done.1.p1.n1
  45.7 1.9 %collective-permute-start.2 = (bf16[64,4096]{1,0:T(8,128)(2,1)}, bf16[64,4096]{1,0:T(8,128)(2,1)}, u32[]{:S(2)}, u32[]{:S(2)}) collective-permute-start(bf16[64,4096]{1,0:T(8,128)(2,1)} %collective-permute-done.1.p1.n1), channel_id=1, source_target_pairs={{0,1},{1,0},{2,3},{3,2},{4,5},{5,4},{6,7},{7,6},{8,9},{9,8},{10,11... | collective-permute-start | bytes 1572872 | tf_op jit(solution)/shard_map/ppermute | solution.py:236
  47.7 0.1 pad_add_fusion.me_ref.ids_ref
  47.8 0.0 copy-done.1
  47.8 0.0 copy-start
  47.8 2.1 %near_m.1.near_m_ref = f32[256,256]{1,0:T(8,128)S(1)} custom-call(bf16[64,4096]{1,0:T(8,128)(2,1)S(1)} %bitcast.8, bf16[64,4096]{1,0:T(8,128)(2,1)} %collective-permute-done.1.p1.n1, bf16[64,4096]{1,0:T(8,128)(2,1)} %collective-permute-done.3.p2.n2, bf16[64,4096]{1,0:T(8,128)(2,1)S(1)} %collective-permute-done.5.p3.n3, bf16[4096,256]{1,0:T(8,128)(2,1)S(1)} %copy-done.1), custom_call_target="tpu_custom_call" | custom-call | tf_op jit(solution)/shard_map/near_m/pallas_call | solution.py:267
  49.8 0.0 copy-done
  49.8 0.0 copy-start.3
  49.9 0.0 copy-start.5
  49.9 2.0 %near_s.1.near_s_ref = f32[256,256]{1,0:T(8,128)S(1)} custom-call(bf16[64,4096]{1,0:T(8,128)(2,1)S(1)} %bitcast.9, bf16[64,4096]{1,0:T(8,128)(2,1)} %collective-permute-done.1.p1.n1, bf16[64,4096]{1,0:T(8,128)(2,1)} %collective-permute-done.3.p2.n2, bf16[64,4096]{1,0:T(8,128)(2,1)S(1)} %collective-permute-done.5.p3.n3, bf16[4096,256]{1,0:T(8,128)(2,1)S(1)} %copy-done), custom_call_target="tpu_custom_call" | custom-call | tf_op jit(solution)/shard_map/near_s/pallas_call | solution.py:267
  51.9 0.0 collective-permute-done.p0.f0
  51.9 0.0 collective-permute-done.6.p3.f3
  51.9 0.0 collective-permute-done.4.p2.f2
  51.9 0.0 collective-permute-done.2.p1.f1
  51.9 0.0 copy-done.3
  51.9 0.0 copy-done.5
  51.9 3.3 %far.1 = (f32[512,256]{1,0:T(8,128)S(1)}, f32[512,256]{1,0:T(8,128)S(1)}, f32[32,8,256]{2,1,0:T(8,128)S(1)}) custom-call(s32[2]{0:T(128)S(1)} %pad_add_fusion.me_ref.ids_ref, bf16[64,4096]{1,0:T(8,128)(2,1)} %collective-permute-done.p0.f0, bf16[64,4096]{1,0:T(8,128)(2,1)} %collective-permute-done.2.p1.f1, bf16[64,4096]{1,0:T(8,128)(2,1)} %collective-permute-done.4.p2.f2, ...), custom_call_target="tpu_custom_call" | custom-call | tf_op jit(solution)/shard_map/far/pallas_call | solution.py:278
  55.3 16.5 %all_to_all.16.stats_ref = f32[32,8,256]{2,1,0:T(8,128)S(1)} all-to-all(f32[32,8,256]{2,1,0:T(8,128)S(1)} %get-tuple-element.20), channel_id=1, replica_groups=mesh['rep'=32,'fsdp'=32] {'fsdp'}, dimensions={0} | all-to-all | bytes 524288 | tf_op jit(solution)/shard_map/all_to_all | solution.py:287
  71.8 4.2 %second.1 = (bf16[8,256,128]{2,1,0:T(8,128)(2,1)S(1)}, bf16[8,256,128]{2,1,0:T(8,128)(2,1)S(1)}, bf16[8,256,128]{2,1,0:T(8,128)(2,1)S(1)}, bf16[8,256,128]{2,1,0:T(8,128)(2,1)S(1)}) custom-call(s32[2]{0:T(128)S(1)} %pad_add_fusion.me_ref.ids_ref, f32[32,8,256]{2,1,0:T(8,128)S(1)} %all_to_all.16.stats_ref, f32[512,256]{1,0:T(8,128)S(1)} %get-tuple-element.21.stream_ref, ...), custom_call_target="tpu_custom_call" | custom-call | tf_op jit(solution)/shard_map/second/pallas_call | solution.py:290
  76.0 3.7 %collective-permute-start.7 = (bf16[8,256,128]{2,1,0:T(8,128)(2,1)S(1)}, bf16[8,256,128]{2,1,0:T(8,128)(2,1)S(1)}, u32[]{:S(2)}, u32[]{:S(2)}) collective-permute-start(bf16[8,256,128]{2,1,0:T(8,128)(2,1)S(1)} %get-tuple-element.23), channel_id=1, source_target_pairs={{0,32},{1,97},{2,34},{3,99},{4,36},{5,101},{6,38},{7,103},{8,40},{... | collective-permute-start | bytes 1572872 | tf_op jit(solution)/shard_map/ppermute | solution.py:304
  79.7 4.0 %collective-permute-start.8 = (bf16[8,256,128]{2,1,0:T(8,128)(2,1)S(1)}, bf16[8,256,128]{2,1,0:T(8,128)(2,1)S(1)}, u32[]{:S(2)}, u32[]{:S(2)}) collective-permute-start(bf16[8,256,128]{2,1,0:T(8,128)(2,1)S(1)} %get-tuple-element.25), channel_id=1, source_target_pairs={{0,128},{32,160},{64,192},{96,224},{128,0},{160,32},{192,64},{224,... | collective-permute-start | bytes 1572872 | tf_op jit(solution)/shard_map/ppermute | solution.py:239
  83.7 16.0 %collective-permute-start.9 = (bf16[8,256,128]{2,1,0:T(8,128)(2,1)S(1)}, bf16[8,256,128]{2,1,0:T(8,128)(2,1)S(1)}, u32[]{:S(2)}, u32[]{:S(2)}) collective-permute-start(bf16[8,256,128]{2,1,0:T(8,128)(2,1)S(1)} %get-tuple-element.26), channel_id=1, source_target_pairs={{0,896},{32,928},{64,960},{96,992},{128,256},{160,288},{192,320},{... | collective-permute-start | bytes 1572872 | tf_op jit(solution)/shard_map/ppermute | solution.py:239
  99.7 0.0 collective-permute-done.7.side_ref
  99.7 0.0 collective-permute-done.8.even_ref
  99.7 10.5 %collective-permute-done.9.odd_ref = bf16[8,256,128]{2,1,0:T(8,128)(2,1)S(1)} collective-permute-done((bf16[8,256,128]{2,1,0:T(8,128)(2,1)S(1)}, bf16[8,256,128]{2,1,0:T(8,128)(2,1)S(1)}, u32[]{:S(2)}, u32[]{:S(2)}) %collective-permute-start.9) | collective-permute-done | bytes 524320 | tf_op jit(solution)/shard_map/ppermute | solution.py:239
  110.2 0.3 third.1
  110.5 29.8 %all_to_all.17.parts_ref = bf16[8,256,128]{2,1,0:T(8,128)(2,1)S(1)} all-to-all(bf16[8,256,128]{2,1,0:T(8,128)(2,1)S(1)} %third.1), channel_id=1, replica_groups={{0,64,288,352,512,576,800,864},{128,192,416,480,640,704,928,992},{32,96..., dimensions={0} | all-to-all | bytes 1048576 | tf_op jit(solution)/shard_map/all_to_all | solution.py:315
  140.3 0.8 last.1
Async XLA Ops:
  0.0 47.8 %copy-start.1 = (bf16[4096,256]{1,0:T(8,128)(2,1)S(1)}, bf16[4096,256]{1,0:T(8,128)(2,1)}, u32[]{:S(2)}) copy-start(bf16[4096,256]{1,0:T(8,128)(2,1)} %t_ref.1) | copy-start | bytes 6291460
  22.6 16.8 %collective-permute-start.5 = (bf16[64,4096]{1,0:T(8,128)(2,1)S(1)}, bf16[64,4096]{1,0:T(8,128)(2,1)S(1)}, u32[]{:S(2)}, u32[]{:S(2)}) collective-permute-start(bf16[64,4096]{1,0:T(8,128)(2,1)S(1)} %bitcast.3), channel_id=1, source_target_pairs={{0,16},{1,17},{2,18},{3,19},{4,20},{5,21},{6,22},{7,23},{8,24},{9,... | collective-permute-start | bytes 1572872 | tf_op jit(solution)/shard_map/ppermute | solution.py:236
  27.5 15.2 %collective-permute-start.3 = (bf16[64,4096]{1,0:T(8,128)(2,1)S(1)}, bf16[64,4096]{1,0:T(8,128)(2,1)}, u32[]{:S(2)}, u32[]{:S(2)}) collective-permute-start(bf16[64,4096]{1,0:T(8,128)(2,1)S(1)} %bitcast.4), channel_id=1, source_target_pairs={{0,14},{1,15},{2,4},{3,5},{4,2},{5,3},{6,8},{7,9},{8,6},{9,7},{10,... | collective-permute-start | bytes 1572872 | tf_op jit(solution)/shard_map/ppermute | solution.py:236
  30.6 15.1 %collective-permute-start.1 = (bf16[64,4096]{1,0:T(8,128)(2,1)S(1)}, bf16[64,4096]{1,0:T(8,128)(2,1)}, u32[]{:S(2)}, u32[]{:S(2)}) collective-permute-start(bf16[64,4096]{1,0:T(8,128)(2,1)S(1)} %bitcast.5), channel_id=1, source_target_pairs={{0,2},{1,3},{2,0},{3,1},{4,6},{5,7},{6,4},{7,5},{8,10},{9,11},{10,... | collective-permute-start | bytes 1572872 | tf_op jit(solution)/shard_map/ppermute | solution.py:236
  33.9 0.9 copy-start.6
  34.8 0.9 copy-start.7
  35.9 0.8 copy-start.2
  36.7 0.8 copy-start.4
  37.5 14.4 %collective-permute-start = (bf16[64,4096]{1,0:T(8,128)(2,1)S(1)}, bf16[64,4096]{1,0:T(8,128)(2,1)}, u32[]{:S(2)}, u32[]{:S(2)}) collective-permute-start(bf16[64,4096]{1,0:T(8,128)(2,1)S(1)} %bitcast.7), channel_id=1, source_target_pairs={{0,1},{1,0},{2,3},{3,2},{4,5},{5,4},{6,7},{7,6},{8,9},{9,8},{10,11... | collective-permute-start | bytes 1572872 | tf_op jit(solution)/shard_map/ppermute | solution.py:236
  39.4 12.5 %collective-permute-start.6 = (bf16[64,4096]{1,0:T(8,128)(2,1)S(1)}, bf16[64,4096]{1,0:T(8,128)(2,1)}, u32[]{:S(2)}, u32[]{:S(2)}) collective-permute-start(bf16[64,4096]{1,0:T(8,128)(2,1)S(1)} %collective-permute-done.5.p3.n3), channel_id=1, source_target_pairs={{0,1},{1,0},{2,3},{3,2},{4,5},{5,4},{6,7},{7,6},{8,9},{9,8},{10,11... | collective-permute-start | bytes 1572872 | tf_op jit(solution)/shard_map/ppermute | solution.py:236
  42.7 9.2 %collective-permute-start.4 = (bf16[64,4096]{1,0:T(8,128)(2,1)}, bf16[64,4096]{1,0:T(8,128)(2,1)}, u32[]{:S(2)}, u32[]{:S(2)}) collective-permute-start(bf16[64,4096]{1,0:T(8,128)(2,1)} %collective-permute-done.3.p2.n2), channel_id=1, source_target_pairs={{0,1},{1,0},{2,3},{3,2},{4,5},{5,4},{6,7},{7,6},{8,9},{9,8},{10,11... | collective-permute-start | bytes 1572872 | tf_op jit(solution)/shard_map/ppermute | solution.py:236
  45.7 6.2 %collective-permute-start.2 = (bf16[64,4096]{1,0:T(8,128)(2,1)}, bf16[64,4096]{1,0:T(8,128)(2,1)}, u32[]{:S(2)}, u32[]{:S(2)}) collective-permute-start(bf16[64,4096]{1,0:T(8,128)(2,1)} %collective-permute-done.1.p1.n1), channel_id=1, source_target_pairs={{0,1},{1,0},{2,3},{3,2},{4,5},{5,4},{6,7},{7,6},{8,9},{9,8},{10,11... | collective-permute-start | bytes 1572872 | tf_op jit(solution)/shard_map/ppermute | solution.py:236
  47.8 2.1 %copy-start = (bf16[4096,256]{1,0:T(8,128)(2,1)S(1)}, bf16[4096,256]{1,0:T(8,128)(2,1)}, u32[]{:S(2)}) copy-start(bf16[4096,256]{1,0:T(8,128)(2,1)} %w_ref.5) | copy-start | bytes 6291460
  49.8 2.1 %copy-start.3 = (f32[512,256]{1,0:T(8,128)S(1)}, f32[512,256]{1,0:T(8,128)}, u32[]{:S(2)}) copy-start(f32[512,256]{1,0:T(8,128)} %copy-done.2) | copy-start | bytes 1572868
  49.9 2.1 %copy-start.5 = (f32[512,256]{1,0:T(8,128)S(1)}, f32[512,256]{1,0:T(8,128)}, u32[]{:S(2)}) copy-start(f32[512,256]{1,0:T(8,128)} %copy-done.4) | copy-start | bytes 1572868
  76.0 23.6 %collective-permute-start.7 = (bf16[8,256,128]{2,1,0:T(8,128)(2,1)S(1)}, bf16[8,256,128]{2,1,0:T(8,128)(2,1)S(1)}, u32[]{:S(2)}, u32[]{:S(2)}) collective-permute-start(bf16[8,256,128]{2,1,0:T(8,128)(2,1)S(1)} %get-tuple-element.23), channel_id=1, source_target_pairs={{0,32},{1,97},{2,34},{3,99},{4,36},{5,101},{6,38},{7,103},{8,40},{... | collective-permute-start | bytes 1572872 | tf_op jit(solution)/shard_map/ppermute | solution.py:304
  79.7 20.0 %collective-permute-start.8 = (bf16[8,256,128]{2,1,0:T(8,128)(2,1)S(1)}, bf16[8,256,128]{2,1,0:T(8,128)(2,1)S(1)}, u32[]{:S(2)}, u32[]{:S(2)}) collective-permute-start(bf16[8,256,128]{2,1,0:T(8,128)(2,1)S(1)} %get-tuple-element.25), channel_id=1, source_target_pairs={{0,128},{32,160},{64,192},{96,224},{128,0},{160,32},{192,64},{224,... | collective-permute-start | bytes 1572872 | tf_op jit(solution)/shard_map/ppermute | solution.py:239
  83.7 26.5 %collective-permute-start.9 = (bf16[8,256,128]{2,1,0:T(8,128)(2,1)S(1)}, bf16[8,256,128]{2,1,0:T(8,128)(2,1)S(1)}, u32[]{:S(2)}, u32[]{:S(2)}) collective-permute-start(bf16[8,256,128]{2,1,0:T(8,128)(2,1)S(1)} %get-tuple-element.26), channel_id=1, source_target_pairs={{0,896},{32,928},{64,960},{96,992},{128,256},{160,288},{192,320},{... | collective-permute-start | bytes 1572872 | tf_op jit(solution)/shard_map/ppermute | solution.py:239

commit v5 on v4

--- a/solution.py
+++ b/solution.py
@@ -75,7 +75,7 @@
     x, y = me // (NY * NC), (me // NC) % NY
     own = (y + 2 * x) % 4
     to_even = 1 + 2 * (y % 2)
-    return [own, (own + to_even) % 4, (own + 4 - to_even) % 4, (own + 2) % 4]
+    return [own, (own + 2) % 4, (own + 4 - to_even) % 4, (own + to_even) % 4]
 
 
 def piece_rows(first, color):
@@ -204,7 +204,7 @@
             out_ref[2 * pair + 1] = out[:, 128:]
 
 
-def third_kernel(side_ref, own_ref, even_ref, odd_ref, out_ref):
+def third_kernel(own_ref, even_ref, odd_ref, side_ref, out_ref):
     f32 = jnp.float32
     for i in range(own_ref.shape[0]):
         out_ref[i] = (
@@ -247,9 +247,9 @@
     ).reshape(PIECE, features)
     near = [
         own,
+        in_group(own, lambda x, y, c: (x + 1, y, c)),
+        in_group(own, lambda x, y, c: (x, odd_partner(y), c)),
         in_group(own, lambda x, y, c: (x, even_partner(y), c)),
-        in_group(own, lambda x, y, c: (x, odd_partner(y), c)),
-        in_group(own, lambda x, y, c: (x + 1, y, c)),
     ]
     res, weighted = pl.pallas_call(
         prep_kernel,
@@ -311,7 +311,7 @@
         out_specs=VMEM,
         compiler_params=PARAMS,
         name="third",
-    )(side, mine, even, odd)
+    )(mine, even, odd, side)
     parts = lax.all_to_all(four, "rep", 0, 0, axis_index_groups=CLASSES)
     return pl.pallas_call(
         last_kernel,

time: 142 us -> 146 us (1.028)
  the two profiles are of different devices: /device:TPU:22 before, /device:TPU:1 now
where the time goes in v5:
time: 146 us; the launch traced here: 145 us
  blocking collectives  67.8 us (46%)
  starting transfers between devices  46.5 us (32%)
  Pallas kernels  12.8 us (9%)
  waiting for transfers between devices  11.7 us (8%)
  local copies, waits for them, and re-layouts  5.24 us (4%)
    all_to_all x1, blocking collectives, local(): parts = lax.all_to_all(four, 'rep', 0, 0, axis_index_groups=CLASSES)  27.6 us
    all_to_all x1, blocking collectives, local(): lax.all_to_all(jnp.broadcast_to(attn_out[None], (4, SHARD, features)), 'f...  23.6 us
    ppermute x2, starting transfers between devices, of_groups(): return lax.ppermute(x, 'rep', rep_perm(step))  20.1 us
    ppermute x7, starting transfers between devices, in_group(): return lax.ppermute(x, 'fsdp', fsdp_perm(step))  20.1 us
    all_to_all x1, blocking collectives, local(): stats = lax.all_to_all(stats, 'fsdp', 0, 0)  16.6 us
    ppermute x1, starting transfers between devices, local(): side = lax.ppermute(side, ('rep', 'fsdp'), side_perm())  6.3 us
    ppermute x2, waiting for transfers between devices, of_groups(): return lax.ppermute(x, 'rep', rep_perm(step))  5.94 us
    ppermute x1, waiting for transfers between devices, local(): side = lax.ppermute(side, ('rep', 'fsdp'), side_perm())  5.77 us
  transfers between devices with their start and end apart: 10, of which 2 were waited for; matrix products, arithmetic and copies ran while one was open for 1% of the time, Pallas kernels for 3%

profile of v5, /device:TPU:1, one launch (start us, length us, event | category | flops | bytes accessed | tf_op | source)
XLA Modules:
  0.0 145.0 jit_solution(7882375981443636675)
XLA Ops:
  0.0 0.0 copy-start.1
  0.0 1.1 broadcast_in_dim.4
  1.1 23.6 %all_to_all.15 = bf16[4,16,4096]{2,1,0:T(8,128)(2,1)S(1)} all-to-all(bf16[4,16,4096]{2,1,0:T(8,128)(2,1)S(1)} %broadcast_in_dim.4), channel_id=1, replica_groups={{0,8,20,28},{1,9,21,29},{2,10,22,30},{3,11,23,31},{4,12,16,24},{5,13,17..., dimensions={0} | all-to-all | bytes 1048576 | tf_op jit(solution)/shard_map/all_to_all | solution.py:244
  24.7 3.6 %collective-permute-start.5 = (bf16[64,4096]{1,0:T(8,128)(2,1)S(1)}, bf16[64,4096]{1,0:T(8,128)(2,1)S(1)}, u32[]{:S(2)}, u32[]{:S(2)}) collective-permute-start(bf16[64,4096]{1,0:T(8,128)(2,1)S(1)} %bitcast.3), channel_id=1, source_target_pairs={{0,2},{1,3},{2,0},{3,1},{4,6},{5,7},{6,4},{7,5},{8,10},{9,11},{10,... | collective-permute-start | bytes 1572872 | tf_op jit(solution)/shard_map/ppermute | solution.py:236
  28.4 1.9 %collective-permute-start.3 = (bf16[64,4096]{1,0:T(8,128)(2,1)S(1)}, bf16[64,4096]{1,0:T(8,128)(2,1)}, u32[]{:S(2)}, u32[]{:S(2)}) collective-permute-start(bf16[64,4096]{1,0:T(8,128)(2,1)S(1)} %bitcast.4), channel_id=1, source_target_pairs={{0,14},{1,15},{2,4},{3,5},{4,2},{5,3},{6,8},{7,9},{8,6},{9,7},{10,... | collective-permute-start | bytes 1572872 | tf_op jit(solution)/shard_map/ppermute | solution.py:236
  30.3 1.9 %collective-permute-start.1 = (bf16[64,4096]{1,0:T(8,128)(2,1)S(1)}, bf16[64,4096]{1,0:T(8,128)(2,1)}, u32[]{:S(2)}, u32[]{:S(2)}) collective-permute-start(bf16[64,4096]{1,0:T(8,128)(2,1)S(1)} %bitcast.5), channel_id=1, source_target_pairs={{0,16},{1,17},{2,18},{3,19},{4,20},{5,21},{6,22},{7,23},{8,24},{9,... | collective-permute-start | bytes 1572872 | tf_op jit(solution)/shard_map/ppermute | solution.py:236
  32.9 0.7 broadcast_in_dim.10.gain_ref
  33.5 0.0 copy-start.6
  33.5 0.9 copy-done.6
  34.5 0.0 copy-start.7
  34.5 0.9 copy-done.7
  35.4 0.1 prep.1
  35.5 0.0 copy-start.2
  35.5 0.8 copy-done.2
  36.3 0.0 copy-start.4
  36.3 0.8 copy-done.4
  37.1 6.1 %collective-permute-start = (bf16[64,4096]{1,0:T(8,128)(2,1)S(1)}, bf16[64,4096]{1,0:T(8,128)(2,1)}, u32[]{:S(2)}, u32[]{:S(2)}) collective-permute-start(bf16[64,4096]{1,0:T(8,128)(2,1)S(1)} %bitcast.7), channel_id=1, source_target_pairs={{0,1},{1,0},{2,3},{3,2},{4,5},{5,4},{6,7},{7,6},{8,9},{9,8},{10,11... | collective-permute-start | bytes 1572872 | tf_op jit(solution)/shard_map/ppermute | solution.py:236
  43.3 0.0 collective-permute-done.5.p3.n3
  43.3 1.9 %collective-permute-start.6 = (bf16[64,4096]{1,0:T(8,128)(2,1)S(1)}, bf16[64,4096]{1,0:T(8,128)(2,1)}, u32[]{:S(2)}, u32[]{:S(2)}) collective-permute-start(bf16[64,4096]{1,0:T(8,128)(2,1)S(1)} %collective-permute-done.5.p3.n3), channel_id=1, source_target_pairs={{0,1},{1,0},{2,3},{3,2},{4,5},{5,4},{6,7},{7,6},{8,9},{9,8},{10,11... | collective-permute-start | bytes 1572872 | tf_op jit(solution)/shard_map/ppermute | solution.py:236
  45.2 0.0 collective-permute-done.3.p2.n2
  45.2 2.6 %collective-permute-start.4 = (bf16[64,4096]{1,0:T(8,128)(2,1)}, bf16[64,4096]{1,0:T(8,128)(2,1)}, u32[]{:S(2)}, u32[]{:S(2)}) collective-permute-start(bf16[64,4096]{1,0:T(8,128)(2,1)} %collective-permute-done.3.p2.n2), channel_id=1, source_target_pairs={{0,1},{1,0},{2,3},{3,2},{4,5},{5,4},{6,7},{7,6},{8,9},{9,8},{10,11... | collective-permute-start | bytes 1572872 | tf_op jit(solution)/shard_map/ppermute | solution.py:236
  47.8 0.0 collective-permute-done.1.p1.n1
  47.8 1.9 %collective-permute-start.2 = (bf16[64,4096]{1,0:T(8,128)(2,1)}, bf16[64,4096]{1,0:T(8,128)(2,1)}, u32[]{:S(2)}, u32[]{:S(2)}) collective-permute-start(bf16[64,4096]{1,0:T(8,128)(2,1)} %collective-permute-done.1.p1.n1), channel_id=1, source_target_pairs={{0,1},{1,0},{2,3},{3,2},{4,5},{5,4},{6,7},{7,6},{8,9},{9,8},{10,11... | collective-permute-start | bytes 1572872 | tf_op jit(solution)/shard_map/ppermute | solution.py:236
  49.8 0.1 pad_add_fusion.me_ref.ids_ref
  49.9 0.0 copy-done.1
  49.9 0.0 copy-start
  49.9 2.1 %near_m.1.near_m_ref = f32[256,256]{1,0:T(8,128)S(1)} custom-call(bf16[64,4096]{1,0:T(8,128)(2,1)S(1)} %bitcast.8, bf16[64,4096]{1,0:T(8,128)(2,1)} %collective-permute-done.1.p1.n1, bf16[64,4096]{1,0:T(8,128)(2,1)} %collective-permute-done.3.p2.n2, bf16[64,4096]{1,0:T(8,128)(2,1)S(1)} %collective-permute-done.5.p3.n3, bf16[4096,256]{1,0:T(8,128)(2,1)S(1)} %copy-done.1), custom_call_target="tpu_custom_call" | custom-call | tf_op jit(solution)/shard_map/near_m/pallas_call | solution.py:267
  51.9 0.0 copy-done
  51.9 0.0 copy-start.3
  52.0 0.0 copy-start.5
  52.0 2.0 %near_s.1.near_s_ref = f32[256,256]{1,0:T(8,128)S(1)} custom-call(bf16[64,4096]{1,0:T(8,128)(2,1)S(1)} %bitcast.9, bf16[64,4096]{1,0:T(8,128)(2,1)} %collective-permute-done.1.p1.n1, bf16[64,4096]{1,0:T(8,128)(2,1)} %collective-permute-done.3.p2.n2, bf16[64,4096]{1,0:T(8,128)(2,1)S(1)} %collective-permute-done.5.p3.n3, bf16[4096,256]{1,0:T(8,128)(2,1)S(1)} %copy-done), custom_call_target="tpu_custom_call" | custom-call | tf_op jit(solution)/shard_map/near_s/pallas_call | solution.py:267
  54.0 0.0 collective-permute-done.p0.f0
  54.0 0.0 collective-permute-done.6.p3.f3
  54.0 0.0 collective-permute-done.4.p2.f2
  54.0 0.0 collective-permute-done.2.p1.f1
  54.0 0.0 copy-done.3
  54.0 0.0 copy-done.5
  54.1 3.3 %far.1 = (f32[512,256]{1,0:T(8,128)S(1)}, f32[512,256]{1,0:T(8,128)S(1)}, f32[32,8,256]{2,1,0:T(8,128)S(1)}) custom-call(s32[2]{0:T(128)S(1)} %pad_add_fusion.me_ref.ids_ref, bf16[64,4096]{1,0:T(8,128)(2,1)} %collective-permute-done.p0.f0, bf16[64,4096]{1,0:T(8,128)(2,1)} %collective-permute-done.2.p1.f1, bf16[64,4096]{1,0:T(8,128)(2,1)} %collective-permute-done.4.p2.f2, ...), custom_call_target="tpu_custom_call" | custom-call | tf_op jit(solution)/shard_map/far/pallas_call | solution.py:278
  57.4 16.6 %all_to_all.16.stats_ref = f32[32,8,256]{2,1,0:T(8,128)S(1)} all-to-all(f32[32,8,256]{2,1,0:T(8,128)S(1)} %get-tuple-element.20), channel_id=1, replica_groups=mesh['rep'=32,'fsdp'=32] {'fsdp'}, dimensions={0} | all-to-all | bytes 524288 | tf_op jit(solution)/shard_map/all_to_all | solution.py:287
  73.9 4.2 %second.1 = (bf16[8,256,128]{2,1,0:T(8,128)(2,1)S(1)}, bf16[8,256,128]{2,1,0:T(8,128)(2,1)S(1)}, bf16[8,256,128]{2,1,0:T(8,128)(2,1)S(1)}, bf16[8,256,128]{2,1,0:T(8,128)(2,1)S(1)}) custom-call(s32[2]{0:T(128)S(1)} %pad_add_fusion.me_ref.ids_ref, f32[32,8,256]{2,1,0:T(8,128)S(1)} %all_to_all.16.stats_ref, f32[512,256]{1,0:T(8,128)S(1)} %get-tuple-element.21.stream_ref, ...), custom_call_target="tpu_custom_call" | custom-call | tf_op jit(solution)/shard_map/second/pallas_call | solution.py:290
  78.2 4.8 %collective-permute-start.7 = (bf16[8,256,128]{2,1,0:T(8,128)(2,1)S(1)}, bf16[8,256,128]{2,1,0:T(8,128)(2,1)S(1)}, u32[]{:S(2)}, u32[]{:S(2)}) collective-permute-start(bf16[8,256,128]{2,1,0:T(8,128)(2,1)S(1)} %get-tuple-element.24), channel_id=1, source_target_pairs={{0,128},{32,160},{64,192},{96,224},{128,0},{160,32},{192,64},{224,... | collective-permute-start | bytes 1572872 | tf_op jit(solution)/shard_map/ppermute | solution.py:239
  83.0 15.3 %collective-permute-start.8 = (bf16[8,256,128]{2,1,0:T(8,128)(2,1)S(1)}, bf16[8,256,128]{2,1,0:T(8,128)(2,1)S(1)}, u32[]{:S(2)}, u32[]{:S(2)}) collective-permute-start(bf16[8,256,128]{2,1,0:T(8,128)(2,1)S(1)} %get-tuple-element.25), channel_id=1, source_target_pairs={{0,896},{32,928},{64,960},{96,992},{128,256},{160,288},{192,320},{... | collective-permute-start | bytes 1572872 | tf_op jit(solution)/shard_map/ppermute | solution.py:239
  98.3 6.3 %collective-permute-start.9 = (bf16[8,256,128]{2,1,0:T(8,128)(2,1)S(1)}, bf16[8,256,128]{2,1,0:T(8,128)(2,1)S(1)}, u32[]{:S(2)}, u32[]{:S(2)}) collective-permute-start(bf16[8,256,128]{2,1,0:T(8,128)(2,1)S(1)} %get-tuple-element.26), channel_id=1, source_target_pairs={{0,32},{1,97},{2,34},{3,99},{4,36},{5,101},{6,38},{7,103},{8,40},{... | collective-permute-start | bytes 1572872 | tf_op jit(solution)/shard_map/ppermute | solution.py:304
  104.6 0.0 collective-permute-done.7.even_ref
  104.6 5.9 %collective-permute-done.8.odd_ref = bf16[8,256,128]{2,1,0:T(8,128)(2,1)S(1)} collective-permute-done((bf16[8,256,128]{2,1,0:T(8,128)(2,1)S(1)}, bf16[8,256,128]{2,1,0:T(8,128)(2,1)S(1)}, u32[]{:S(2)}, u32[]{:S(2)}) %collective-permute-start.8) | collective-permute-done | bytes 524320 | tf_op jit(solution)/shard_map/ppermute | solution.py:239
  110.6 5.8 %collective-permute-done.9.side_ref = bf16[8,256,128]{2,1,0:T(8,128)(2,1)S(1)} collective-permute-done((bf16[8,256,128]{2,1,0:T(8,128)(2,1)S(1)}, bf16[8,256,128]{2,1,0:T(8,128)(2,1)S(1)}, u32[]{:S(2)}, u32[]{:S(2)}) %collective-permute-start.9) | collective-permute-done | bytes 524320 | tf_op jit(solution)/shard_map/ppermute | solution.py:304
  116.3 0.3 third.1
  116.6 27.6 %all_to_all.17.parts_ref = bf16[8,256,128]{2,1,0:T(8,128)(2,1)S(1)} all-to-all(bf16[8,256,128]{2,1,0:T(8,128)(2,1)S(1)} %third.1), channel_id=1, replica_groups={{0,64,288,352,512,576,800,864},{128,192,416,480,640,704,928,992},{32,96..., dimensions={0} | all-to-all | bytes 1048576 | tf_op jit(solution)/shard_map/all_to_all | solution.py:315
  144.2 0.8 last.1
Async XLA Ops:
  0.0 49.9 %copy-start.1 = (bf16[4096,256]{1,0:T(8,128)(2,1)S(1)}, bf16[4096,256]{1,0:T(8,128)(2,1)}, u32[]{:S(2)}) copy-start(bf16[4096,256]{1,0:T(8,128)(2,1)} %t_ref.1) | copy-start | bytes 6291460
  24.7 18.5 %collective-permute-start.5 = (bf16[64,4096]{1,0:T(8,128)(2,1)S(1)}, bf16[64,4096]{1,0:T(8,128)(2,1)S(1)}, u32[]{:S(2)}, u32[]{:S(2)}) collective-permute-start(bf16[64,4096]{1,0:T(8,128)(2,1)S(1)} %bitcast.3), channel_id=1, source_target_pairs={{0,2},{1,3},{2,0},{3,1},{4,6},{5,7},{6,4},{7,5},{8,10},{9,11},{10,... | collective-permute-start | bytes 1572872 | tf_op jit(solution)/shard_map/ppermute | solution.py:236
  28.4 16.8 %collective-permute-start.3 = (bf16[64,4096]{1,0:T(8,128)(2,1)S(1)}, bf16[64,4096]{1,0:T(8,128)(2,1)}, u32[]{:S(2)}, u32[]{:S(2)}) collective-permute-start(bf16[64,4096]{1,0:T(8,128)(2,1)S(1)} %bitcast.4), channel_id=1, source_target_pairs={{0,14},{1,15},{2,4},{3,5},{4,2},{5,3},{6,8},{7,9},{8,6},{9,7},{10,... | collective-permute-start | bytes 1572872 | tf_op jit(solution)/shard_map/ppermute | solution.py:236
  30.3 17.5 %collective-permute-start.1 = (bf16[64,4096]{1,0:T(8,128)(2,1)S(1)}, bf16[64,4096]{1,0:T(8,128)(2,1)}, u32[]{:S(2)}, u32[]{:S(2)}) collective-permute-start(bf16[64,4096]{1,0:T(8,128)(2,1)S(1)} %bitcast.5), channel_id=1, source_target_pairs={{0,16},{1,17},{2,18},{3,19},{4,20},{5,21},{6,22},{7,23},{8,24},{9,... | collective-permute-start | bytes 1572872 | tf_op jit(solution)/shard_map/ppermute | solution.py:236
  33.5 0.9 copy-start.6
  34.5 0.9 copy-start.7
  35.5 0.8 copy-start.2
  36.3 0.8 copy-start.4
  37.1 16.9 %collective-permute-start = (bf16[64,4096]{1,0:T(8,128)(2,1)S(1)}, bf16[64,4096]{1,0:T(8,128)(2,1)}, u32[]{:S(2)}, u32[]{:S(2)}) collective-permute-start(bf16[64,4096]{1,0:T(8,128)(2,1)S(1)} %bitcast.7), channel_id=1, source_target_pairs={{0,1},{1,0},{2,3},{3,2},{4,5},{5,4},{6,7},{7,6},{8,9},{9,8},{10,11... | collective-permute-start | bytes 1572872 | tf_op jit(solution)/shard_map/ppermute | solution.py:236
  43.3 10.7 %collective-permute-start.6 = (bf16[64,4096]{1,0:T(8,128)(2,1)S(1)}, bf16[64,4096]{1,0:T(8,128)(2,1)}, u32[]{:S(2)}, u32[]{:S(2)}) collective-permute-start(bf16[64,4096]{1,0:T(8,128)(2,1)S(1)} %collective-permute-done.5.p3.n3), channel_id=1, source_target_pairs={{0,1},{1,0},{2,3},{3,2},{4,5},{5,4},{6,7},{7,6},{8,9},{9,8},{10,11... | collective-permute-start | bytes 1572872 | tf_op jit(solution)/shard_map/ppermute | solution.py:236
  45.2 8.8 %collective-permute-start.4 = (bf16[64,4096]{1,0:T(8,128)(2,1)}, bf16[64,4096]{1,0:T(8,128)(2,1)}, u32[]{:S(2)}, u32[]{:S(2)}) collective-permute-start(bf16[64,4096]{1,0:T(8,128)(2,1)} %collective-permute-done.3.p2.n2), channel_id=1, source_target_pairs={{0,1},{1,0},{2,3},{3,2},{4,5},{5,4},{6,7},{7,6},{8,9},{9,8},{10,11... | collective-permute-start | bytes 1572872 | tf_op jit(solution)/shard_map/ppermute | solution.py:236
  47.8 6.2 %collective-permute-start.2 = (bf16[64,4096]{1,0:T(8,128)(2,1)}, bf16[64,4096]{1,0:T(8,128)(2,1)}, u32[]{:S(2)}, u32[]{:S(2)}) collective-permute-start(bf16[64,4096]{1,0:T(8,128)(2,1)} %collective-permute-done.1.p1.n1), channel_id=1, source_target_pairs={{0,1},{1,0},{2,3},{3,2},{4,5},{5,4},{6,7},{7,6},{8,9},{9,8},{10,11... | collective-permute-start | bytes 1572872 | tf_op jit(solution)/shard_map/ppermute | solution.py:236
  49.9 2.1 %copy-start = (bf16[4096,256]{1,0:T(8,128)(2,1)S(1)}, bf16[4096,256]{1,0:T(8,128)(2,1)}, u32[]{:S(2)}) copy-start(bf16[4096,256]{1,0:T(8,128)(2,1)} %w_ref.5) | copy-start | bytes 6291460
  51.9 2.1 %copy-start.3 = (f32[512,256]{1,0:T(8,128)S(1)}, f32[512,256]{1,0:T(8,128)}, u32[]{:S(2)}) copy-start(f32[512,256]{1,0:T(8,128)} %copy-done.2) | copy-start | bytes 1572868
  52.0 2.1 %copy-start.5 = (f32[512,256]{1,0:T(8,128)S(1)}, f32[512,256]{1,0:T(8,128)}, u32[]{:S(2)}) copy-start(f32[512,256]{1,0:T(8,128)} %copy-done.4) | copy-start | bytes 1572868
  78.2 26.4 %collective-permute-start.7 = (bf16[8,256,128]{2,1,0:T(8,128)(2,1)S(1)}, bf16[8,256,128]{2,1,0:T(8,128)(2,1)S(1)}, u32[]{:S(2)}, u32[]{:S(2)}) collective-permute-start(bf16[8,256,128]{2,1,0:T(8,128)(2,1)S(1)} %get-tuple-element.24), channel_id=1, source_target_pairs={{0,128},{32,160},{64,192},{96,224},{128,0},{160,32},{192,64},{224,... | collective-permute-start | bytes 1572872 | tf_op jit(solution)/shard_map/ppermute | solution.py:239
  83.0 27.6 %collective-permute-start.8 = (bf16[8,256,128]{2,1,0:T(8,128)(2,1)S(1)}, bf16[8,256,128]{2,1,0:T(8,128)(2,1)S(1)}, u32[]{:S(2)}, u32[]{:S(2)}) collective-permute-start(bf16[8,256,128]{2,1,0:T(8,128)(2,1)S(1)} %get-tuple-element.25), channel_id=1, source_target_pairs={{0,896},{32,928},{64,960},{96,992},{128,256},{160,288},{192,320},{... | collective-permute-start | bytes 1572872 | tf_op jit(solution)/shard_map/ppermute | solution.py:239
  98.3 18.0 %collective-permute-start.9 = (bf16[8,256,128]{2,1,0:T(8,128)(2,1)S(1)}, bf16[8,256,128]{2,1,0:T(8,128)(2,1)S(1)}, u32[]{:S(2)}, u32[]{:S(2)}) collective-permute-start(bf16[8,256,128]{2,1,0:T(8,128)(2,1)S(1)} %get-tuple-element.26), channel_id=1, source_target_pairs={{0,32},{1,97},{2,34},{3,99},{4,36},{5,101},{6,38},{7,103},{8,40},{... | collective-permute-start | bytes 1572872 | tf_op jit(solution)/shard_map/ppermute | solution.py:304

commit v6 on v5

--- a/solution.py
+++ b/solution.py
@@ -82,17 +82,6 @@
     return pl.ds(pl.multiple_of(first + color * PIECE, PIECE), PIECE)
 
 
-def prep_kernel(len_ref, after_ref, res_ref, cot_ref, gain_ref, res_out, weighted_ref):
-    gain = gain_ref[...].astype(jnp.float32)
-    for i, block in enumerate(BLOCKS):
-        token = block * SHARD + lax.broadcasted_iota(jnp.int32, (SHARD, 1), 0)
-        live = (token < len_ref[0]).astype(jnp.float32)
-        there = pl.ds(i * SHARD, SHARD)
-        here = pl.ds(block * SHARD, SHARD)
-        weighted_ref[there, :] = cot_ref[here, :].astype(jnp.float32) * gain * live
-        res_out[there, :] = res_ref[here, :].astype(jnp.float32)
-
-
 def product(pieces, w_ref):
     a = jnp.concatenate([piece[...] for piece in pieces], axis=0)
     return jnp.dot(a, w_ref[...], preferred_element_type=jnp.float32)
@@ -103,8 +92,9 @@
 
 
 def far_kernel(
-    me_ref, p0, p1, p2, p3, w_ref, t_ref, near_s_ref, near_m_ref, res_ref, weighted_ref,
-    stream_ref, moved_ref, stats_ref,
+    me_ref, len_ref, p0, p1, p2, p3, w_ref, t_ref, near_s_ref, near_m_ref,
+    res_ref, cot_ref, gain_ref,
+    stream_ref, moved_ref, weighted_ref, stats_ref,
 ):
     me = me_ref[0]
     core = me % NC
@@ -118,8 +108,15 @@
         moved_ref[near, :] = near_m_ref[here, :]
         stream_ref[far, :] = s[here]
         moved_ref[far, :] = m[here]
-    stream = stream_ref[...] + res_ref[...]
-    stream_ref[...] = stream
+    gain = gain_ref[...].astype(jnp.float32)
+    for i, block in enumerate(BLOCKS):
+        token = block * SHARD + lax.broadcasted_iota(jnp.int32, (SHARD, 1), 0)
+        live = (token < len_ref[0]).astype(jnp.float32)
+        there = pl.ds(i * SHARD, SHARD)
+        here = pl.ds(block * SHARD, SHARD)
+        weighted_ref[there, :] = cot_ref[here, :].astype(jnp.float32) * gain * live
+        stream_ref[there, :] += res_ref[here, :].astype(jnp.float32)
+    stream = stream_ref[...]
     moved = moved_ref[...]
     weighted = weighted_ref[...]
     sums = [
@@ -251,17 +248,8 @@
         in_group(own, lambda x, y, c: (x, odd_partner(y), c)),
         in_group(own, lambda x, y, c: (x, even_partner(y), c)),
     ]
-    res, weighted = pl.pallas_call(
-        prep_kernel,
-        out_shape=(shape(rows, columns), shape(rows, columns)),
-        in_specs=[SMEM, ANY, VMEM, VMEM, VMEM],
-        out_specs=(VMEM,) * 2,
-        compiler_params=PARAMS,
-        name="prep",
-    )(seq_len, own, residual, cotangent, gain)
-    ready, res = lax.optimization_barrier((own, res))
-
-    far = [in_group(piece, lambda x, y, c: (x, y, c + 1)) for piece in [ready] + near[1:]]
+    near[3], gain = lax.optimization_barrier((near[3], gain))
+    far = [in_group(piece, lambda x, y, c: (x, y, c + 1)) for piece in near]
 
     near_s, near_m = (
         pl.pallas_call(
@@ -275,14 +263,18 @@
         for name, w in (("near_s", out_weight), ("near_m", tangent))
     )
 
-    stream, moved, stats = pl.pallas_call(
+    whole = shape(rows, columns)
+    stream, moved, weighted, stats = pl.pallas_call(
         far_kernel,
-        out_shape=(shape(rows, columns), shape(rows, columns), shape(32, 8, HALF)),
-        in_specs=[SMEM] + [VMEM] * 10,
-        out_specs=(VMEM,) * 3,
+        out_shape=(whole, whole, whole, shape(32, 8, HALF)),
+        in_specs=[SMEM, SMEM] + [VMEM] * 11,
+        out_specs=(VMEM,) * 4,
         compiler_params=PARAMS,
         name="far",
-    )(ids, *far, out_weight, tangent, near_s, near_m, res, weighted)
+    )(
+        ids, seq_len, *far, out_weight, tangent, near_s, near_m,
+        residual, cotangent, gain,
+    )
 
     stats = lax.all_to_all(stats, "fsdp", 0, 0)
 

time: 146 us -> 146 us (level)
  starting transfers between devices: 46.5 us -> 50.6 us
  Pallas kernels: 12.8 us -> 8.93 us
    ppermute x7, starting transfers between devices: 20.1 us -> 24 us  [in_group(): return lax.ppermute(x, 'fsdp', fsdp_perm(step))]
    pallas_call x2, Pallas kernels: 4.07 us -> 1.45 us  [local(): pl.pallas_call(near_kernel, out_shape=shape(HALF, columns), in_specs=[VME...]
    pallas_call x2 -> x1, Pallas kernels: 3.42 us -> 3.02 us  [local(): pl.pallas_call(far_kernel, out_shape=(whole, whole, whole, shape(32, 8, H...]
    unnamed x16 -> x10, local copies, waits for them, and re-layouts: 3.49 us -> 3.33 us
  transfers between devices with their start and end apart: 10 -> 10, of which waited for: 2 -> 3; matrix products, arithmetic and copies ran while one was open for 1% -> 1% of each run, Pallas kernels for 3% -> 1%
where the time goes in v6:
time: 146 us; the launch traced here: 145 us
  blocking collectives  67.5 us (46%)
  starting transfers between devices  50.6 us (35%)
  waiting for transfers between devices  11.9 us (8%)
  Pallas kernels  8.93 us (6%)
  local copies, waits for them, and re-layouts  4.92 us (3%)
    all_to_all x1, blocking collectives, local(): parts = lax.all_to_all(four, 'rep', 0, 0, axis_index_groups=CLASSES)  27.3 us
    ppermute x7, starting transfers between devices, in_group(): return lax.ppermute(x, 'fsdp', fsdp_perm(step))  24 us
    all_to_all x1, blocking collectives, local(): lax.all_to_all(jnp.broadcast_to(attn_out[None], (4, SHARD, features)), 'f...  23.6 us
    ppermute x2, starting transfers between devices, of_groups(): return lax.ppermute(x, 'rep', rep_perm(step))  20.1 us
    all_to_all x1, blocking collectives, local(): stats = lax.all_to_all(stats, 'fsdp', 0, 0)  16.6 us
    ppermute x1, starting transfers between devices, local(): side = lax.ppermute(side, ('rep', 'fsdp'), side_perm())  6.53 us
    ppermute x1, waiting for transfers between devices, local(): side = lax.ppermute(side, ('rep', 'fsdp'), side_perm())  6 us
    ppermute x2, waiting for transfers between devices, of_groups(): return lax.ppermute(x, 'rep', rep_perm(step))  5.71 us
  transfers between devices with their start and end apart: 10, of which 3 were waited for; matrix products, arithmetic and copies ran while one was open for 1% of the time, Pallas kernels for 1%

profile of v6, /device:TPU:1, one launch (start us, length us, event | category | flops | bytes accessed | tf_op | source)
XLA Modules:
  0.0 144.8 jit_solution(10198126916348252614)
XLA Ops:
  0.0 0.9 broadcast_in_dim.4
  0.9 23.6 %all_to_all.15 = bf16[4,16,4096]{2,1,0:T(8,128)(2,1)S(1)} all-to-all(bf16[4,16,4096]{2,1,0:T(8,128)(2,1)S(1)} %broadcast_in_dim.4), channel_id=1, replica_groups={{0,8,20,28},{1,9,21,29},{2,10,22,30},{3,11,23,31},{4,12,16,24},{5,13,17..., dimensions={0} | all-to-all | bytes 1048576 | tf_op jit(solution)/shard_map/all_to_all | solution.py:241
  24.6 3.6 %collective-permute-start.5 = (bf16[64,4096]{1,0:T(8,128)(2,1)S(1)}, bf16[64,4096]{1,0:T(8,128)(2,1)S(1)}, u32[]{:S(2)}, u32[]{:S(2)}) collective-permute-start(bf16[64,4096]{1,0:T(8,128)(2,1)S(1)} %bitcast.3), channel_id=1, source_target_pairs={{0,2},{1,3},{2,0},{3,1},{4,6},{5,7},{6,4},{7,5},{8,10},{9,11},{10,... | collective-permute-start | bytes 1572872 | tf_op jit(solution)/shard_map/ppermute | solution.py:233
  28.2 1.9 %collective-permute-start.3 = (bf16[64,4096]{1,0:T(8,128)(2,1)S(1)}, bf16[64,4096]{1,0:T(8,128)(2,1)S(1)}, u32[]{:S(2)}, u32[]{:S(2)}) collective-permute-start(bf16[64,4096]{1,0:T(8,128)(2,1)S(1)} %bitcast.4), channel_id=1, source_target_pairs={{0,14},{1,15},{2,4},{3,5},{4,2},{5,3},{6,8},{7,9},{8,6},{9,7},{10,... | collective-permute-start | bytes 1572872 | tf_op jit(solution)/shard_map/ppermute | solution.py:233
  30.1 1.9 %collective-permute-start.1 = (bf16[64,4096]{1,0:T(8,128)(2,1)S(1)}, bf16[64,4096]{1,0:T(8,128)(2,1)S(1)}, u32[]{:S(2)}, u32[]{:S(2)}) collective-permute-start(bf16[64,4096]{1,0:T(8,128)(2,1)S(1)} %bitcast.5), channel_id=1, source_target_pairs={{0,16},{1,17},{2,18},{3,19},{4,20},{5,21},{6,22},{7,23},{8,24},{9,... | collective-permute-start | bytes 1572872 | tf_op jit(solution)/shard_map/ppermute | solution.py:233
  32.1 0.7 broadcast_in_dim.10.gain_ref
  32.7 6.1 %collective-permute-start = (bf16[64,4096]{1,0:T(8,128)(2,1)S(1)}, bf16[64,4096]{1,0:T(8,128)(2,1)S(1)}, u32[]{:S(2)}, u32[]{:S(2)}) collective-permute-start(bf16[64,4096]{1,0:T(8,128)(2,1)S(1)} %bitcast.6), channel_id=1, source_target_pairs={{0,1},{1,0},{2,3},{3,2},{4,5},{5,4},{6,7},{7,6},{8,9},{9,8},{10,11... | collective-permute-start | bytes 1572872 | tf_op jit(solution)/shard_map/ppermute | solution.py:233
  38.9 0.0 collective-permute-done.5.p3.n3
  38.9 4.1 %collective-permute-start.6 = (bf16[64,4096]{1,0:T(8,128)(2,1)S(1)}, bf16[64,4096]{1,0:T(8,128)(2,1)S(1)}, u32[]{:S(2)}, u32[]{:S(2)}) collective-permute-start(bf16[64,4096]{1,0:T(8,128)(2,1)S(1)} %collective-permute-done.5.p3.n3), channel_id=1, source_target_pairs={{0,1},{1,0},{2,3},{3,2},{4,5},{5,4},{6,7},{7,6},{8,9},{9,8},{10,11... | collective-permute-start | bytes 1572872 | tf_op jit(solution)/shard_map/ppermute | solution.py:233
  43.0 0.2 collective-permute-done.3.p2.n2
  43.2 4.4 %collective-permute-start.4 = (bf16[64,4096]{1,0:T(8,128)(2,1)S(1)}, bf16[64,4096]{1,0:T(8,128)(2,1)}, u32[]{:S(2)}, u32[]{:S(2)}) collective-permute-start(bf16[64,4096]{1,0:T(8,128)(2,1)S(1)} %collective-permute-done.3.p2.n2), channel_id=1, source_target_pairs={{0,1},{1,0},{2,3},{3,2},{4,5},{5,4},{6,7},{7,6},{8,9},{9,8},{10,11... | collective-permute-start | bytes 1572872 | tf_op jit(solution)/shard_map/ppermute | solution.py:233
  47.6 0.0 collective-permute-done.1.p1.n1
  47.6 1.9 %collective-permute-start.2 = (bf16[64,4096]{1,0:T(8,128)(2,1)S(1)}, bf16[64,4096]{1,0:T(8,128)(2,1)}, u32[]{:S(2)}, u32[]{:S(2)}) collective-permute-start(bf16[64,4096]{1,0:T(8,128)(2,1)S(1)} %collective-permute-done.1.p1.n1), channel_id=1, source_target_pairs={{0,1},{1,0},{2,3},{3,2},{4,5},{5,4},{6,7},{7,6},{8,9},{9,8},{10,11... | collective-permute-start | bytes 1572872 | tf_op jit(solution)/shard_map/ppermute | solution.py:233
  50.2 0.1 pad_add_fusion.me_ref.ids_ref
  50.3 0.0 copy-start.1
  50.3 1.6 %copy-done.1 = bf16[4096,256]{1,0:T(8,128)(2,1)S(1)} copy-done((bf16[4096,256]{1,0:T(8,128)(2,1)S(1)}, bf16[4096,256]{1,0:T(8,128)(2,1)}, u32[]{:S(2)}) %copy-start.1) | copy-done | bytes 2097176
  51.8 0.0 copy-start
  51.8 0.7 near_m.1.near_m_ref
  52.6 0.9 copy-done
  53.4 0.0 copy-start.2
  53.4 0.0 copy-start.3
  53.4 0.0 copy-start.4
  53.4 0.8 near_s.1.near_s_ref
  54.2 0.0 collective-permute-done.p0.f0
  54.2 0.0 collective-permute-done.6.p3.f3
  54.2 0.0 collective-permute-done.4.p2.f2
  54.2 0.0 collective-permute-done.2.p1.f1
  54.2 0.8 copy-done.2
  55.0 0.0 copy-done.3
  55.0 0.1 copy-done.4
  55.1 3.0 %far.1 = (f32[512,256]{1,0:T(8,128)S(1)}, f32[512,256]{1,0:T(8,128)S(1)}, f32[512,256]{1,0:T(8,128)S(1)}, f32[32,8,256]{2,1,0:T(8,128)S(1)}) custom-call(s32[2]{0:T(128)S(1)} %pad_add_fusion.me_ref.ids_ref, s32[1]{0:T(128)S(6)} %copy.8.len_ref, bf16[64,4096]{1,0:T(8,128)(2,1)S(1)} %collective-permute-done.p0.f0, ...), custom_call_target="tpu_custom_call" | custom-call | tf_op jit(solution)/shard_map/far/pallas_call | solution.py:267
  58.1 16.6 %all_to_all.16.stats_ref = f32[32,8,256]{2,1,0:T(8,128)S(1)} all-to-all(f32[32,8,256]{2,1,0:T(8,128)S(1)} %get-tuple-element.17), channel_id=1, replica_groups=mesh['rep'=32,'fsdp'=32] {'fsdp'}, dimensions={0} | all-to-all | bytes 524288 | tf_op jit(solution)/shard_map/all_to_all | solution.py:279
  74.7 3.4 %second.1 = (bf16[8,256,128]{2,1,0:T(8,128)(2,1)S(1)}, bf16[8,256,128]{2,1,0:T(8,128)(2,1)S(1)}, bf16[8,256,128]{2,1,0:T(8,128)(2,1)S(1)}, bf16[8,256,128]{2,1,0:T(8,128)(2,1)S(1)}) custom-call(s32[2]{0:T(128)S(1)} %pad_add_fusion.me_ref.ids_ref, f32[32,8,256]{2,1,0:T(8,128)S(1)} %all_to_all.16.stats_ref, f32[512,256]{1,0:T(8,128)S(1)} %get-tuple-element.18.stream_ref, ...), custom_call_target="tpu_custom_call" | custom-call | tf_op jit(solution)/shard_map/second/pallas_call | solution.py:282
  78.1 4.8 %collective-permute-start.7 = (bf16[8,256,128]{2,1,0:T(8,128)(2,1)S(1)}, bf16[8,256,128]{2,1,0:T(8,128)(2,1)S(1)}, u32[]{:S(2)}, u32[]{:S(2)}) collective-permute-start(bf16[8,256,128]{2,1,0:T(8,128)(2,1)S(1)} %get-tuple-element.22), channel_id=1, source_target_pairs={{0,128},{32,160},{64,192},{96,224},{128,0},{160,32},{192,64},{224,... | collective-permute-start | bytes 1572872 | tf_op jit(solution)/shard_map/ppermute | solution.py:236
  83.0 15.3 %collective-permute-start.8 = (bf16[8,256,128]{2,1,0:T(8,128)(2,1)S(1)}, bf16[8,256,128]{2,1,0:T(8,128)(2,1)S(1)}, u32[]{:S(2)}, u32[]{:S(2)}) collective-permute-start(bf16[8,256,128]{2,1,0:T(8,128)(2,1)S(1)} %get-tuple-element.23), channel_id=1, source_target_pairs={{0,896},{32,928},{64,960},{96,992},{128,256},{160,288},{192,320},{... | collective-permute-start | bytes 1572872 | tf_op jit(solution)/shard_map/ppermute | solution.py:236
  98.3 6.5 %collective-permute-start.9 = (bf16[8,256,128]{2,1,0:T(8,128)(2,1)S(1)}, bf16[8,256,128]{2,1,0:T(8,128)(2,1)S(1)}, u32[]{:S(2)}, u32[]{:S(2)}) collective-permute-start(bf16[8,256,128]{2,1,0:T(8,128)(2,1)S(1)} %get-tuple-element.24), channel_id=1, source_target_pairs={{0,32},{1,97},{2,34},{3,99},{4,36},{5,101},{6,38},{7,103},{8,40},{... | collective-permute-start | bytes 1572872 | tf_op jit(solution)/shard_map/ppermute | solution.py:296
  104.8 0.0 collective-permute-done.7.even_ref
  104.8 5.7 %collective-permute-done.8.odd_ref = bf16[8,256,128]{2,1,0:T(8,128)(2,1)S(1)} collective-permute-done((bf16[8,256,128]{2,1,0:T(8,128)(2,1)S(1)}, bf16[8,256,128]{2,1,0:T(8,128)(2,1)S(1)}, u32[]{:S(2)}, u32[]{:S(2)}) %collective-permute-start.8) | collective-permute-done | bytes 524320 | tf_op jit(solution)/shard_map/ppermute | solution.py:236
  110.5 6.0 %collective-permute-done.9.side_ref = bf16[8,256,128]{2,1,0:T(8,128)(2,1)S(1)} collective-permute-done((bf16[8,256,128]{2,1,0:T(8,128)(2,1)S(1)}, bf16[8,256,128]{2,1,0:T(8,128)(2,1)S(1)}, u32[]{:S(2)}, u32[]{:S(2)}) %collective-permute-start.9) | collective-permute-done | bytes 524320 | tf_op jit(solution)/shard_map/ppermute | solution.py:296
  116.5 0.3 third.1
  116.8 27.3 %all_to_all.17.parts_ref = bf16[8,256,128]{2,1,0:T(8,128)(2,1)S(1)} all-to-all(bf16[8,256,128]{2,1,0:T(8,128)(2,1)S(1)} %third.1), channel_id=1, replica_groups={{0,64,288,352,512,576,800,864},{128,192,416,480,640,704,928,992},{32,96..., dimensions={0} | all-to-all | bytes 1048576 | tf_op jit(solution)/shard_map/all_to_all | solution.py:307
  144.0 0.8 last.1
Async XLA Ops:
  24.6 14.3 %collective-permute-start.5 = (bf16[64,4096]{1,0:T(8,128)(2,1)S(1)}, bf16[64,4096]{1,0:T(8,128)(2,1)S(1)}, u32[]{:S(2)}, u32[]{:S(2)}) collective-permute-start(bf16[64,4096]{1,0:T(8,128)(2,1)S(1)} %bitcast.3), channel_id=1, source_target_pairs={{0,2},{1,3},{2,0},{3,1},{4,6},{5,7},{6,4},{7,5},{8,10},{9,11},{10,... | collective-permute-start | bytes 1572872 | tf_op jit(solution)/shard_map/ppermute | solution.py:233
  28.2 15.0 %collective-permute-start.3 = (bf16[64,4096]{1,0:T(8,128)(2,1)S(1)}, bf16[64,4096]{1,0:T(8,128)(2,1)S(1)}, u32[]{:S(2)}, u32[]{:S(2)}) collective-permute-start(bf16[64,4096]{1,0:T(8,128)(2,1)S(1)} %bitcast.4), channel_id=1, source_target_pairs={{0,14},{1,15},{2,4},{3,5},{4,2},{5,3},{6,8},{7,9},{8,6},{9,7},{10,... | collective-permute-start | bytes 1572872 | tf_op jit(solution)/shard_map/ppermute | solution.py:233
  30.1 17.4 %collective-permute-start.1 = (bf16[64,4096]{1,0:T(8,128)(2,1)S(1)}, bf16[64,4096]{1,0:T(8,128)(2,1)S(1)}, u32[]{:S(2)}, u32[]{:S(2)}) collective-permute-start(bf16[64,4096]{1,0:T(8,128)(2,1)S(1)} %bitcast.5), channel_id=1, source_target_pairs={{0,16},{1,17},{2,18},{3,19},{4,20},{5,21},{6,22},{7,23},{8,24},{9,... | collective-permute-start | bytes 1572872 | tf_op jit(solution)/shard_map/ppermute | solution.py:233
  32.7 21.5 %collective-permute-start = (bf16[64,4096]{1,0:T(8,128)(2,1)S(1)}, bf16[64,4096]{1,0:T(8,128)(2,1)S(1)}, u32[]{:S(2)}, u32[]{:S(2)}) collective-permute-start(bf16[64,4096]{1,0:T(8,128)(2,1)S(1)} %bitcast.6), channel_id=1, source_target_pairs={{0,1},{1,0},{2,3},{3,2},{4,5},{5,4},{6,7},{7,6},{8,9},{9,8},{10,11... | collective-permute-start | bytes 1572872 | tf_op jit(solution)/shard_map/ppermute | solution.py:233
  38.9 15.3 %collective-permute-start.6 = (bf16[64,4096]{1,0:T(8,128)(2,1)S(1)}, bf16[64,4096]{1,0:T(8,128)(2,1)S(1)}, u32[]{:S(2)}, u32[]{:S(2)}) collective-permute-start(bf16[64,4096]{1,0:T(8,128)(2,1)S(1)} %collective-permute-done.5.p3.n3), channel_id=1, source_target_pairs={{0,1},{1,0},{2,3},{3,2},{4,5},{5,4},{6,7},{7,6},{8,9},{9,8},{10,11... | collective-permute-start | bytes 1572872 | tf_op jit(solution)/shard_map/ppermute | solution.py:233
  43.2 11.0 %collective-permute-start.4 = (bf16[64,4096]{1,0:T(8,128)(2,1)S(1)}, bf16[64,4096]{1,0:T(8,128)(2,1)}, u32[]{:S(2)}, u32[]{:S(2)}) collective-permute-start(bf16[64,4096]{1,0:T(8,128)(2,1)S(1)} %collective-permute-done.3.p2.n2), channel_id=1, source_target_pairs={{0,1},{1,0},{2,3},{3,2},{4,5},{5,4},{6,7},{7,6},{8,9},{9,8},{10,11... | collective-permute-start | bytes 1572872 | tf_op jit(solution)/shard_map/ppermute | solution.py:233
  47.6 6.7 %collective-permute-start.2 = (bf16[64,4096]{1,0:T(8,128)(2,1)S(1)}, bf16[64,4096]{1,0:T(8,128)(2,1)}, u32[]{:S(2)}, u32[]{:S(2)}) collective-permute-start(bf16[64,4096]{1,0:T(8,128)(2,1)S(1)} %collective-permute-done.1.p1.n1), channel_id=1, source_target_pairs={{0,1},{1,0},{2,3},{3,2},{4,5},{5,4},{6,7},{7,6},{8,9},{9,8},{10,11... | collective-permute-start | bytes 1572872 | tf_op jit(solution)/shard_map/ppermute | solution.py:233
  50.3 1.6 %copy-start.1 = (bf16[4096,256]{1,0:T(8,128)(2,1)S(1)}, bf16[4096,256]{1,0:T(8,128)(2,1)}, u32[]{:S(2)}) copy-start(bf16[4096,256]{1,0:T(8,128)(2,1)} %t_ref.1) | copy-start | bytes 6291460
  51.8 1.6 %copy-start = (bf16[4096,256]{1,0:T(8,128)(2,1)S(1)}, bf16[4096,256]{1,0:T(8,128)(2,1)}, u32[]{:S(2)}) copy-start(bf16[4096,256]{1,0:T(8,128)(2,1)} %w_ref.5) | copy-start | bytes 6291460
  53.4 1.6 %copy-start.2 = (bf16[4096,256]{1,0:T(8,128)(2,1)S(1)}, bf16[4096,256]{1,0:T(8,128)(2,1)}, u32[]{:S(2)}) copy-start(bf16[4096,256]{1,0:T(8,128)(2,1)} %t_ref.1) | copy-start | bytes 6291460
  53.4 1.6 %copy-start.3 = (bf16[512,256]{1,0:T(8,128)(2,1)S(1)}, bf16[512,256]{1,0:T(8,128)(2,1)}, u32[]{:S(2)}) copy-start(bf16[512,256]{1,0:T(8,128)(2,1)} %res_ref.1) | copy-start | bytes 786436
  53.4 1.7 %copy-start.4 = (bf16[512,256]{1,0:T(8,128)(2,1)S(1)}, bf16[512,256]{1,0:T(8,128)(2,1)}, u32[]{:S(2)}) copy-start(bf16[512,256]{1,0:T(8,128)(2,1)} %cot_ref.1) | copy-start | bytes 786436
  78.1 26.7 %collective-permute-start.7 = (bf16[8,256,128]{2,1,0:T(8,128)(2,1)S(1)}, bf16[8,256,128]{2,1,0:T(8,128)(2,1)S(1)}, u32[]{:S(2)}, u32[]{:S(2)}) collective-permute-start(bf16[8,256,128]{2,1,0:T(8,128)(2,1)S(1)} %get-tuple-element.22), channel_id=1, source_target_pairs={{0,128},{32,160},{64,192},{96,224},{128,0},{160,32},{192,64},{224,... | collective-permute-start | bytes 1572872 | tf_op jit(solution)/shard_map/ppermute | solution.py:236
  83.0 27.6 %collective-permute-start.8 = (bf16[8,256,128]{2,1,0:T(8,128)(2,1)S(1)}, bf16[8,256,128]{2,1,0:T(8,128)(2,1)S(1)}, u32[]{:S(2)}, u32[]{:S(2)}) collective-permute-start(bf16[8,256,128]{2,1,0:T(8,128)(2,1)S(1)} %get-tuple-element.23), channel_id=1, source_target_pairs={{0,896},{32,928},{64,960},{96,992},{128,256},{160,288},{192,320},{... | collective-permute-start | bytes 1572872 | tf_op jit(solution)/shard_map/ppermute | solution.py:236
  98.3 18.3 %collective-permute-start.9 = (bf16[8,256,128]{2,1,0:T(8,128)(2,1)S(1)}, bf16[8,256,128]{2,1,0:T(8,128)(2,1)S(1)}, u32[]{:S(2)}, u32[]{:S(2)}) collective-permute-start(bf16[8,256,128]{2,1,0:T(8,128)(2,1)S(1)} %get-tuple-element.24), channel_id=1, source_target_pairs={{0,32},{1,97},{2,34},{3,99},{4,36},{5,101},{6,38},{7,103},{8,40},{... | collective-permute-start | bytes 1572872 | tf_op jit(solution)/shard_map/ppermute | solution.py:296

commit v7 on v6

--- a/solution.py
+++ b/solution.py
@@ -75,7 +75,7 @@
     x, y = me // (NY * NC), (me // NC) % NY
     own = (y + 2 * x) % 4
     to_even = 1 + 2 * (y % 2)
-    return [own, (own + 2) % 4, (own + 4 - to_even) % 4, (own + to_even) % 4]
+    return [own, (own + to_even) % 4, (own + 4 - to_even) % 4, (own + 2) % 4]
 
 
 def piece_rows(first, color):
@@ -201,7 +201,7 @@
             out_ref[2 * pair + 1] = out[:, 128:]
 
 
-def third_kernel(own_ref, even_ref, odd_ref, side_ref, out_ref):
+def third_kernel(side_ref, own_ref, even_ref, odd_ref, out_ref):
     f32 = jnp.float32
     for i in range(own_ref.shape[0]):
         out_ref[i] = (
@@ -244,12 +244,12 @@
     ).reshape(PIECE, features)
     near = [
         own,
+        in_group(own, lambda x, y, c: (x, even_partner(y), c)),
+        in_group(own, lambda x, y, c: (x, odd_partner(y), c)),
         in_group(own, lambda x, y, c: (x + 1, y, c)),
-        in_group(own, lambda x, y, c: (x, odd_partner(y), c)),
-        in_group(own, lambda x, y, c: (x, even_partner(y), c)),
     ]
-    near[3], gain = lax.optimization_barrier((near[3], gain))
-    far = [in_group(piece, lambda x, y, c: (x, y, c + 1)) for piece in near]
+    ready, gain, ids = lax.optimization_barrier((own, gain, ids))
+    far = [in_group(piece, lambda x, y, c: (x, y, c + 1)) for piece in [ready] + near[1:]]
 
     near_s, near_m = (
         pl.pallas_call(
@@ -303,7 +303,7 @@
         out_specs=VMEM,
         compiler_params=PARAMS,
         name="third",
-    )(mine, even, odd, side)
+    )(side, mine, even, odd)
     parts = lax.all_to_all(four, "rep", 0, 0, axis_index_groups=CLASSES)
     return pl.pallas_call(
         last_kernel,

time: 146 us -> 140 us (0.959)
  the two profiles are of different devices: /device:TPU:1 before, /device:TPU:20 now
where the time goes in v7:
time: 140 us; the launch traced here: 139 us
  blocking collectives  71.4 us (51%)
  starting transfers between devices  39.2 us (28%)
  waiting for transfers between devices  14.7 us (10%)
  Pallas kernels  7.85 us (6%)
  local copies, waits for them, and re-layouts  4.92 us (4%)
    all_to_all x1, blocking collectives, local(): parts = lax.all_to_all(four, 'rep', 0, 0, axis_index_groups=CLASSES)  30.8 us
    all_to_all x1, blocking collectives, local(): lax.all_to_all(jnp.broadcast_to(attn_out[None], (4, SHARD, features)), 'f...  23.9 us
    ppermute x2, starting transfers between devices, of_groups(): return lax.ppermute(x, 'rep', rep_perm(step))  19.9 us
    all_to_all x1, blocking collectives, local(): stats = lax.all_to_all(stats, 'fsdp', 0, 0)  16.6 us
    ppermute x7, starting transfers between devices, in_group(): return lax.ppermute(x, 'fsdp', fsdp_perm(step))  16.6 us
    ppermute x2, waiting for transfers between devices, of_groups(): return lax.ppermute(x, 'rep', rep_perm(step))  9.88 us
    ppermute x7, waiting for transfers between devices, in_group(): return lax.ppermute(x, 'fsdp', fsdp_perm(step))  4.85 us
    unnamed x10, local copies, waits for them, and re-layouts  3.32 us
  transfers between devices with their start and end apart: 10, of which 3 were waited for; matrix products, arithmetic and copies ran while one was open for 1% of the time, Pallas kernels for 1%

profile of v7, /device:TPU:20, one launch (start us, length us, event | category | flops | bytes accessed | tf_op | source)
XLA Modules:
  0.0 139.0 jit_solution(5024643557799177065)
XLA Ops:
  0.0 0.9 broadcast_in_dim.4
  0.9 23.9 %all_to_all.15 = bf16[4,16,4096]{2,1,0:T(8,128)(2,1)S(1)} all-to-all(bf16[4,16,4096]{2,1,0:T(8,128)(2,1)S(1)} %broadcast_in_dim.4), channel_id=1, replica_groups={{0,8,20,28},{1,9,21,29},{2,10,22,30},{3,11,23,31},{4,12,16,24},{5,13,17..., dimensions={0} | all-to-all | bytes 1048576 | tf_op jit(solution)/shard_map/all_to_all | solution.py:241
  24.9 1.9 %collective-permute-start.5 = (bf16[64,4096]{1,0:T(8,128)(2,1)S(1)}, bf16[64,4096]{1,0:T(8,128)(2,1)S(1)}, u32[]{:S(2)}, u32[]{:S(2)}) collective-permute-start(bf16[64,4096]{1,0:T(8,128)(2,1)S(1)} %bitcast.3), channel_id=1, source_target_pairs={{0,16},{1,17},{2,18},{3,19},{4,20},{5,21},{6,22},{7,23},{8,24},{9,... | collective-permute-start | bytes 1572872 | tf_op jit(solution)/shard_map/ppermute | solution.py:233
  26.8 3.2 %collective-permute-start.3 = (bf16[64,4096]{1,0:T(8,128)(2,1)S(1)}, bf16[64,4096]{1,0:T(8,128)(2,1)S(1)}, u32[]{:S(2)}, u32[]{:S(2)}) collective-permute-start(bf16[64,4096]{1,0:T(8,128)(2,1)S(1)} %bitcast.4), channel_id=1, source_target_pairs={{0,14},{1,15},{2,4},{3,5},{4,2},{5,3},{6,8},{7,9},{8,6},{9,7},{10,... | collective-permute-start | bytes 1572872 | tf_op jit(solution)/shard_map/ppermute | solution.py:233
  30.0 3.4 %collective-permute-start.1 = (bf16[64,4096]{1,0:T(8,128)(2,1)S(1)}, bf16[64,4096]{1,0:T(8,128)(2,1)S(1)}, u32[]{:S(2)}, u32[]{:S(2)}) collective-permute-start(bf16[64,4096]{1,0:T(8,128)(2,1)S(1)} %bitcast.5), channel_id=1, source_target_pairs={{0,2},{1,3},{2,0},{3,1},{4,6},{5,7},{6,4},{7,5},{8,10},{9,11},{10,... | collective-permute-start | bytes 1572872 | tf_op jit(solution)/shard_map/ppermute | solution.py:233
  33.4 0.7 broadcast_in_dim.10.gain_ref
  34.1 0.1 pad_add_fusion.me_ref.ids_ref
  34.1 1.9 %collective-permute-start = (bf16[64,4096]{1,0:T(8,128)(2,1)S(1)}, bf16[64,4096]{1,0:T(8,128)(2,1)S(1)}, u32[]{:S(2)}, u32[]{:S(2)}) collective-permute-start(bf16[64,4096]{1,0:T(8,128)(2,1)S(1)} %bitcast.6), channel_id=1, source_target_pairs={{0,1},{1,0},{2,3},{3,2},{4,5},{5,4},{6,7},{7,6},{8,9},{9,8},{10,11... | collective-permute-start | bytes 1572872 | tf_op jit(solution)/shard_map/ppermute | solution.py:233
  36.1 4.2 %collective-permute-done.5.p3.n3 = bf16[64,4096]{1,0:T(8,128)(2,1)S(1)} collective-permute-done((bf16[64,4096]{1,0:T(8,128)(2,1)S(1)}, bf16[64,4096]{1,0:T(8,128)(2,1)S(1)}, u32[]{:S(2)}, u32[]{:S(2)}) %collective-permute-start.5) | collective-permute-done | bytes 524320 | tf_op jit(solution)/shard_map/ppermute | solution.py:233
  40.3 1.9 %collective-permute-start.6 = (bf16[64,4096]{1,0:T(8,128)(2,1)S(1)}, bf16[64,4096]{1,0:T(8,128)(2,1)S(1)}, u32[]{:S(2)}, u32[]{:S(2)}) collective-permute-start(bf16[64,4096]{1,0:T(8,128)(2,1)S(1)} %collective-permute-done.5.p3.n3), channel_id=1, source_target_pairs={{0,1},{1,0},{2,3},{3,2},{4,5},{5,4},{6,7},{7,6},{8,9},{9,8},{10,11... | collective-permute-start | bytes 1572872 | tf_op jit(solution)/shard_map/ppermute | solution.py:233
  42.2 0.0 collective-permute-done.3.p2.n2
  42.2 2.4 %collective-permute-start.4 = (bf16[64,4096]{1,0:T(8,128)(2,1)S(1)}, bf16[64,4096]{1,0:T(8,128)(2,1)S(1)}, u32[]{:S(2)}, u32[]{:S(2)}) collective-permute-start(bf16[64,4096]{1,0:T(8,128)(2,1)S(1)} %collective-permute-done.3.p2.n2), channel_id=1, source_target_pairs={{0,1},{1,0},{2,3},{3,2},{4,5},{5,4},{6,7},{7,6},{8,9},{9,8},{10,11... | collective-permute-start | bytes 1572872 | tf_op jit(solution)/shard_map/ppermute | solution.py:233
  44.6 0.6 collective-permute-done.1.p1.n1
  45.2 1.9 %collective-permute-start.2 = (bf16[64,4096]{1,0:T(8,128)(2,1)S(1)}, bf16[64,4096]{1,0:T(8,128)(2,1)S(1)}, u32[]{:S(2)}, u32[]{:S(2)}) collective-permute-start(bf16[64,4096]{1,0:T(8,128)(2,1)S(1)} %collective-permute-done.1.p1.n1), channel_id=1, source_target_pairs={{0,1},{1,0},{2,3},{3,2},{4,5},{5,4},{6,7},{7,6},{8,9},{9,8},{10,11... | collective-permute-start | bytes 1572872 | tf_op jit(solution)/shard_map/ppermute | solution.py:233
  47.8 0.0 copy-start.1
  47.8 1.6 %copy-done.1 = bf16[4096,256]{1,0:T(8,128)(2,1)S(1)} copy-done((bf16[4096,256]{1,0:T(8,128)(2,1)S(1)}, bf16[4096,256]{1,0:T(8,128)(2,1)}, u32[]{:S(2)}) %copy-start.1) | copy-done | bytes 2097176
  49.4 0.0 copy-start
  49.4 0.7 near_m.1.near_m_ref
  50.1 0.9 copy-done
  51.0 0.0 copy-start.2
  51.0 0.0 copy-start.3
  51.0 0.0 copy-start.4
  51.0 0.8 near_s.1.near_s_ref
  51.7 0.0 collective-permute-done.p0.f0
  51.8 0.0 collective-permute-done.6.p3.f3
  51.8 0.0 collective-permute-done.4.p2.f2
  51.8 0.0 collective-permute-done.2.p1.f1
  51.8 0.8 copy-done.2
  52.6 0.0 copy-done.3
  52.6 0.1 copy-done.4
  52.6 2.4 %far.1 = (f32[512,256]{1,0:T(8,128)S(1)}, f32[512,256]{1,0:T(8,128)S(1)}, f32[512,256]{1,0:T(8,128)S(1)}, f32[32,8,256]{2,1,0:T(8,128)S(1)}) custom-call(s32[2]{0:T(128)S(1)} %pad_add_fusion.me_ref.ids_ref, s32[1]{0:T(128)S(6)} %copy.8.len_ref, bf16[64,4096]{1,0:T(8,128)(2,1)S(1)} %collective-permute-done.p0.f0, ...), custom_call_target="tpu_custom_call" | custom-call | tf_op jit(solution)/shard_map/far/pallas_call | solution.py:267
  55.0 16.6 %all_to_all.16.stats_ref = f32[32,8,256]{2,1,0:T(8,128)S(1)} all-to-all(f32[32,8,256]{2,1,0:T(8,128)S(1)} %get-tuple-element.19), channel_id=1, replica_groups=mesh['rep'=32,'fsdp'=32] {'fsdp'}, dimensions={0} | all-to-all | bytes 524288 | tf_op jit(solution)/shard_map/all_to_all | solution.py:279
  71.6 3.0 %second.1 = (bf16[8,256,128]{2,1,0:T(8,128)(2,1)S(1)}, bf16[8,256,128]{2,1,0:T(8,128)(2,1)S(1)}, bf16[8,256,128]{2,1,0:T(8,128)(2,1)S(1)}, bf16[8,256,128]{2,1,0:T(8,128)(2,1)S(1)}) custom-call(s32[2]{0:T(128)S(1)} %pad_add_fusion.me_ref.ids_ref, f32[32,8,256]{2,1,0:T(8,128)S(1)} %all_to_all.16.stats_ref, f32[512,256]{1,0:T(8,128)S(1)} %get-tuple-element.20.stream_ref, ...), custom_call_target="tpu_custom_call" | custom-call | tf_op jit(solution)/shard_map/second/pallas_call | solution.py:282
  74.7 2.7 %collective-permute-start.7 = (bf16[8,256,128]{2,1,0:T(8,128)(2,1)S(1)}, bf16[8,256,128]{2,1,0:T(8,128)(2,1)S(1)}, u32[]{:S(2)}, u32[]{:S(2)}) collective-permute-start(bf16[8,256,128]{2,1,0:T(8,128)(2,1)S(1)} %get-tuple-element.23), channel_id=1, source_target_pairs={{0,32},{1,97},{2,34},{3,99},{4,36},{5,101},{6,38},{7,103},{8,40},{... | collective-permute-start | bytes 1572872 | tf_op jit(solution)/shard_map/ppermute | solution.py:296
  77.4 5.1 %collective-permute-start.8 = (bf16[8,256,128]{2,1,0:T(8,128)(2,1)S(1)}, bf16[8,256,128]{2,1,0:T(8,128)(2,1)S(1)}, u32[]{:S(2)}, u32[]{:S(2)}) collective-permute-start(bf16[8,256,128]{2,1,0:T(8,128)(2,1)S(1)} %get-tuple-element.25), channel_id=1, source_target_pairs={{0,128},{32,160},{64,192},{96,224},{128,0},{160,32},{192,64},{224,... | collective-permute-start | bytes 1572872 | tf_op jit(solution)/shard_map/ppermute | solution.py:236
  82.4 14.8 %collective-permute-start.9 = (bf16[8,256,128]{2,1,0:T(8,128)(2,1)S(1)}, bf16[8,256,128]{2,1,0:T(8,128)(2,1)S(1)}, u32[]{:S(2)}, u32[]{:S(2)}) collective-permute-start(bf16[8,256,128]{2,1,0:T(8,128)(2,1)S(1)} %get-tuple-element.26), channel_id=1, source_target_pairs={{0,896},{32,928},{64,960},{96,992},{128,256},{160,288},{192,320},{... | collective-permute-start | bytes 1572872 | tf_op jit(solution)/shard_map/ppermute | solution.py:236
  97.3 0.0 collective-permute-done.7.side_ref
  97.3 0.0 collective-permute-done.8.even_ref
  97.3 9.9 %collective-permute-done.9.odd_ref = bf16[8,256,128]{2,1,0:T(8,128)(2,1)S(1)} collective-permute-done((bf16[8,256,128]{2,1,0:T(8,128)(2,1)S(1)}, bf16[8,256,128]{2,1,0:T(8,128)(2,1)S(1)}, u32[]{:S(2)}, u32[]{:S(2)}) %collective-permute-start.9) | collective-permute-done | bytes 524320 | tf_op jit(solution)/shard_map/ppermute | solution.py:236
  107.2 0.3 third.1
  107.4 30.8 %all_to_all.17.parts_ref = bf16[8,256,128]{2,1,0:T(8,128)(2,1)S(1)} all-to-all(bf16[8,256,128]{2,1,0:T(8,128)(2,1)S(1)} %third.1), channel_id=1, replica_groups={{0,64,288,352,512,576,800,864},{128,192,416,480,640,704,928,992},{32,96..., dimensions={0} | all-to-all | bytes 1048576 | tf_op jit(solution)/shard_map/all_to_all | solution.py:307
  138.2 0.8 last.1
Async XLA Ops:
  24.9 15.4 %collective-permute-start.5 = (bf16[64,4096]{1,0:T(8,128)(2,1)S(1)}, bf16[64,4096]{1,0:T(8,128)(2,1)S(1)}, u32[]{:S(2)}, u32[]{:S(2)}) collective-permute-start(bf16[64,4096]{1,0:T(8,128)(2,1)S(1)} %bitcast.3), channel_id=1, source_target_pairs={{0,16},{1,17},{2,18},{3,19},{4,20},{5,21},{6,22},{7,23},{8,24},{9,... | collective-permute-start | bytes 1572872 | tf_op jit(solution)/shard_map/ppermute | solution.py:233
  26.8 15.4 %collective-permute-start.3 = (bf16[64,4096]{1,0:T(8,128)(2,1)S(1)}, bf16[64,4096]{1,0:T(8,128)(2,1)S(1)}, u32[]{:S(2)}, u32[]{:S(2)}) collective-permute-start(bf16[64,4096]{1,0:T(8,128)(2,1)S(1)} %bitcast.4), channel_id=1, source_target_pairs={{0,14},{1,15},{2,4},{3,5},{4,2},{5,3},{6,8},{7,9},{8,6},{9,7},{10,... | collective-permute-start | bytes 1572872 | tf_op jit(solution)/shard_map/ppermute | solution.py:233
  30.0 15.3 %collective-permute-start.1 = (bf16[64,4096]{1,0:T(8,128)(2,1)S(1)}, bf16[64,4096]{1,0:T(8,128)(2,1)S(1)}, u32[]{:S(2)}, u32[]{:S(2)}) collective-permute-start(bf16[64,4096]{1,0:T(8,128)(2,1)S(1)} %bitcast.5), channel_id=1, source_target_pairs={{0,2},{1,3},{2,0},{3,1},{4,6},{5,7},{6,4},{7,5},{8,10},{9,11},{10,... | collective-permute-start | bytes 1572872 | tf_op jit(solution)/shard_map/ppermute | solution.py:233
  34.1 17.6 %collective-permute-start = (bf16[64,4096]{1,0:T(8,128)(2,1)S(1)}, bf16[64,4096]{1,0:T(8,128)(2,1)S(1)}, u32[]{:S(2)}, u32[]{:S(2)}) collective-permute-start(bf16[64,4096]{1,0:T(8,128)(2,1)S(1)} %bitcast.6), channel_id=1, source_target_pairs={{0,1},{1,0},{2,3},{3,2},{4,5},{5,4},{6,7},{7,6},{8,9},{9,8},{10,11... | collective-permute-start | bytes 1572872 | tf_op jit(solution)/shard_map/ppermute | solution.py:233
  40.3 11.5 %collective-permute-start.6 = (bf16[64,4096]{1,0:T(8,128)(2,1)S(1)}, bf16[64,4096]{1,0:T(8,128)(2,1)S(1)}, u32[]{:S(2)}, u32[]{:S(2)}) collective-permute-start(bf16[64,4096]{1,0:T(8,128)(2,1)S(1)} %collective-permute-done.5.p3.n3), channel_id=1, source_target_pairs={{0,1},{1,0},{2,3},{3,2},{4,5},{5,4},{6,7},{7,6},{8,9},{9,8},{10,11... | collective-permute-start | bytes 1572872 | tf_op jit(solution)/shard_map/ppermute | solution.py:233
  42.2 9.6 %collective-permute-start.4 = (bf16[64,4096]{1,0:T(8,128)(2,1)S(1)}, bf16[64,4096]{1,0:T(8,128)(2,1)S(1)}, u32[]{:S(2)}, u32[]{:S(2)}) collective-permute-start(bf16[64,4096]{1,0:T(8,128)(2,1)S(1)} %collective-permute-done.3.p2.n2), channel_id=1, source_target_pairs={{0,1},{1,0},{2,3},{3,2},{4,5},{5,4},{6,7},{7,6},{8,9},{9,8},{10,11... | collective-permute-start | bytes 1572872 | tf_op jit(solution)/shard_map/ppermute | solution.py:233
  45.2 6.5 %collective-permute-start.2 = (bf16[64,4096]{1,0:T(8,128)(2,1)S(1)}, bf16[64,4096]{1,0:T(8,128)(2,1)S(1)}, u32[]{:S(2)}, u32[]{:S(2)}) collective-permute-start(bf16[64,4096]{1,0:T(8,128)(2,1)S(1)} %collective-permute-done.1.p1.n1), channel_id=1, source_target_pairs={{0,1},{1,0},{2,3},{3,2},{4,5},{5,4},{6,7},{7,6},{8,9},{9,8},{10,11... | collective-permute-start | bytes 1572872 | tf_op jit(solution)/shard_map/ppermute | solution.py:233
  47.8 1.6 %copy-start.1 = (bf16[4096,256]{1,0:T(8,128)(2,1)S(1)}, bf16[4096,256]{1,0:T(8,128)(2,1)}, u32[]{:S(2)}) copy-start(bf16[4096,256]{1,0:T(8,128)(2,1)} %t_ref.1) | copy-start | bytes 6291460
  49.4 1.6 %copy-start = (bf16[4096,256]{1,0:T(8,128)(2,1)S(1)}, bf16[4096,256]{1,0:T(8,128)(2,1)}, u32[]{:S(2)}) copy-start(bf16[4096,256]{1,0:T(8,128)(2,1)} %w_ref.5) | copy-start | bytes 6291460
  51.0 1.6 %copy-start.2 = (bf16[4096,256]{1,0:T(8,128)(2,1)S(1)}, bf16[4096,256]{1,0:T(8,128)(2,1)}, u32[]{:S(2)}) copy-start(bf16[4096,256]{1,0:T(8,128)(2,1)} %t_ref.1) | copy-start | bytes 6291460
  51.0 1.6 %copy-start.3 = (bf16[512,256]{1,0:T(8,128)(2,1)S(1)}, bf16[512,256]{1,0:T(8,128)(2,1)}, u32[]{:S(2)}) copy-start(bf16[512,256]{1,0:T(8,128)(2,1)} %res_ref.1) | copy-start | bytes 786436
  51.0 1.7 %copy-start.4 = (bf16[512,256]{1,0:T(8,128)(2,1)S(1)}, bf16[512,256]{1,0:T(8,128)(2,1)}, u32[]{:S(2)}) copy-start(bf16[512,256]{1,0:T(8,128)(2,1)} %cot_ref.1) | copy-start | bytes 786436
  74.7 22.6 %collective-permute-start.7 = (bf16[8,256,128]{2,1,0:T(8,128)(2,1)S(1)}, bf16[8,256,128]{2,1,0:T(8,128)(2,1)S(1)}, u32[]{:S(2)}, u32[]{:S(2)}) collective-permute-start(bf16[8,256,128]{2,1,0:T(8,128)(2,1)S(1)} %get-tuple-element.23), channel_id=1, source_target_pairs={{0,32},{1,97},{2,34},{3,99},{4,36},{5,101},{6,38},{7,103},{8,40},{... | collective-permute-start | bytes 1572872 | tf_op jit(solution)/shard_map/ppermute | solution.py:296
  77.4 19.9 %collective-permute-start.8 = (bf16[8,256,128]{2,1,0:T(8,128)(2,1)S(1)}, bf16[8,256,128]{2,1,0:T(8,128)(2,1)S(1)}, u32[]{:S(2)}, u32[]{:S(2)}) collective-permute-start(bf16[8,256,128]{2,1,0:T(8,128)(2,1)S(1)} %get-tuple-element.25), channel_id=1, source_target_pairs={{0,128},{32,160},{64,192},{96,224},{128,0},{160,32},{192,64},{224,... | collective-permute-start | bytes 1572872 | tf_op jit(solution)/shard_map/ppermute | solution.py:236
  82.4 24.8 %collective-permute-start.9 = (bf16[8,256,128]{2,1,0:T(8,128)(2,1)S(1)}, bf16[8,256,128]{2,1,0:T(8,128)(2,1)S(1)}, u32[]{:S(2)}, u32[]{:S(2)}) collective-permute-start(bf16[8,256,128]{2,1,0:T(8,128)(2,1)S(1)} %get-tuple-element.26), channel_id=1, source_target_pairs={{0,896},{32,928},{64,960},{96,992},{128,256},{160,288},{192,320},{... | collective-permute-start | bytes 1572872 | tf_op jit(solution)/shard_map/ppermute | solution.py:236

commit v8 on v7

--- a/solution.py
+++ b/solution.py
@@ -92,22 +92,21 @@
 
 
 def far_kernel(
-    me_ref, len_ref, p0, p1, p2, p3, w_ref, t_ref, near_s_ref, near_m_ref,
+    me_ref, len_ref, n0, n1, n2, n3, f0, f1, f2, f3, w_ref, t_ref, near_s_ref,
     res_ref, cot_ref, gain_ref,
     stream_ref, moved_ref, weighted_ref, stats_ref,
 ):
     me = me_ref[0]
     core = me % NC
-    pieces = (p0, p1, p2, p3)
-    s, m = product(pieces, w_ref), product(pieces, t_ref)
-    for i, color in enumerate(piece_colors(me)):
-        here = slice(i * PIECE, (i + 1) * PIECE)
-        near = piece_rows(core * HALF, color)
-        far = piece_rows((1 - core) * HALF, color)
-        stream_ref[near, :] = near_s_ref[here, :]
-        moved_ref[near, :] = near_m_ref[here, :]
-        stream_ref[far, :] = s[here]
-        moved_ref[far, :] = m[here]
+    near, far = (n0, n1, n2, n3), (f0, f1, f2, f3)
+    for first, target, value in (
+        (core, stream_ref, near_s_ref[...]),
+        (1 - core, stream_ref, product(far, w_ref)),
+        (core, moved_ref, product(near, t_ref)),
+        (1 - core, moved_ref, product(far, t_ref)),
+    ):
+        for i, color in enumerate(piece_colors(me)):
+            target[piece_rows(first * HALF, color), :] = value[i * PIECE : (i + 1) * PIECE]
     gain = gain_ref[...].astype(jnp.float32)
     for i, block in enumerate(BLOCKS):
         token = block * SHARD + lax.broadcasted_iota(jnp.int32, (SHARD, 1), 0)
@@ -251,28 +250,25 @@
     ready, gain, ids = lax.optimization_barrier((own, gain, ids))
     far = [in_group(piece, lambda x, y, c: (x, y, c + 1)) for piece in [ready] + near[1:]]
 
-    near_s, near_m = (
-        pl.pallas_call(
-            near_kernel,
-            out_shape=shape(HALF, columns),
-            in_specs=[VMEM] * 5,
-            out_specs=VMEM,
-            compiler_params=PARAMS,
-            name=name,
-        )(*near, w)
-        for name, w in (("near_s", out_weight), ("near_m", tangent))
-    )
+    near_s = pl.pallas_call(
+        near_kernel,
+        out_shape=shape(HALF, columns),
+        in_specs=[VMEM] * 5,
+        out_specs=VMEM,
+        compiler_params=PARAMS,
+        name="near",
+    )(*near, out_weight)
 
     whole = shape(rows, columns)
     stream, moved, weighted, stats = pl.pallas_call(
         far_kernel,
         out_shape=(whole, whole, whole, shape(32, 8, HALF)),
-        in_specs=[SMEM, SMEM] + [VMEM] * 11,
+        in_specs=[SMEM, SMEM] + [VMEM] * 14,
         out_specs=(VMEM,) * 4,
         compiler_params=PARAMS,
         name="far",
     )(
-        ids, seq_len, *far, out_weight, tangent, near_s, near_m,
+        ids, seq_len, *near, *far, out_weight, tangent, near_s,
         residual, cotangent, gain,
     )
 

time: 140 us -> 138 us (0.986)
    unnamed x10 -> x8, local copies, waits for them, and re-layouts: 3.32 us -> 2.49 us
where the time goes in v8:
time: 138 us
  blocking collectives  71.4 us (52%)
  starting transfers between devices  39.2 us (28%)
  waiting for transfers between devices  14.7 us (11%)
  Pallas kernels  7.52 us (5%)
  local copies, waits for them, and re-layouts  4.09 us (3%)
    all_to_all x1, blocking collectives, local(): parts = lax.all_to_all(four, 'rep', 0, 0, axis_index_groups=CLASSES)  30.8 us
    all_to_all x1, blocking collectives, local(): lax.all_to_all(jnp.broadcast_to(attn_out[None], (4, SHARD, features)), 'f...  23.9 us
    ppermute x2, starting transfers between devices, of_groups(): return lax.ppermute(x, 'rep', rep_perm(step))  19.9 us
    all_to_all x1, blocking collectives, local(): stats = lax.all_to_all(stats, 'fsdp', 0, 0)  16.6 us
    ppermute x7, starting transfers between devices, in_group(): return lax.ppermute(x, 'fsdp', fsdp_perm(step))  16.6 us
    ppermute x2, waiting for transfers between devices, of_groups(): return lax.ppermute(x, 'rep', rep_perm(step))  9.88 us
    ppermute x7, waiting for transfers between devices, in_group(): return lax.ppermute(x, 'fsdp', fsdp_perm(step))  4.85 us
    pallas_call x1, Pallas kernels, local(): pl.pallas_call(second_kernel, out_shape=(whole,) * 4, in_specs=[SMEM] + [...  3.02 us
  transfers between devices with their start and end apart: 10, of which 3 were waited for; matrix products, arithmetic and copies ran while one was open for 1% of the time, Pallas kernels for 1%

profile of v8, /device:TPU:20, one launch (start us, length us, event | category | flops | bytes accessed | tf_op | source)
XLA Modules:
  0.0 137.8 jit_solution(7706608584833881700)
XLA Ops:
  0.0 0.9 broadcast_in_dim.4
  0.9 23.9 %all_to_all.15 = bf16[4,16,4096]{2,1,0:T(8,128)(2,1)S(1)} all-to-all(bf16[4,16,4096]{2,1,0:T(8,128)(2,1)S(1)} %broadcast_in_dim.4), channel_id=1, replica_groups={{0,8,20,28},{1,9,21,29},{2,10,22,30},{3,11,23,31},{4,12,16,24},{5,13,17..., dimensions={0} | all-to-all | bytes 1048576 | tf_op jit(solution)/shard_map/all_to_all | solution.py:240
  24.9 1.9 %collective-permute-start.2 = (bf16[64,4096]{1,0:T(8,128)(2,1)S(1)}, bf16[64,4096]{1,0:T(8,128)(2,1)S(1)}, u32[]{:S(2)}, u32[]{:S(2)}) collective-permute-start(bf16[64,4096]{1,0:T(8,128)(2,1)S(1)} %bitcast.3), channel_id=1, source_target_pairs={{0,16},{1,17},{2,18},{3,19},{4,20},{5,21},{6,22},{7,23},{8,24},{9,... | collective-permute-start | bytes 1572872 | tf_op jit(solution)/shard_map/ppermute | solution.py:232
  26.8 3.2 %collective-permute-start.1 = (bf16[64,4096]{1,0:T(8,128)(2,1)S(1)}, bf16[64,4096]{1,0:T(8,128)(2,1)S(1)}, u32[]{:S(2)}, u32[]{:S(2)}) collective-permute-start(bf16[64,4096]{1,0:T(8,128)(2,1)S(1)} %bitcast.4), channel_id=1, source_target_pairs={{0,14},{1,15},{2,4},{3,5},{4,2},{5,3},{6,8},{7,9},{8,6},{9,7},{10,... | collective-permute-start | bytes 1572872 | tf_op jit(solution)/shard_map/ppermute | solution.py:232
  30.0 3.4 %collective-permute-start = (bf16[64,4096]{1,0:T(8,128)(2,1)S(1)}, bf16[64,4096]{1,0:T(8,128)(2,1)S(1)}, u32[]{:S(2)}, u32[]{:S(2)}) collective-permute-start(bf16[64,4096]{1,0:T(8,128)(2,1)S(1)} %bitcast.5), channel_id=1, source_target_pairs={{0,2},{1,3},{2,0},{3,1},{4,6},{5,7},{6,4},{7,5},{8,10},{9,11},{10,... | collective-permute-start | bytes 1572872 | tf_op jit(solution)/shard_map/ppermute | solution.py:232
  33.4 0.7 broadcast_in_dim.10.gain_ref
  34.1 0.1 pad_add_fusion.me_ref.ids_ref
  34.1 1.9 %collective-permute-start.3 = (bf16[64,4096]{1,0:T(8,128)(2,1)S(1)}, bf16[64,4096]{1,0:T(8,128)(2,1)S(1)}, u32[]{:S(2)}, u32[]{:S(2)}) collective-permute-start(bf16[64,4096]{1,0:T(8,128)(2,1)S(1)} %bitcast.6), channel_id=1, source_target_pairs={{0,1},{1,0},{2,3},{3,2},{4,5},{5,4},{6,7},{7,6},{8,9},{9,8},{10,11... | collective-permute-start | bytes 1572872 | tf_op jit(solution)/shard_map/ppermute | solution.py:232
  36.1 4.2 %collective-permute-done.2.p3.n3 = bf16[64,4096]{1,0:T(8,128)(2,1)S(1)} collective-permute-done((bf16[64,4096]{1,0:T(8,128)(2,1)S(1)}, bf16[64,4096]{1,0:T(8,128)(2,1)S(1)}, u32[]{:S(2)}, u32[]{:S(2)}) %collective-permute-start.2) | collective-permute-done | bytes 524320 | tf_op jit(solution)/shard_map/ppermute | solution.py:232
  40.3 1.9 %collective-permute-start.6 = (bf16[64,4096]{1,0:T(8,128)(2,1)S(1)}, bf16[64,4096]{1,0:T(8,128)(2,1)S(1)}, u32[]{:S(2)}, u32[]{:S(2)}) collective-permute-start(bf16[64,4096]{1,0:T(8,128)(2,1)S(1)} %collective-permute-done.2.p3.n3), channel_id=1, source_target_pairs={{0,1},{1,0},{2,3},{3,2},{4,5},{5,4},{6,7},{7,6},{8,9},{9,8},{10,11... | collective-permute-start | bytes 1572872 | tf_op jit(solution)/shard_map/ppermute | solution.py:232
  42.2 0.0 collective-permute-done.1.p2.n2
  42.2 2.4 %collective-permute-start.5 = (bf16[64,4096]{1,0:T(8,128)(2,1)S(1)}, bf16[64,4096]{1,0:T(8,128)(2,1)S(1)}, u32[]{:S(2)}, u32[]{:S(2)}) collective-permute-start(bf16[64,4096]{1,0:T(8,128)(2,1)S(1)} %collective-permute-done.1.p2.n2), channel_id=1, source_target_pairs={{0,1},{1,0},{2,3},{3,2},{4,5},{5,4},{6,7},{7,6},{8,9},{9,8},{10,11... | collective-permute-start | bytes 1572872 | tf_op jit(solution)/shard_map/ppermute | solution.py:232
  44.6 0.6 collective-permute-done.p1.n1
  45.2 1.9 %collective-permute-start.4 = (bf16[64,4096]{1,0:T(8,128)(2,1)S(1)}, bf16[64,4096]{1,0:T(8,128)(2,1)S(1)}, u32[]{:S(2)}, u32[]{:S(2)}) collective-permute-start(bf16[64,4096]{1,0:T(8,128)(2,1)S(1)} %collective-permute-done.p1.n1), channel_id=1, source_target_pairs={{0,1},{1,0},{2,3},{3,2},{4,5},{5,4},{6,7},{7,6},{8,9},{9,8},{10,11... | collective-permute-start | bytes 1572872 | tf_op jit(solution)/shard_map/ppermute | solution.py:232
  47.8 0.0 copy-start
  47.8 1.6 %copy-done = bf16[4096,256]{1,0:T(8,128)(2,1)S(1)} copy-done((bf16[4096,256]{1,0:T(8,128)(2,1)S(1)}, bf16[4096,256]{1,0:T(8,128)(2,1)}, u32[]{:S(2)}) %copy-start) | copy-done | bytes 2097176
  49.4 0.0 copy-start.1
  49.4 0.0 copy-start.2
  49.4 0.0 copy-start.3
  49.4 0.7 near.1.near_s_ref
  50.1 0.0 collective-permute-done.3.f0
  50.1 0.0 collective-permute-done.6.f3
  50.1 0.0 collective-permute-done.5.f2
  50.1 0.0 collective-permute-done.4.f1
  50.2 0.8 copy-done.1
  51.0 0.0 copy-done.2
  51.0 0.1 copy-done.3
  51.0 2.8 %far.1 = (f32[512,256]{1,0:T(8,128)S(1)}, f32[512,256]{1,0:T(8,128)S(1)}, f32[512,256]{1,0:T(8,128)S(1)}, f32[32,8,256]{2,1,0:T(8,128)S(1)}) custom-call(s32[2]{0:T(128)S(1)} %pad_add_fusion.me_ref.ids_ref, s32[1]{0:T(128)S(6)} %copy.8.len_ref, bf16[64,4096]{1,0:T(8,128)(2,1)S(1)} %bitcast.8, bf16[64,4096]{1,0:T(8,128)(2,1)S(1)} %collective-permute-done.p1.n1, ...), custom_call_target="tpu_custom_call" | custom-call | tf_op jit(solution)/shard_map/far/pallas_call | solution.py:263
  53.8 16.6 %all_to_all.16.stats_ref = f32[32,8,256]{2,1,0:T(8,128)S(1)} all-to-all(f32[32,8,256]{2,1,0:T(8,128)S(1)} %get-tuple-element.19), channel_id=1, replica_groups=mesh['rep'=32,'fsdp'=32] {'fsdp'}, dimensions={0} | all-to-all | bytes 524288 | tf_op jit(solution)/shard_map/all_to_all | solution.py:275
  70.5 3.0 %second.1 = (bf16[8,256,128]{2,1,0:T(8,128)(2,1)S(1)}, bf16[8,256,128]{2,1,0:T(8,128)(2,1)S(1)}, bf16[8,256,128]{2,1,0:T(8,128)(2,1)S(1)}, bf16[8,256,128]{2,1,0:T(8,128)(2,1)S(1)}) custom-call(s32[2]{0:T(128)S(1)} %pad_add_fusion.me_ref.ids_ref, f32[32,8,256]{2,1,0:T(8,128)S(1)} %all_to_all.16.stats_ref, f32[512,256]{1,0:T(8,128)S(1)} %get-tuple-element.20.stream_ref, ...), custom_call_target="tpu_custom_call" | custom-call | tf_op jit(solution)/shard_map/second/pallas_call | solution.py:278
  73.5 2.7 %collective-permute-start.7 = (bf16[8,256,128]{2,1,0:T(8,128)(2,1)S(1)}, bf16[8,256,128]{2,1,0:T(8,128)(2,1)S(1)}, u32[]{:S(2)}, u32[]{:S(2)}) collective-permute-start(bf16[8,256,128]{2,1,0:T(8,128)(2,1)S(1)} %get-tuple-element.23), channel_id=1, source_target_pairs={{0,32},{1,97},{2,34},{3,99},{4,36},{5,101},{6,38},{7,103},{8,40},{... | collective-permute-start | bytes 1572872 | tf_op jit(solution)/shard_map/ppermute | solution.py:292
  76.2 5.1 %collective-permute-start.8 = (bf16[8,256,128]{2,1,0:T(8,128)(2,1)S(1)}, bf16[8,256,128]{2,1,0:T(8,128)(2,1)S(1)}, u32[]{:S(2)}, u32[]{:S(2)}) collective-permute-start(bf16[8,256,128]{2,1,0:T(8,128)(2,1)S(1)} %get-tuple-element.25), channel_id=1, source_target_pairs={{0,128},{32,160},{64,192},{96,224},{128,0},{160,32},{192,64},{224,... | collective-permute-start | bytes 1572872 | tf_op jit(solution)/shard_map/ppermute | solution.py:235
  81.3 14.8 %collective-permute-start.9 = (bf16[8,256,128]{2,1,0:T(8,128)(2,1)S(1)}, bf16[8,256,128]{2,1,0:T(8,128)(2,1)S(1)}, u32[]{:S(2)}, u32[]{:S(2)}) collective-permute-start(bf16[8,256,128]{2,1,0:T(8,128)(2,1)S(1)} %get-tuple-element.26), channel_id=1, source_target_pairs={{0,896},{32,928},{64,960},{96,992},{128,256},{160,288},{192,320},{... | collective-permute-start | bytes 1572872 | tf_op jit(solution)/shard_map/ppermute | solution.py:235
  96.1 0.0 collective-permute-done.7.side_ref
  96.1 0.0 collective-permute-done.8.even_ref
  96.1 9.9 %collective-permute-done.9.odd_ref = bf16[8,256,128]{2,1,0:T(8,128)(2,1)S(1)} collective-permute-done((bf16[8,256,128]{2,1,0:T(8,128)(2,1)S(1)}, bf16[8,256,128]{2,1,0:T(8,128)(2,1)S(1)}, u32[]{:S(2)}, u32[]{:S(2)}) %collective-permute-start.9) | collective-permute-done | bytes 524320 | tf_op jit(solution)/shard_map/ppermute | solution.py:235
  106.0 0.3 third.1
  106.3 30.8 %all_to_all.17.parts_ref = bf16[8,256,128]{2,1,0:T(8,128)(2,1)S(1)} all-to-all(bf16[8,256,128]{2,1,0:T(8,128)(2,1)S(1)} %third.1), channel_id=1, replica_groups={{0,64,288,352,512,576,800,864},{128,192,416,480,640,704,928,992},{32,96..., dimensions={0} | all-to-all | bytes 1048576 | tf_op jit(solution)/shard_map/all_to_all | solution.py:303
  137.1 0.8 last.1
Async XLA Ops:
  24.9 15.4 %collective-permute-start.2 = (bf16[64,4096]{1,0:T(8,128)(2,1)S(1)}, bf16[64,4096]{1,0:T(8,128)(2,1)S(1)}, u32[]{:S(2)}, u32[]{:S(2)}) collective-permute-start(bf16[64,4096]{1,0:T(8,128)(2,1)S(1)} %bitcast.3), channel_id=1, source_target_pairs={{0,16},{1,17},{2,18},{3,19},{4,20},{5,21},{6,22},{7,23},{8,24},{9,... | collective-permute-start | bytes 1572872 | tf_op jit(solution)/shard_map/ppermute | solution.py:232
  26.8 15.4 %collective-permute-start.1 = (bf16[64,4096]{1,0:T(8,128)(2,1)S(1)}, bf16[64,4096]{1,0:T(8,128)(2,1)S(1)}, u32[]{:S(2)}, u32[]{:S(2)}) collective-permute-start(bf16[64,4096]{1,0:T(8,128)(2,1)S(1)} %bitcast.4), channel_id=1, source_target_pairs={{0,14},{1,15},{2,4},{3,5},{4,2},{5,3},{6,8},{7,9},{8,6},{9,7},{10,... | collective-permute-start | bytes 1572872 | tf_op jit(solution)/shard_map/ppermute | solution.py:232
  30.0 15.3 %collective-permute-start = (bf16[64,4096]{1,0:T(8,128)(2,1)S(1)}, bf16[64,4096]{1,0:T(8,128)(2,1)S(1)}, u32[]{:S(2)}, u32[]{:S(2)}) collective-permute-start(bf16[64,4096]{1,0:T(8,128)(2,1)S(1)} %bitcast.5), channel_id=1, source_target_pairs={{0,2},{1,3},{2,0},{3,1},{4,6},{5,7},{6,4},{7,5},{8,10},{9,11},{10,... | collective-permute-start | bytes 1572872 | tf_op jit(solution)/shard_map/ppermute | solution.py:232
  34.1 16.0 %collective-permute-start.3 = (bf16[64,4096]{1,0:T(8,128)(2,1)S(1)}, bf16[64,4096]{1,0:T(8,128)(2,1)S(1)}, u32[]{:S(2)}, u32[]{:S(2)}) collective-permute-start(bf16[64,4096]{1,0:T(8,128)(2,1)S(1)} %bitcast.6), channel_id=1, source_target_pairs={{0,1},{1,0},{2,3},{3,2},{4,5},{5,4},{6,7},{7,6},{8,9},{9,8},{10,11... | collective-permute-start | bytes 1572872 | tf_op jit(solution)/shard_map/ppermute | solution.py:232
  40.3 9.8 %collective-permute-start.6 = (bf16[64,4096]{1,0:T(8,128)(2,1)S(1)}, bf16[64,4096]{1,0:T(8,128)(2,1)S(1)}, u32[]{:S(2)}, u32[]{:S(2)}) collective-permute-start(bf16[64,4096]{1,0:T(8,128)(2,1)S(1)} %collective-permute-done.2.p3.n3), channel_id=1, source_target_pairs={{0,1},{1,0},{2,3},{3,2},{4,5},{5,4},{6,7},{7,6},{8,9},{9,8},{10,11... | collective-permute-start | bytes 1572872 | tf_op jit(solution)/shard_map/ppermute | solution.py:232
  42.2 7.9 %collective-permute-start.5 = (bf16[64,4096]{1,0:T(8,128)(2,1)S(1)}, bf16[64,4096]{1,0:T(8,128)(2,1)S(1)}, u32[]{:S(2)}, u32[]{:S(2)}) collective-permute-start(bf16[64,4096]{1,0:T(8,128)(2,1)S(1)} %collective-permute-done.1.p2.n2), channel_id=1, source_target_pairs={{0,1},{1,0},{2,3},{3,2},{4,5},{5,4},{6,7},{7,6},{8,9},{9,8},{10,11... | collective-permute-start | bytes 1572872 | tf_op jit(solution)/shard_map/ppermute | solution.py:232
  45.2 4.9 %collective-permute-start.4 = (bf16[64,4096]{1,0:T(8,128)(2,1)S(1)}, bf16[64,4096]{1,0:T(8,128)(2,1)S(1)}, u32[]{:S(2)}, u32[]{:S(2)}) collective-permute-start(bf16[64,4096]{1,0:T(8,128)(2,1)S(1)} %collective-permute-done.p1.n1), channel_id=1, source_target_pairs={{0,1},{1,0},{2,3},{3,2},{4,5},{5,4},{6,7},{7,6},{8,9},{9,8},{10,11... | collective-permute-start | bytes 1572872 | tf_op jit(solution)/shard_map/ppermute | solution.py:232
  47.8 1.6 %copy-start = (bf16[4096,256]{1,0:T(8,128)(2,1)S(1)}, bf16[4096,256]{1,0:T(8,128)(2,1)}, u32[]{:S(2)}) copy-start(bf16[4096,256]{1,0:T(8,128)(2,1)} %w_ref.3) | copy-start | bytes 6291460
  49.4 1.6 %copy-start.1 = (bf16[4096,256]{1,0:T(8,128)(2,1)S(1)}, bf16[4096,256]{1,0:T(8,128)(2,1)}, u32[]{:S(2)}) copy-start(bf16[4096,256]{1,0:T(8,128)(2,1)} %t_ref.1) | copy-start | bytes 6291460
  49.4 1.6 %copy-start.2 = (bf16[512,256]{1,0:T(8,128)(2,1)S(1)}, bf16[512,256]{1,0:T(8,128)(2,1)}, u32[]{:S(2)}) copy-start(bf16[512,256]{1,0:T(8,128)(2,1)} %res_ref.1) | copy-start | bytes 786436
  49.4 1.7 %copy-start.3 = (bf16[512,256]{1,0:T(8,128)(2,1)S(1)}, bf16[512,256]{1,0:T(8,128)(2,1)}, u32[]{:S(2)}) copy-start(bf16[512,256]{1,0:T(8,128)(2,1)} %cot_ref.1) | copy-start | bytes 786436
  73.5 22.6 %collective-permute-start.7 = (bf16[8,256,128]{2,1,0:T(8,128)(2,1)S(1)}, bf16[8,256,128]{2,1,0:T(8,128)(2,1)S(1)}, u32[]{:S(2)}, u32[]{:S(2)}) collective-permute-start(bf16[8,256,128]{2,1,0:T(8,128)(2,1)S(1)} %get-tuple-element.23), channel_id=1, source_target_pairs={{0,32},{1,97},{2,34},{3,99},{4,36},{5,101},{6,38},{7,103},{8,40},{... | collective-permute-start | bytes 1572872 | tf_op jit(solution)/shard_map/ppermute | solution.py:292
  76.2 19.9 %collective-permute-start.8 = (bf16[8,256,128]{2,1,0:T(8,128)(2,1)S(1)}, bf16[8,256,128]{2,1,0:T(8,128)(2,1)S(1)}, u32[]{:S(2)}, u32[]{:S(2)}) collective-permute-start(bf16[8,256,128]{2,1,0:T(8,128)(2,1)S(1)} %get-tuple-element.25), channel_id=1, source_target_pairs={{0,128},{32,160},{64,192},{96,224},{128,0},{160,32},{192,64},{224,... | collective-permute-start | bytes 1572872 | tf_op jit(solution)/shard_map/ppermute | solution.py:235
  81.3 24.8 %collective-permute-start.9 = (bf16[8,256,128]{2,1,0:T(8,128)(2,1)S(1)}, bf16[8,256,128]{2,1,0:T(8,128)(2,1)S(1)}, u32[]{:S(2)}, u32[]{:S(2)}) collective-permute-start(bf16[8,256,128]{2,1,0:T(8,128)(2,1)S(1)} %get-tuple-element.26), channel_id=1, source_target_pairs={{0,896},{32,928},{64,960},{96,992},{128,256},{160,288},{192,320},{... | collective-permute-start | bytes 1572872 | tf_op jit(solution)/shard_map/ppermute | solution.py:235

commit v9 on v8

--- a/solution.py
+++ b/solution.py
@@ -14,7 +14,6 @@
 HALF = 256
 VMEM = pl.BlockSpec(memory_space=pltpu.VMEM)
 SMEM = pl.BlockSpec(memory_space=pltpu.SMEM)
-ANY = pl.BlockSpec(memory_space=pl.ANY)
 PARAMS = pltpu.CompilerParams(vmem_limit_bytes=16 * 1024 * 1024)
 
 
@@ -137,14 +136,8 @@
 def second_kernel(
     ids_ref, stats_ref, stream_ref, moved_ref, weighted_ref,
     n0, n1, n2, n3, f0, f1, f2, f3,
-    own_ref, side_ref, even_ref, odd_ref, curv_ref, a_ref, sems,
+    own_ref, side_ref, even_ref, odd_ref, curv_ref,
 ):
-    copies = [
-        pltpu.make_async_copy(piece, a_ref.at[pl.ds(i * PIECE, PIECE)], sems.at[i])
-        for i, piece in enumerate((n0, n1, n2, n3, f0, f1, f2, f3))
-    ]
-    for copy in copies:
-        copy.start()
     total = jnp.sum(stats_ref[...], axis=0)
     coefs = []
     for h in range(2):
@@ -176,8 +169,7 @@
         axis=0,
     )
     curv_t = curv.T.astype(jnp.bfloat16)
-    for copy in copies:
-        copy.wait()
+    pieces = (n0, n1, n2, n3, f0, f1, f2, f3)
     color = ids_ref[1]
     to_even = 1 + 2 * (color % 2)
     for out_ref, step in (
@@ -190,7 +182,7 @@
             columns = []
             for k in range(2):
                 at = pl.ds(pl.multiple_of((z * NH + h + 2 * k) * 128, 128), 128)
-                columns.append(a_ref[:, at])
+                columns.append(jnp.concatenate([p[:, at] for p in pieces], axis=0))
             out = jnp.dot(
                 curv_t,
                 jnp.concatenate(columns, axis=1),
@@ -278,13 +270,9 @@
     mine, side, even, odd = pl.pallas_call(
         second_kernel,
         out_shape=(whole,) * 4,
-        in_specs=[SMEM] + [VMEM] * 4 + [ANY] * 8,
+        in_specs=[SMEM] + [VMEM] * 12,
         out_specs=(VMEM,) * 4,
-        scratch_shapes=[
-            pltpu.VMEM((rows, columns), f32),
-            pltpu.VMEM((rows, features), bf16),
-            pltpu.SemaphoreType.DMA((8,)),
-        ],
+        scratch_shapes=[pltpu.VMEM((rows, columns), f32)],
         compiler_params=PARAMS,
         name="second",
     )(ids, stats, stream, moved, weighted, *near, *far)

time: 138 us -> 138 us (level)
  no operation moved by 1% of the time
where the time goes in v9:
time: 138 us
  blocking collectives  71.4 us (52%)
  starting transfers between devices  39.2 us (28%)
  waiting for transfers between devices  14.7 us (11%)
  Pallas kernels  7.18 us (5%)
  local copies, waits for them, and re-layouts  4.09 us (3%)
    all_to_all x1, blocking collectives, local(): parts = lax.all_to_all(four, 'rep', 0, 0, axis_index_groups=CLASSES)  30.8 us
    all_to_all x1, blocking collectives, local(): lax.all_to_all(jnp.broadcast_to(attn_out[None], (4, SHARD, features)), 'f...  23.9 us
    ppermute x2, starting transfers between devices, of_groups(): return lax.ppermute(x, 'rep', rep_perm(step))  19.9 us
    all_to_all x1, blocking collectives, local(): stats = lax.all_to_all(stats, 'fsdp', 0, 0)  16.6 us
    ppermute x7, starting transfers between devices, in_group(): return lax.ppermute(x, 'fsdp', fsdp_perm(step))  16.6 us
    ppermute x2, waiting for transfers between devices, of_groups(): return lax.ppermute(x, 'rep', rep_perm(step))  9.89 us
    ppermute x7, waiting for transfers between devices, in_group(): return lax.ppermute(x, 'fsdp', fsdp_perm(step))  4.85 us
    pallas_call x1, Pallas kernels, local(): pl.pallas_call(far_kernel, out_shape=(whole, whole, whole, shape(32, 8, H...  2.77 us
  transfers between devices with their start and end apart: 10, of which 3 were waited for; matrix products, arithmetic and copies ran while one was open for 1% of the time, Pallas kernels for 1%

profile of v9, /device:TPU:20, one launch (start us, length us, event | category | flops | bytes accessed | tf_op | source)
XLA Modules:
  0.0 137.5 jit_solution(3739157237149340210)
XLA Ops:
  0.0 0.9 broadcast_in_dim.4
  0.9 23.9 %all_to_all.15 = bf16[4,16,4096]{2,1,0:T(8,128)(2,1)S(1)} all-to-all(bf16[4,16,4096]{2,1,0:T(8,128)(2,1)S(1)} %broadcast_in_dim.4), channel_id=1, replica_groups={{0,8,20,28},{1,9,21,29},{2,10,22,30},{3,11,23,31},{4,12,16,24},{5,13,17..., dimensions={0} | all-to-all | bytes 1048576 | tf_op jit(solution)/shard_map/all_to_all | solution.py:232
  24.9 1.9 %collective-permute-start.2 = (bf16[64,4096]{1,0:T(8,128)(2,1)S(1)}, bf16[64,4096]{1,0:T(8,128)(2,1)S(1)}, u32[]{:S(2)}, u32[]{:S(2)}) collective-permute-start(bf16[64,4096]{1,0:T(8,128)(2,1)S(1)} %bitcast.3), channel_id=1, source_target_pairs={{0,16},{1,17},{2,18},{3,19},{4,20},{5,21},{6,22},{7,23},{8,24},{9,... | collective-permute-start | bytes 1572872 | tf_op jit(solution)/shard_map/ppermute | solution.py:224
  26.8 3.2 %collective-permute-start.1 = (bf16[64,4096]{1,0:T(8,128)(2,1)S(1)}, bf16[64,4096]{1,0:T(8,128)(2,1)S(1)}, u32[]{:S(2)}, u32[]{:S(2)}) collective-permute-start(bf16[64,4096]{1,0:T(8,128)(2,1)S(1)} %bitcast.4), channel_id=1, source_target_pairs={{0,14},{1,15},{2,4},{3,5},{4,2},{5,3},{6,8},{7,9},{8,6},{9,7},{10,... | collective-permute-start | bytes 1572872 | tf_op jit(solution)/shard_map/ppermute | solution.py:224
  30.0 3.4 %collective-permute-start = (bf16[64,4096]{1,0:T(8,128)(2,1)S(1)}, bf16[64,4096]{1,0:T(8,128)(2,1)S(1)}, u32[]{:S(2)}, u32[]{:S(2)}) collective-permute-start(bf16[64,4096]{1,0:T(8,128)(2,1)S(1)} %bitcast.5), channel_id=1, source_target_pairs={{0,2},{1,3},{2,0},{3,1},{4,6},{5,7},{6,4},{7,5},{8,10},{9,11},{10,... | collective-permute-start | bytes 1572872 | tf_op jit(solution)/shard_map/ppermute | solution.py:224
  33.4 0.7 broadcast_in_dim.10.gain_ref
  34.1 0.1 pad_add_fusion.me_ref.ids_ref
  34.1 1.9 %collective-permute-start.3 = (bf16[64,4096]{1,0:T(8,128)(2,1)S(1)}, bf16[64,4096]{1,0:T(8,128)(2,1)S(1)}, u32[]{:S(2)}, u32[]{:S(2)}) collective-permute-start(bf16[64,4096]{1,0:T(8,128)(2,1)S(1)} %bitcast.6), channel_id=1, source_target_pairs={{0,1},{1,0},{2,3},{3,2},{4,5},{5,4},{6,7},{7,6},{8,9},{9,8},{10,11... | collective-permute-start | bytes 1572872 | tf_op jit(solution)/shard_map/ppermute | solution.py:224
  36.1 4.2 %collective-permute-done.2.p3.n3 = bf16[64,4096]{1,0:T(8,128)(2,1)S(1)} collective-permute-done((bf16[64,4096]{1,0:T(8,128)(2,1)S(1)}, bf16[64,4096]{1,0:T(8,128)(2,1)S(1)}, u32[]{:S(2)}, u32[]{:S(2)}) %collective-permute-start.2) | collective-permute-done | bytes 524320 | tf_op jit(solution)/shard_map/ppermute | solution.py:224
  40.3 1.9 %collective-permute-start.6 = (bf16[64,4096]{1,0:T(8,128)(2,1)S(1)}, bf16[64,4096]{1,0:T(8,128)(2,1)S(1)}, u32[]{:S(2)}, u32[]{:S(2)}) collective-permute-start(bf16[64,4096]{1,0:T(8,128)(2,1)S(1)} %collective-permute-done.2.p3.n3), channel_id=1, source_target_pairs={{0,1},{1,0},{2,3},{3,2},{4,5},{5,4},{6,7},{7,6},{8,9},{9,8},{10,11... | collective-permute-start | bytes 1572872 | tf_op jit(solution)/shard_map/ppermute | solution.py:224
  42.2 0.0 collective-permute-done.1.p2.n2
  42.2 2.4 %collective-permute-start.5 = (bf16[64,4096]{1,0:T(8,128)(2,1)S(1)}, bf16[64,4096]{1,0:T(8,128)(2,1)S(1)}, u32[]{:S(2)}, u32[]{:S(2)}) collective-permute-start(bf16[64,4096]{1,0:T(8,128)(2,1)S(1)} %collective-permute-done.1.p2.n2), channel_id=1, source_target_pairs={{0,1},{1,0},{2,3},{3,2},{4,5},{5,4},{6,7},{7,6},{8,9},{9,8},{10,11... | collective-permute-start | bytes 1572872 | tf_op jit(solution)/shard_map/ppermute | solution.py:224
  44.6 0.6 collective-permute-done.p1.n1
  45.2 1.9 %collective-permute-start.4 = (bf16[64,4096]{1,0:T(8,128)(2,1)S(1)}, bf16[64,4096]{1,0:T(8,128)(2,1)S(1)}, u32[]{:S(2)}, u32[]{:S(2)}) collective-permute-start(bf16[64,4096]{1,0:T(8,128)(2,1)S(1)} %collective-permute-done.p1.n1), channel_id=1, source_target_pairs={{0,1},{1,0},{2,3},{3,2},{4,5},{5,4},{6,7},{7,6},{8,9},{9,8},{10,11... | collective-permute-start | bytes 1572872 | tf_op jit(solution)/shard_map/ppermute | solution.py:224
  47.8 0.0 copy-start
  47.8 1.6 %copy-done = bf16[4096,256]{1,0:T(8,128)(2,1)S(1)} copy-done((bf16[4096,256]{1,0:T(8,128)(2,1)S(1)}, bf16[4096,256]{1,0:T(8,128)(2,1)}, u32[]{:S(2)}) %copy-start) | copy-done | bytes 2097176
  49.4 0.0 copy-start.1
  49.4 0.0 copy-start.2
  49.4 0.0 copy-start.3
  49.4 0.7 near.1.near_s_ref
  50.1 0.0 collective-permute-done.3.f0
  50.1 0.0 collective-permute-done.6.f3
  50.1 0.0 collective-permute-done.5.f2
  50.1 0.0 collective-permute-done.4.f1
  50.2 0.8 copy-done.1
  51.0 0.0 copy-done.2
  51.0 0.1 copy-done.3
  51.0 2.8 %far.1 = (f32[512,256]{1,0:T(8,128)S(1)}, f32[512,256]{1,0:T(8,128)S(1)}, f32[512,256]{1,0:T(8,128)S(1)}, f32[32,8,256]{2,1,0:T(8,128)S(1)}) custom-call(s32[2]{0:T(128)S(1)} %pad_add_fusion.me_ref.ids_ref, s32[1]{0:T(128)S(6)} %copy.8.len_ref, bf16[64,4096]{1,0:T(8,128)(2,1)S(1)} %bitcast.8, bf16[64,4096]{1,0:T(8,128)(2,1)S(1)} %collective-permute-done.p1.n1, ...), custom_call_target="tpu_custom_call" | custom-call | tf_op jit(solution)/shard_map/far/pallas_call | solution.py:255
  53.8 16.6 %all_to_all.16.stats_ref = f32[32,8,256]{2,1,0:T(8,128)S(1)} all-to-all(f32[32,8,256]{2,1,0:T(8,128)S(1)} %get-tuple-element.19), channel_id=1, replica_groups=mesh['rep'=32,'fsdp'=32] {'fsdp'}, dimensions={0} | all-to-all | bytes 524288 | tf_op jit(solution)/shard_map/all_to_all | solution.py:267
  70.5 2.7 %second.1 = (bf16[8,256,128]{2,1,0:T(8,128)(2,1)S(1)}, bf16[8,256,128]{2,1,0:T(8,128)(2,1)S(1)}, bf16[8,256,128]{2,1,0:T(8,128)(2,1)S(1)}, bf16[8,256,128]{2,1,0:T(8,128)(2,1)S(1)}) custom-call(s32[2]{0:T(128)S(1)} %pad_add_fusion.me_ref.ids_ref, f32[32,8,256]{2,1,0:T(8,128)S(1)} %all_to_all.16.stats_ref, f32[512,256]{1,0:T(8,128)S(1)} %get-tuple-element.20.stream_ref, ...), custom_call_target="tpu_custom_call" | custom-call | tf_op jit(solution)/shard_map/second/pallas_call | solution.py:270
  73.2 2.7 %collective-permute-start.7 = (bf16[8,256,128]{2,1,0:T(8,128)(2,1)S(1)}, bf16[8,256,128]{2,1,0:T(8,128)(2,1)S(1)}, u32[]{:S(2)}, u32[]{:S(2)}) collective-permute-start(bf16[8,256,128]{2,1,0:T(8,128)(2,1)S(1)} %get-tuple-element.23), channel_id=1, source_target_pairs={{0,32},{1,97},{2,34},{3,99},{4,36},{5,101},{6,38},{7,103},{8,40},{... | collective-permute-start | bytes 1572872 | tf_op jit(solution)/shard_map/ppermute | solution.py:280
  75.8 5.1 %collective-permute-start.8 = (bf16[8,256,128]{2,1,0:T(8,128)(2,1)S(1)}, bf16[8,256,128]{2,1,0:T(8,128)(2,1)S(1)}, u32[]{:S(2)}, u32[]{:S(2)}) collective-permute-start(bf16[8,256,128]{2,1,0:T(8,128)(2,1)S(1)} %get-tuple-element.25), channel_id=1, source_target_pairs={{0,128},{32,160},{64,192},{96,224},{128,0},{160,32},{192,64},{224,... | collective-permute-start | bytes 1572872 | tf_op jit(solution)/shard_map/ppermute | solution.py:227
  80.9 14.8 %collective-permute-start.9 = (bf16[8,256,128]{2,1,0:T(8,128)(2,1)S(1)}, bf16[8,256,128]{2,1,0:T(8,128)(2,1)S(1)}, u32[]{:S(2)}, u32[]{:S(2)}) collective-permute-start(bf16[8,256,128]{2,1,0:T(8,128)(2,1)S(1)} %get-tuple-element.26), channel_id=1, source_target_pairs={{0,896},{32,928},{64,960},{96,992},{128,256},{160,288},{192,320},{... | collective-permute-start | bytes 1572872 | tf_op jit(solution)/shard_map/ppermute | solution.py:227
  95.8 0.0 collective-permute-done.7.side_ref
  95.8 0.0 collective-permute-done.8.even_ref
  95.8 9.9 %collective-permute-done.9.odd_ref = bf16[8,256,128]{2,1,0:T(8,128)(2,1)S(1)} collective-permute-done((bf16[8,256,128]{2,1,0:T(8,128)(2,1)S(1)}, bf16[8,256,128]{2,1,0:T(8,128)(2,1)S(1)}, u32[]{:S(2)}, u32[]{:S(2)}) %collective-permute-start.9) | collective-permute-done | bytes 524320 | tf_op jit(solution)/shard_map/ppermute | solution.py:227
  105.7 0.3 third.1
  106.0 30.8 %all_to_all.17.parts_ref = bf16[8,256,128]{2,1,0:T(8,128)(2,1)S(1)} all-to-all(bf16[8,256,128]{2,1,0:T(8,128)(2,1)S(1)} %third.1), channel_id=1, replica_groups={{0,64,288,352,512,576,800,864},{128,192,416,480,640,704,928,992},{32,96..., dimensions={0} | all-to-all | bytes 1048576 | tf_op jit(solution)/shard_map/all_to_all | solution.py:291
  136.7 0.8 last.1
Async XLA Ops:
  24.9 15.4 %collective-permute-start.2 = (bf16[64,4096]{1,0:T(8,128)(2,1)S(1)}, bf16[64,4096]{1,0:T(8,128)(2,1)S(1)}, u32[]{:S(2)}, u32[]{:S(2)}) collective-permute-start(bf16[64,4096]{1,0:T(8,128)(2,1)S(1)} %bitcast.3), channel_id=1, source_target_pairs={{0,16},{1,17},{2,18},{3,19},{4,20},{5,21},{6,22},{7,23},{8,24},{9,... | collective-permute-start | bytes 1572872 | tf_op jit(solution)/shard_map/ppermute | solution.py:224
  26.8 15.4 %collective-permute-start.1 = (bf16[64,4096]{1,0:T(8,128)(2,1)S(1)}, bf16[64,4096]{1,0:T(8,128)(2,1)S(1)}, u32[]{:S(2)}, u32[]{:S(2)}) collective-permute-start(bf16[64,4096]{1,0:T(8,128)(2,1)S(1)} %bitcast.4), channel_id=1, source_target_pairs={{0,14},{1,15},{2,4},{3,5},{4,2},{5,3},{6,8},{7,9},{8,6},{9,7},{10,... | collective-permute-start | bytes 1572872 | tf_op jit(solution)/shard_map/ppermute | solution.py:224
  30.0 15.3 %collective-permute-start = (bf16[64,4096]{1,0:T(8,128)(2,1)S(1)}, bf16[64,4096]{1,0:T(8,128)(2,1)S(1)}, u32[]{:S(2)}, u32[]{:S(2)}) collective-permute-start(bf16[64,4096]{1,0:T(8,128)(2,1)S(1)} %bitcast.5), channel_id=1, source_target_pairs={{0,2},{1,3},{2,0},{3,1},{4,6},{5,7},{6,4},{7,5},{8,10},{9,11},{10,... | collective-permute-start | bytes 1572872 | tf_op jit(solution)/shard_map/ppermute | solution.py:224
  34.1 16.0 %collective-permute-start.3 = (bf16[64,4096]{1,0:T(8,128)(2,1)S(1)}, bf16[64,4096]{1,0:T(8,128)(2,1)S(1)}, u32[]{:S(2)}, u32[]{:S(2)}) collective-permute-start(bf16[64,4096]{1,0:T(8,128)(2,1)S(1)} %bitcast.6), channel_id=1, source_target_pairs={{0,1},{1,0},{2,3},{3,2},{4,5},{5,4},{6,7},{7,6},{8,9},{9,8},{10,11... | collective-permute-start | bytes 1572872 | tf_op jit(solution)/shard_map/ppermute | solution.py:224
  40.3 9.8 %collective-permute-start.6 = (bf16[64,4096]{1,0:T(8,128)(2,1)S(1)}, bf16[64,4096]{1,0:T(8,128)(2,1)S(1)}, u32[]{:S(2)}, u32[]{:S(2)}) collective-permute-start(bf16[64,4096]{1,0:T(8,128)(2,1)S(1)} %collective-permute-done.2.p3.n3), channel_id=1, source_target_pairs={{0,1},{1,0},{2,3},{3,2},{4,5},{5,4},{6,7},{7,6},{8,9},{9,8},{10,11... | collective-permute-start | bytes 1572872 | tf_op jit(solution)/shard_map/ppermute | solution.py:224
  42.2 7.9 %collective-permute-start.5 = (bf16[64,4096]{1,0:T(8,128)(2,1)S(1)}, bf16[64,4096]{1,0:T(8,128)(2,1)S(1)}, u32[]{:S(2)}, u32[]{:S(2)}) collective-permute-start(bf16[64,4096]{1,0:T(8,128)(2,1)S(1)} %collective-permute-done.1.p2.n2), channel_id=1, source_target_pairs={{0,1},{1,0},{2,3},{3,2},{4,5},{5,4},{6,7},{7,6},{8,9},{9,8},{10,11... | collective-permute-start | bytes 1572872 | tf_op jit(solution)/shard_map/ppermute | solution.py:224
  45.2 4.9 %collective-permute-start.4 = (bf16[64,4096]{1,0:T(8,128)(2,1)S(1)}, bf16[64,4096]{1,0:T(8,128)(2,1)S(1)}, u32[]{:S(2)}, u32[]{:S(2)}) collective-permute-start(bf16[64,4096]{1,0:T(8,128)(2,1)S(1)} %collective-permute-done.p1.n1), channel_id=1, source_target_pairs={{0,1},{1,0},{2,3},{3,2},{4,5},{5,4},{6,7},{7,6},{8,9},{9,8},{10,11... | collective-permute-start | bytes 1572872 | tf_op jit(solution)/shard_map/ppermute | solution.py:224
  47.8 1.6 %copy-start = (bf16[4096,256]{1,0:T(8,128)(2,1)S(1)}, bf16[4096,256]{1,0:T(8,128)(2,1)}, u32[]{:S(2)}) copy-start(bf16[4096,256]{1,0:T(8,128)(2,1)} %w_ref.3) | copy-start | bytes 6291460
  49.4 1.6 %copy-start.1 = (bf16[4096,256]{1,0:T(8,128)(2,1)S(1)}, bf16[4096,256]{1,0:T(8,128)(2,1)}, u32[]{:S(2)}) copy-start(bf16[4096,256]{1,0:T(8,128)(2,1)} %t_ref.1) | copy-start | bytes 6291460
  49.4 1.6 %copy-start.2 = (bf16[512,256]{1,0:T(8,128)(2,1)S(1)}, bf16[512,256]{1,0:T(8,128)(2,1)}, u32[]{:S(2)}) copy-start(bf16[512,256]{1,0:T(8,128)(2,1)} %res_ref.1) | copy-start | bytes 786436
  49.4 1.7 %copy-start.3 = (bf16[512,256]{1,0:T(8,128)(2,1)S(1)}, bf16[512,256]{1,0:T(8,128)(2,1)}, u32[]{:S(2)}) copy-start(bf16[512,256]{1,0:T(8,128)(2,1)} %cot_ref.1) | copy-start | bytes 786436
  73.2 22.6 %collective-permute-start.7 = (bf16[8,256,128]{2,1,0:T(8,128)(2,1)S(1)}, bf16[8,256,128]{2,1,0:T(8,128)(2,1)S(1)}, u32[]{:S(2)}, u32[]{:S(2)}) collective-permute-start(bf16[8,256,128]{2,1,0:T(8,128)(2,1)S(1)} %get-tuple-element.23), channel_id=1, source_target_pairs={{0,32},{1,97},{2,34},{3,99},{4,36},{5,101},{6,38},{7,103},{8,40},{... | collective-permute-start | bytes 1572872 | tf_op jit(solution)/shard_map/ppermute | solution.py:280
  75.8 20.0 %collective-permute-start.8 = (bf16[8,256,128]{2,1,0:T(8,128)(2,1)S(1)}, bf16[8,256,128]{2,1,0:T(8,128)(2,1)S(1)}, u32[]{:S(2)}, u32[]{:S(2)}) collective-permute-start(bf16[8,256,128]{2,1,0:T(8,128)(2,1)S(1)} %get-tuple-element.25), channel_id=1, source_target_pairs={{0,128},{32,160},{64,192},{96,224},{128,0},{160,32},{192,64},{224,... | collective-permute-start | bytes 1572872 | tf_op jit(solution)/shard_map/ppermute | solution.py:227
  80.9 24.8 %collective-permute-start.9 = (bf16[8,256,128]{2,1,0:T(8,128)(2,1)S(1)}, bf16[8,256,128]{2,1,0:T(8,128)(2,1)S(1)}, u32[]{:S(2)}, u32[]{:S(2)}) collective-permute-start(bf16[8,256,128]{2,1,0:T(8,128)(2,1)S(1)} %get-tuple-element.26), channel_id=1, source_target_pairs={{0,896},{32,928},{64,960},{96,992},{128,256},{160,288},{192,320},{... | collective-permute-start | bytes 1572872 | tf_op jit(solution)/shard_map/ppermute | solution.py:227

commit v10 on v9

--- a/solution.py
+++ b/solution.py
@@ -229,10 +229,7 @@
     def shape(*dims, dtype=f32):
         return jax.ShapeDtypeStruct(dims, dtype)
 
-    own = lax.all_to_all(
-        jnp.broadcast_to(attn_out[None], (4, SHARD, features)),
-        "fsdp", 0, 0, axis_index_groups=TEAMS,
-    ).reshape(PIECE, features)
+    own = lax.all_gather(attn_out, "fsdp", axis=0, tiled=True, axis_index_groups=TEAMS)
     near = [
         own,
         in_group(own, lambda x, y, c: (x, even_partner(y), c)),

time: 138 us -> 143 us (1.036)
  the two profiles are of different devices: /device:TPU:20 before, /device:TPU:1 now
where the time goes in v10:
time: 143 us; the launch traced here: 141 us
  blocking collectives  66.2 us (46%)
  starting transfers between devices  51.1 us (36%)
  waiting for transfers between devices  12.2 us (9%)
  Pallas kernels  7.18 us (5%)
  local copies, waits for them, and re-layouts  3.15 us (2%)
    ppermute x7, starting transfers between devices, in_group(): return lax.ppermute(x, 'fsdp', fsdp_perm(step))  27.7 us
    all_gather x1, blocking collectives, local(): lax.all_gather(attn_out, 'fsdp', axis=0, tiled=True, axis_index_groups=TE...  27.4 us
    all_to_all x1, blocking collectives, local(): parts = lax.all_to_all(four, 'rep', 0, 0, axis_index_groups=CLASSES)  23 us
    ppermute x2, starting transfers between devices, of_groups(): return lax.ppermute(x, 'rep', rep_perm(step))  21.3 us
    all_to_all x1, blocking collectives, local(): stats = lax.all_to_all(stats, 'fsdp', 0, 0)  15.8 us
    ppermute x2, waiting for transfers between devices, of_groups(): return lax.ppermute(x, 'rep', rep_perm(step))  12.2 us
  transfers between devices with their start and end apart: 10, of which 1 were waited for; matrix products, arithmetic and copies ran while one was open for 1% of the time, Pallas kernels for 1%

profile of v10, /device:TPU:1, one launch (start us, length us, event | category | flops | bytes accessed | tf_op | source)
XLA Modules:
  0.0 140.9 jit_solution(1996203095926946910)
XLA Ops:
  0.0 27.4 %all_gather.3.p0.n0 = bf16[64,4096]{1,0:T(8,128)(2,1)S(1)} all-gather(bf16[16,4096]{1,0:T(8,128)(2,1)} %param.7), channel_id=1, replica_groups={{0,8,20,28},{1,9,21,29},{2,10,22,30},{3,11,23,31},{4,12,16,24},{5,13,17..., dimensions={0}, use_global_device_ids=true | all-gather | bytes 655360 | tf_op jit(solution)/shard_map/all_gather | solution.py:232
  27.4 1.9 %collective-permute-start.2 = (bf16[64,4096]{1,0:T(8,128)(2,1)S(1)}, bf16[64,4096]{1,0:T(8,128)(2,1)S(1)}, u32[]{:S(2)}, u32[]{:S(2)}) collective-permute-start(bf16[64,4096]{1,0:T(8,128)(2,1)S(1)} %all_gather.3.p0.n0), channel_id=1, source_target_pairs={{0,16},{1,17},{2,18},{3,19},{4,20},{5,21},{6,22},{7,23},{8,24},{9,... | collective-permute-start | bytes 1572872 | tf_op jit(solution)/shard_map/ppermute | solution.py:224
  29.3 2.0 %collective-permute-start.1 = (bf16[64,4096]{1,0:T(8,128)(2,1)S(1)}, bf16[64,4096]{1,0:T(8,128)(2,1)S(1)}, u32[]{:S(2)}, u32[]{:S(2)}) collective-permute-start(bf16[64,4096]{1,0:T(8,128)(2,1)S(1)} %all_gather.3.p0.n0), channel_id=1, source_target_pairs={{0,14},{1,15},{2,4},{3,5},{4,2},{5,3},{6,8},{7,9},{8,6},{9,7},{10,... | collective-permute-start | bytes 1572872 | tf_op jit(solution)/shard_map/ppermute | solution.py:224
  31.3 5.6 %collective-permute-start = (bf16[64,4096]{1,0:T(8,128)(2,1)S(1)}, bf16[64,4096]{1,0:T(8,128)(2,1)S(1)}, u32[]{:S(2)}, u32[]{:S(2)}) collective-permute-start(bf16[64,4096]{1,0:T(8,128)(2,1)S(1)} %all_gather.3.p0.n0), channel_id=1, source_target_pairs={{0,2},{1,3},{2,0},{3,1},{4,6},{5,7},{6,4},{7,5},{8,10},{9,11},{10,... | collective-permute-start | bytes 1572872 | tf_op jit(solution)/shard_map/ppermute | solution.py:224
  37.0 0.7 broadcast_in_dim.3.gain_ref
  37.7 0.1 pad_add_fusion.me_ref.ids_ref
  37.8 11.7 %collective-permute-start.3 = (bf16[64,4096]{1,0:T(8,128)(2,1)S(1)}, bf16[64,4096]{1,0:T(8,128)(2,1)S(1)}, u32[]{:S(2)}, u32[]{:S(2)}) collective-permute-start(bf16[64,4096]{1,0:T(8,128)(2,1)S(1)} %all_gather.3.p0.n0), channel_id=1, source_target_pairs={{0,1},{1,0},{2,3},{3,2},{4,5},{5,4},{6,7},{7,6},{8,9},{9,8},{10,11... | collective-permute-start | bytes 1572872 | tf_op jit(solution)/shard_map/ppermute | solution.py:224
  49.5 0.0 collective-permute-done.2.p3.n3
  49.5 1.9 %collective-permute-start.6 = (bf16[64,4096]{1,0:T(8,128)(2,1)S(1)}, bf16[64,4096]{1,0:T(8,128)(2,1)S(1)}, u32[]{:S(2)}, u32[]{:S(2)}) collective-permute-start(bf16[64,4096]{1,0:T(8,128)(2,1)S(1)} %collective-permute-done.2.p3.n3), channel_id=1, source_target_pairs={{0,1},{1,0},{2,3},{3,2},{4,5},{5,4},{6,7},{7,6},{8,9},{9,8},{10,11... | collective-permute-start | bytes 1572872 | tf_op jit(solution)/shard_map/ppermute | solution.py:224
  51.4 0.0 collective-permute-done.1.p2.n2
  51.5 2.6 %collective-permute-start.5 = (bf16[64,4096]{1,0:T(8,128)(2,1)S(1)}, bf16[64,4096]{1,0:T(8,128)(2,1)S(1)}, u32[]{:S(2)}, u32[]{:S(2)}) collective-permute-start(bf16[64,4096]{1,0:T(8,128)(2,1)S(1)} %collective-permute-done.1.p2.n2), channel_id=1, source_target_pairs={{0,1},{1,0},{2,3},{3,2},{4,5},{5,4},{6,7},{7,6},{8,9},{9,8},{10,11... | collective-permute-start | bytes 1572872 | tf_op jit(solution)/shard_map/ppermute | solution.py:224
  54.1 0.0 collective-permute-done.p1.n1
  54.1 1.9 %collective-permute-start.4 = (bf16[64,4096]{1,0:T(8,128)(2,1)S(1)}, bf16[64,4096]{1,0:T(8,128)(2,1)S(1)}, u32[]{:S(2)}, u32[]{:S(2)}) collective-permute-start(bf16[64,4096]{1,0:T(8,128)(2,1)S(1)} %collective-permute-done.p1.n1), channel_id=1, source_target_pairs={{0,1},{1,0},{2,3},{3,2},{4,5},{5,4},{6,7},{7,6},{8,9},{9,8},{10,11... | collective-permute-start | bytes 1572872 | tf_op jit(solution)/shard_map/ppermute | solution.py:224
  56.7 0.0 copy-start
  56.7 1.6 %copy-done = bf16[4096,256]{1,0:T(8,128)(2,1)S(1)} copy-done((bf16[4096,256]{1,0:T(8,128)(2,1)S(1)}, bf16[4096,256]{1,0:T(8,128)(2,1)}, u32[]{:S(2)}) %copy-start) | copy-done | bytes 2097176
  58.3 0.0 copy-start.1
  58.3 0.0 copy-start.2
  58.3 0.0 copy-start.3
  58.3 0.7 near.1.near_s_ref
  59.0 0.0 collective-permute-done.3.f0
  59.0 0.0 collective-permute-done.6.f3
  59.0 0.0 collective-permute-done.5.f2
  59.0 0.0 collective-permute-done.4.f1
  59.0 0.8 copy-done.1
  59.8 0.0 copy-done.2
  59.9 0.1 copy-done.3
  59.9 2.8 %far.1 = (f32[512,256]{1,0:T(8,128)S(1)}, f32[512,256]{1,0:T(8,128)S(1)}, f32[512,256]{1,0:T(8,128)S(1)}, f32[32,8,256]{2,1,0:T(8,128)S(1)}) custom-call(s32[2]{0:T(128)S(1)} %pad_add_fusion.me_ref.ids_ref, s32[1]{0:T(128)S(6)} %copy.8.len_ref, bf16[64,4096]{1,0:T(8,128)(2,1)S(1)} %all_gather.3.p0.n0, bf16[64,4096]{1,0:T(8,128)(2,1)S(1)} %collective-permute-done.p1.n1, ...), custom_call_target="tpu_custom_call" | custom-call | tf_op jit(solution)/shard_map/far/pallas_call | solution.py:252
  62.7 15.8 %all_to_all.10.stats_ref = f32[32,8,256]{2,1,0:T(8,128)S(1)} all-to-all(f32[32,8,256]{2,1,0:T(8,128)S(1)} %get-tuple-element.19), channel_id=1, replica_groups=mesh['rep'=32,'fsdp'=32] {'fsdp'}, dimensions={0} | all-to-all | bytes 524288 | tf_op jit(solution)/shard_map/all_to_all | solution.py:264
  78.5 2.7 %second.1 = (bf16[8,256,128]{2,1,0:T(8,128)(2,1)S(1)}, bf16[8,256,128]{2,1,0:T(8,128)(2,1)S(1)}, bf16[8,256,128]{2,1,0:T(8,128)(2,1)S(1)}, bf16[8,256,128]{2,1,0:T(8,128)(2,1)S(1)}) custom-call(s32[2]{0:T(128)S(1)} %pad_add_fusion.me_ref.ids_ref, f32[32,8,256]{2,1,0:T(8,128)S(1)} %all_to_all.10.stats_ref, f32[512,256]{1,0:T(8,128)S(1)} %get-tuple-element.20.stream_ref, ...), custom_call_target="tpu_custom_call" | custom-call | tf_op jit(solution)/shard_map/second/pallas_call | solution.py:267
  81.2 2.1 %collective-permute-start.7 = (bf16[8,256,128]{2,1,0:T(8,128)(2,1)S(1)}, bf16[8,256,128]{2,1,0:T(8,128)(2,1)S(1)}, u32[]{:S(2)}, u32[]{:S(2)}) collective-permute-start(bf16[8,256,128]{2,1,0:T(8,128)(2,1)S(1)} %get-tuple-element.23), channel_id=1, source_target_pairs={{0,32},{1,97},{2,34},{3,99},{4,36},{5,101},{6,38},{7,103},{8,40},{... | collective-permute-start | bytes 1572872 | tf_op jit(solution)/shard_map/ppermute | solution.py:277
  83.3 4.6 %collective-permute-start.8 = (bf16[8,256,128]{2,1,0:T(8,128)(2,1)S(1)}, bf16[8,256,128]{2,1,0:T(8,128)(2,1)S(1)}, u32[]{:S(2)}, u32[]{:S(2)}) collective-permute-start(bf16[8,256,128]{2,1,0:T(8,128)(2,1)S(1)} %get-tuple-element.25), channel_id=1, source_target_pairs={{0,128},{32,160},{64,192},{96,224},{128,0},{160,32},{192,64},{224,... | collective-permute-start | bytes 1572872 | tf_op jit(solution)/shard_map/ppermute | solution.py:227
  87.9 16.7 %collective-permute-start.9 = (bf16[8,256,128]{2,1,0:T(8,128)(2,1)S(1)}, bf16[8,256,128]{2,1,0:T(8,128)(2,1)S(1)}, u32[]{:S(2)}, u32[]{:S(2)}) collective-permute-start(bf16[8,256,128]{2,1,0:T(8,128)(2,1)S(1)} %get-tuple-element.26), channel_id=1, source_target_pairs={{0,896},{32,928},{64,960},{96,992},{128,256},{160,288},{192,320},{... | collective-permute-start | bytes 1572872 | tf_op jit(solution)/shard_map/ppermute | solution.py:227
  104.6 0.0 collective-permute-done.7.side_ref
  104.6 0.0 collective-permute-done.8.even_ref
  104.6 12.2 %collective-permute-done.9.odd_ref = bf16[8,256,128]{2,1,0:T(8,128)(2,1)S(1)} collective-permute-done((bf16[8,256,128]{2,1,0:T(8,128)(2,1)S(1)}, bf16[8,256,128]{2,1,0:T(8,128)(2,1)S(1)}, u32[]{:S(2)}, u32[]{:S(2)}) %collective-permute-start.9) | collective-permute-done | bytes 524320 | tf_op jit(solution)/shard_map/ppermute | solution.py:227
  116.8 0.3 third.1
  117.1 23.0 %all_to_all.11.parts_ref = bf16[8,256,128]{2,1,0:T(8,128)(2,1)S(1)} all-to-all(bf16[8,256,128]{2,1,0:T(8,128)(2,1)S(1)} %third.1), channel_id=1, replica_groups={{0,64,288,352,512,576,800,864},{128,192,416,480,640,704,928,992},{32,96..., dimensions={0} | all-to-all | bytes 1048576 | tf_op jit(solution)/shard_map/all_to_all | solution.py:288
  140.1 0.8 last.1
Async XLA Ops:
  27.4 22.1 %collective-permute-start.2 = (bf16[64,4096]{1,0:T(8,128)(2,1)S(1)}, bf16[64,4096]{1,0:T(8,128)(2,1)S(1)}, u32[]{:S(2)}, u32[]{:S(2)}) collective-permute-start(bf16[64,4096]{1,0:T(8,128)(2,1)S(1)} %all_gather.3.p0.n0), channel_id=1, source_target_pairs={{0,16},{1,17},{2,18},{3,19},{4,20},{5,21},{6,22},{7,23},{8,24},{9,... | collective-permute-start | bytes 1572872 | tf_op jit(solution)/shard_map/ppermute | solution.py:224
  29.3 22.1 %collective-permute-start.1 = (bf16[64,4096]{1,0:T(8,128)(2,1)S(1)}, bf16[64,4096]{1,0:T(8,128)(2,1)S(1)}, u32[]{:S(2)}, u32[]{:S(2)}) collective-permute-start(bf16[64,4096]{1,0:T(8,128)(2,1)S(1)} %all_gather.3.p0.n0), channel_id=1, source_target_pairs={{0,14},{1,15},{2,4},{3,5},{4,2},{5,3},{6,8},{7,9},{8,6},{9,7},{10,... | collective-permute-start | bytes 1572872 | tf_op jit(solution)/shard_map/ppermute | solution.py:224
  31.3 22.7 %collective-permute-start = (bf16[64,4096]{1,0:T(8,128)(2,1)S(1)}, bf16[64,4096]{1,0:T(8,128)(2,1)S(1)}, u32[]{:S(2)}, u32[]{:S(2)}) collective-permute-start(bf16[64,4096]{1,0:T(8,128)(2,1)S(1)} %all_gather.3.p0.n0), channel_id=1, source_target_pairs={{0,2},{1,3},{2,0},{3,1},{4,6},{5,7},{6,4},{7,5},{8,10},{9,11},{10,... | collective-permute-start | bytes 1572872 | tf_op jit(solution)/shard_map/ppermute | solution.py:224
  37.8 21.2 %collective-permute-start.3 = (bf16[64,4096]{1,0:T(8,128)(2,1)S(1)}, bf16[64,4096]{1,0:T(8,128)(2,1)S(1)}, u32[]{:S(2)}, u32[]{:S(2)}) collective-permute-start(bf16[64,4096]{1,0:T(8,128)(2,1)S(1)} %all_gather.3.p0.n0), channel_id=1, source_target_pairs={{0,1},{1,0},{2,3},{3,2},{4,5},{5,4},{6,7},{7,6},{8,9},{9,8},{10,11... | collective-permute-start | bytes 1572872 | tf_op jit(solution)/shard_map/ppermute | solution.py:224
  49.5 9.5 %collective-permute-start.6 = (bf16[64,4096]{1,0:T(8,128)(2,1)S(1)}, bf16[64,4096]{1,0:T(8,128)(2,1)S(1)}, u32[]{:S(2)}, u32[]{:S(2)}) collective-permute-start(bf16[64,4096]{1,0:T(8,128)(2,1)S(1)} %collective-permute-done.2.p3.n3), channel_id=1, source_target_pairs={{0,1},{1,0},{2,3},{3,2},{4,5},{5,4},{6,7},{7,6},{8,9},{9,8},{10,11... | collective-permute-start | bytes 1572872 | tf_op jit(solution)/shard_map/ppermute | solution.py:224
  51.5 7.5 %collective-permute-start.5 = (bf16[64,4096]{1,0:T(8,128)(2,1)S(1)}, bf16[64,4096]{1,0:T(8,128)(2,1)S(1)}, u32[]{:S(2)}, u32[]{:S(2)}) collective-permute-start(bf16[64,4096]{1,0:T(8,128)(2,1)S(1)} %collective-permute-done.1.p2.n2), channel_id=1, source_target_pairs={{0,1},{1,0},{2,3},{3,2},{4,5},{5,4},{6,7},{7,6},{8,9},{9,8},{10,11... | collective-permute-start | bytes 1572872 | tf_op jit(solution)/shard_map/ppermute | solution.py:224
  54.1 4.9 %collective-permute-start.4 = (bf16[64,4096]{1,0:T(8,128)(2,1)S(1)}, bf16[64,4096]{1,0:T(8,128)(2,1)S(1)}, u32[]{:S(2)}, u32[]{:S(2)}) collective-permute-start(bf16[64,4096]{1,0:T(8,128)(2,1)S(1)} %collective-permute-done.p1.n1), channel_id=1, source_target_pairs={{0,1},{1,0},{2,3},{3,2},{4,5},{5,4},{6,7},{7,6},{8,9},{9,8},{10,11... | collective-permute-start | bytes 1572872 | tf_op jit(solution)/shard_map/ppermute | solution.py:224
  56.7 1.6 %copy-start = (bf16[4096,256]{1,0:T(8,128)(2,1)S(1)}, bf16[4096,256]{1,0:T(8,128)(2,1)}, u32[]{:S(2)}) copy-start(bf16[4096,256]{1,0:T(8,128)(2,1)} %w_ref.3) | copy-start | bytes 6291460
  58.3 1.6 %copy-start.1 = (bf16[4096,256]{1,0:T(8,128)(2,1)S(1)}, bf16[4096,256]{1,0:T(8,128)(2,1)}, u32[]{:S(2)}) copy-start(bf16[4096,256]{1,0:T(8,128)(2,1)} %t_ref.1) | copy-start | bytes 6291460
  58.3 1.6 %copy-start.2 = (bf16[512,256]{1,0:T(8,128)(2,1)S(1)}, bf16[512,256]{1,0:T(8,128)(2,1)}, u32[]{:S(2)}) copy-start(bf16[512,256]{1,0:T(8,128)(2,1)} %res_ref.1) | copy-start | bytes 786436
  58.3 1.7 %copy-start.3 = (bf16[512,256]{1,0:T(8,128)(2,1)S(1)}, bf16[512,256]{1,0:T(8,128)(2,1)}, u32[]{:S(2)}) copy-start(bf16[512,256]{1,0:T(8,128)(2,1)} %cot_ref.1) | copy-start | bytes 786436
  81.2 23.4 %collective-permute-start.7 = (bf16[8,256,128]{2,1,0:T(8,128)(2,1)S(1)}, bf16[8,256,128]{2,1,0:T(8,128)(2,1)S(1)}, u32[]{:S(2)}, u32[]{:S(2)}) collective-permute-start(bf16[8,256,128]{2,1,0:T(8,128)(2,1)S(1)} %get-tuple-element.23), channel_id=1, source_target_pairs={{0,32},{1,97},{2,34},{3,99},{4,36},{5,101},{6,38},{7,103},{8,40},{... | collective-permute-start | bytes 1572872 | tf_op jit(solution)/shard_map/ppermute | solution.py:277
  83.3 21.4 %collective-permute-start.8 = (bf16[8,256,128]{2,1,0:T(8,128)(2,1)S(1)}, bf16[8,256,128]{2,1,0:T(8,128)(2,1)S(1)}, u32[]{:S(2)}, u32[]{:S(2)}) collective-permute-start(bf16[8,256,128]{2,1,0:T(8,128)(2,1)S(1)} %get-tuple-element.25), channel_id=1, source_target_pairs={{0,128},{32,160},{64,192},{96,224},{128,0},{160,32},{192,64},{224,... | collective-permute-start | bytes 1572872 | tf_op jit(solution)/shard_map/ppermute | solution.py:227
  87.9 29.0 %collective-permute-start.9 = (bf16[8,256,128]{2,1,0:T(8,128)(2,1)S(1)}, bf16[8,256,128]{2,1,0:T(8,128)(2,1)S(1)}, u32[]{:S(2)}, u32[]{:S(2)}) collective-permute-start(bf16[8,256,128]{2,1,0:T(8,128)(2,1)S(1)} %get-tuple-element.26), channel_id=1, source_target_pairs={{0,896},{32,928},{64,960},{96,992},{128,256},{160,288},{192,320},{... | collective-permute-start | bytes 1572872 | tf_op jit(solution)/shard_map/ppermute | solution.py:227
